TPU v7x, 128 devices: a whole 4x4x4 slice. The times are simulated.
128 devices in a mesh: band: 16 (over y_lo, x, core), off: 2 (over y_hi), rep: 4 (over z).
Axes of the slice: x: 4, y: 4 (y_hi: 2, y_lo: 2; y = y_hi * 2 + y_lo), z: 4, core: 2. Of those that a mesh axis runs over, the one named last changes fastest.
Arguments:
- feats: bfloat16 [4096, 1024], P(('rep', 'band')), parts along dimension 0, may hold values from -6 to 6
- w_proj: bfloat16 [1024, 128], replicated, may hold values from -0.1875 to 0.1875
- conv_w: bfloat16 [576, 64], replicated, may hold values from -0.25 to 0.25
- conv_b: float32 [64], replicated, may hold values from -3 to 3
- w_out: float32 [64], replicated, may hold values from -0.75 to 0.75
- target: float32 [4096, 4, 64], P(('rep', 'band'), 'off'), parts along dimension 0, may hold values from -6 to 6
- mask: int32 [4096], P('rep'), parts along dimension 0, may hold values 0 or 1
Outputs:
- loss: float32 [4], P('rep'), parts along dimension 0
- grad_proj: float32 [4096, 128], P('rep'), parts along dimension 0
- grad_conv: float32 [2304, 64], P('rep'), parts along dimension 0
- grad_bias: float32 [256], P('rep'), parts along dimension 0
- grad_wout: float32 [256], P('rep'), parts along dimension 0
- grad_feats: bfloat16 [4096, 1024], P(('rep', 'band', 'off')), parts along dimension 0
There are 4 independent parts, one for each index of `rep`. A program takes and returns all parts, laid end to end along the dimension named above; an argument that names none is the same for every part. Nothing has to cross between parts.
All inputs are finite; a program needn't handle non-finite values.
Results may differ from a plain program's by a relative error of at most 0.029.
Values may be sent and summed in bfloat16 or wider, within the bound.
No kernel may reach another device: no remote copies, remote signals or barrier semaphores. Data moves between devices by JAX's collectives and lax.ppermute only.
A program may use at most 192 MiB of HBM per device.

v0:
```python
import jax
import jax.numpy as jnp
from jax import lax
from jax.experimental import pallas as pl
from jax.experimental.pallas import tpu as pltpu
from jax.sharding import PartitionSpec as P

GELU_K = 0.7978845608028654
GELU_C = 0.044715
GROUP = ("band", "off")
PEERS = 32
SLOT = 48
F32 = jnp.float32
BF16 = jnp.bfloat16


def gelu_parts(x, half):
    square = x * x
    t = jnp.tanh(x * (GELU_K + (GELU_K * GELU_C) * square))
    one_plus = 1.0 + t
    scaled = x * half
    value = scaled * one_plus
    slope = one_plus * (half + (scaled * (1.0 - t)) * (GELU_K + (3.0 * GELU_K * GELU_C) * square))
    return value, slope


def lane_ids(shape):
    return lax.broadcasted_iota(jnp.int32, shape, len(shape) - 1)


def row_ids(shape):
    return lax.broadcasted_iota(jnp.int32, shape, len(shape) - 2)


def dot(a, b):
    return jnp.dot(a, b, preferred_element_type=F32)


def tile_kernel(
    own, before, after1, after2, after3, after4, mask, target, fwd_w, bwd_w, conv_b2, w_out2, pred_w,
    out,
    rows_u, cols_v, pair, slope, grads, goal, pre, hid16, hid32, weighted, guess, row_mask, col_mask,
    grad_rows, grad_cols, grad_w, bins,
):
    band = lax.axis_index("band")
    off = lax.axis_index("off")
    first = band + 2 * off
    near = off == 0
    half_lane = lane_ids((1, 128)) < 64

    zero_rows = jnp.zeros((128, 1280), BF16)
    grads[0:128, :] = zero_rows
    grads[640:768, :] = zero_rows
    grads[128:640, 0:128] = jnp.zeros((512, 128), BF16)
    grads[128:640, 1152:1280] = jnp.zeros((512, 128), BF16)
    bins[...] = jnp.zeros(bins.shape, F32)

    mine = own[...].astype(F32)
    b_before = before[...].astype(F32)
    b_1 = after1[...].astype(F32)
    b_2 = after2[...].astype(F32)
    b_3 = after3[...].astype(F32)
    b_4 = after4[...].astype(F32)
    u = jnp.concatenate([b_before[8:16], mine, b_1[0:8]], axis=0)
    rows_u[...] = jnp.where(half_lane, u, pltpu.roll(u, 64, 1))
    v = jnp.concatenate(
        [
            jnp.where(near, b_before[8:16], b_1[56:64]),
            jnp.where(near, mine, b_2),
            jnp.where(near, b_1, b_3),
            jnp.where(near, b_2[0:8], b_4[0:8]),
        ],
        axis=0,
    ).reshape(9, 2, 8, 128)
    v_low = v[:, 0].reshape(72, 128)
    v_high = v[:, 1].reshape(72, 128)
    cols_v[...] = jnp.where(half_lane, pltpu.roll(v_low, 64, 1), v_high)

    mask_all = mask[...].astype(F32)
    mask_lane = lane_ids((8, 128))
    by_band = jnp.concatenate(
        [jnp.where(mask_lane < 64, mask_all, 0.0), jnp.where(mask_lane < 64, 0.0, mask_all)], axis=0
    ).astype(BF16)
    sums_row = dot(by_band, jnp.ones((128, 128), BF16))
    sums_col = lax.dot_general(
        jnp.ones((16, 128), BF16), by_band, (((1,), (1,)), ((), ())), preferred_element_type=F32
    )
    at = lax.broadcasted_iota(jnp.int32, (16, 16), 0)
    to = lax.broadcasted_iota(jnp.int32, (16, 16), 1)
    apart = (2 * (to % 8) + to // 8) - (2 * (at % 8) + at // 8)
    near_diagonal = (apart >= 0) & (apart < 4)
    count = jnp.sum(jnp.where(near_diagonal, sums_row[:, 0:16] * sums_col, 0.0))
    scale = 1.0 / count

    def mask_rows(which):
        inside = jnp.minimum(which, 15)
        line = mask[pl.ds(inside // 2, 1), :].astype(F32)
        line = jnp.where(which < 16, line, 0.0)
        spot = row_ids((64, 128)) + 64 * (inside % 2)
        spread = jnp.where(lane_ids((64, 128)) == spot, line, 0.0)
        return dot(spread.astype(BF16), jnp.ones((128, 128), BF16))

    row_mask[...] = (
        jnp.broadcast_to(mask_rows(band)[:, None, :] * (2.0 * scale), (64, 8, 128)).reshape(512, 128)
    )
    col_all = jnp.concatenate([mask_rows(first), mask_rows(first + 1)], axis=0).reshape(8, 2, 8, 128)
    col_mask[...] = jnp.where(half_lane, col_all[:, 0].reshape(64, 128), col_all[:, 1].reshape(64, 128))

    lines = jnp.broadcast_to(target[...][:, None, :], (64, 8, 128)).reshape(512, 128)
    lines = jnp.where(lane_ids((512, 128)) % 8 == row_ids((512, 128)) % 8, lines, 0.0)
    lines_hi = lines.astype(BF16)
    lines_lo = (lines - lines_hi.astype(F32)).astype(BF16)
    spread = (
        (row_ids((128, 1024)) // 8 == lane_ids((128, 1024)) // 64).astype(F32).astype(BF16)
    )
    goal[...] = dot(
        jnp.concatenate([lines_hi, lines_lo], axis=1), jnp.concatenate([spread, spread], axis=0)
    )

    def pair_step(aq, carry):
        row = pl.multiple_of(aq * 64, 64)
        here = rows_u[pl.ds(pl.multiple_of(aq * 8, 8), 8), :]
        row_at = band * 8 + aq - 1
        row_in = (row_at >= 0) & (row_at < 128)
        for bp in range(9):
            block = first * 8 - 1 + 2 * bp
            spot = jnp.where(half_lane, block, block + 1)
            half = jnp.where((spot >= 0) & (spot < 128) & row_in, 0.5, 0.0)
            x = (here[:, None, :] + cols_v[bp * 8 : bp * 8 + 8, :][None, :, :]).reshape(64, 128)
            value, grade = gelu_parts(x, half)
            pair[pl.ds(row, 64), bp * 128 : bp * 128 + 128] = value.astype(BF16)
            slope[pl.ds(row, 64), bp * 128 : bp * 128 + 128] = grade
        return carry

    lax.fori_loop(0, 10, pair_step, 0)

    bias2 = conv_b2[...]
    out_w2 = w_out2[...]
    zero8 = jnp.zeros((8, 128), F32)
    totals = (zero8, zero8, zero8)
    for bp in range(8):
        lane = bp * 128
        pre[...] = (
            dot(pair[0:512, lane : lane + 256], fwd_w[0:256, :])
            + dot(pair[64:576, lane : lane + 256], fwd_w[256:512, :])
            + dot(pair[128:640, lane : lane + 256], fwd_w[512:768, :])
        )

        def act_step(aq, carry):
            row = pl.ds(pl.multiple_of(aq * 64, 64), 64)
            value, grade = gelu_parts(pre[row, :] + bias2, 0.5)
            hid32[row, :] = value
            hid16[row, :] = value.astype(BF16)
            weighted[row, :] = grade * out_w2
            return carry

        lax.fori_loop(0, 8, act_step, 0)
        low = hid16[...]
        guess[...] = dot(jnp.concatenate([low, low], axis=1), pred_w[...])

        def loss_step(aq, carry):
            loss_sum, bias_sum, out_sum = carry
            start = pl.multiple_of(aq * 64, 64)
            row = pl.ds(start, 64)
            weight = (row_mask[row, :].reshape(8, 8, 128) * col_mask[bp * 8 : bp * 8 + 8, :][None]).reshape(64, 128)
            residue = guess[row, :] - goal[row, lane : lane + 128]
            grad_pred = weight * residue
            grad_pre = grad_pred * weighted[row, :]
            grads[pl.ds(pl.multiple_of(start + 128, 64), 64), lane + 128 : lane + 256] = grad_pre.astype(BF16)
            loss_sum = loss_sum + jnp.sum((grad_pred * residue).reshape(8, 8, 128), axis=0)
            bias_sum = bias_sum + jnp.sum(grad_pre.reshape(8, 8, 128), axis=0)
            out_sum = out_sum + jnp.sum((grad_pred * hid32[row, :]).reshape(8, 8, 128), axis=0)
            return loss_sum, bias_sum, out_sum

        totals = lax.fori_loop(0, 8, loss_step, totals)

    for bp in range(8):
        lane = bp * 128
        turned = grads[128:640, lane + 128 : lane + 256].T
        for ty in range(3):
            part = dot(turned, pair[ty * 64 : ty * 64 + 512, lane : lane + 256])
            if bp == 0:
                grad_w[:, ty * 256 : ty * 256 + 256] = part
            else:
                grad_w[:, ty * 256 : ty * 256 + 256] += part

    for bp in range(9):
        lane = bp * 128
        part = (
            dot(grads[128:768, lane : lane + 256], bwd_w[0:256, :])
            + dot(grads[64:704, lane : lane + 256], bwd_w[256:512, :])
            + dot(grads[0:640, lane : lane + 256], bwd_w[512:768, :])
        ) * slope[:, lane : lane + 128]
        if bp == 0:
            grad_rows[...] = part
        else:
            grad_rows[...] += part
        grad_cols[bp * 8 : bp * 8 + 8, :] = jnp.sum(part.reshape(80, 8, 128), axis=0)

    row_part = jnp.sum(grad_rows[...].reshape(80, 8, 128), axis=1)
    row_part = jnp.where(half_lane, row_part + pltpu.roll(row_part, 64, 1), 0.0)
    bins[pl.ds(pl.multiple_of(band * 64 + 56, 8), 80), :] += row_part
    col_part = grad_cols[...]
    col_low = pltpu.roll(col_part, 64, 1).reshape(9, 1, 8, 128)
    col_part = jnp.concatenate([col_low, col_part.reshape(9, 1, 8, 128)], axis=1).reshape(144, 128)
    col_part = jnp.where(half_lane, 0.0, col_part)
    bins[pl.ds(pl.multiple_of(first * 64 + 56, 8), 144), :] += col_part
    out[:, 0:32, :] = bins[64:1088, :].reshape(32, 32, 128).astype(BF16)

    taps = []
    for ty in range(3):
        low = grad_w[0:64, ty * 256 : ty * 256 + 192]
        high = grad_w[64:128, ty * 256 + 64 : ty * 256 + 256]
        taps.append((low + high).T)
    conv_grad = jnp.concatenate(taps, axis=0)
    conv_grad = jnp.concatenate([conv_grad[0:288], conv_grad[288:576]], axis=1)

    loss_sum, bias_sum, out_sum = totals
    bias_row = jnp.sum(bias_sum, axis=0, keepdims=True)
    bias_row = bias_row + pltpu.roll(bias_row, 64, 1)
    out_row = jnp.sum(out_sum, axis=0, keepdims=True)
    out_row = out_row + pltpu.roll(out_row, 64, 1)
    small_row = jnp.where(half_lane, bias_row, out_row)
    loss_row = jnp.broadcast_to(jnp.sum(loss_sum, keepdims=True) * (0.5 / 64.0), (1, 128))
    small_hi = small_row.astype(BF16).astype(F32)
    loss_hi = loss_row.astype(BF16).astype(F32)
    tail = jnp.concatenate(
        [small_hi, small_row - small_hi, loss_hi, loss_row - loss_hi, jnp.zeros((3, 128), F32)], axis=0
    )
    tail = jnp.broadcast_to(tail[None], (PEERS, 7, 128))
    rest = jnp.concatenate([conv_grad[256:288].reshape(PEERS, 1, 128), tail], axis=1)
    out[:, 32:48, :] = jnp.concatenate([conv_grad[0:256].reshape(PEERS, 8, 128), rest], axis=1).astype(BF16)


def tile_call(*operands):
    shapes = [
        ((80, 128), F32), ((72, 128), F32), ((640, 1152), BF16), ((640, 1152), F32), ((768, 1280), BF16),
        ((512, 1024), F32), ((512, 128), F32), ((512, 128), BF16), ((512, 128), F32), ((512, 128), F32),
        ((512, 128), F32), ((512, 128), F32), ((64, 128), F32), ((640, 128), F32), ((72, 128), F32),
        ((128, 768), F32), ((1408, 128), F32),
    ]
    return pl.pallas_call(
        tile_kernel,
        out_shape=jax.ShapeDtypeStruct((PEERS, SLOT, 128), BF16),
        in_specs=[pl.BlockSpec(memory_space=pltpu.VMEM)] * len(operands),
        out_specs=pl.BlockSpec(memory_space=pltpu.VMEM),
        scratch_shapes=[pltpu.VMEM(shape, kind) for shape, kind in shapes],
        compiler_params=pltpu.CompilerParams(vmem_limit_bytes=40 * 2**20),
        cost_estimate=pl.CostEstimate(flops=2 * 10**9, bytes_accessed=10**6, transcendentals=10**6),
        name="tiles",
    )(*operands)


def sum_kernel(parts, out, small):
    total = jnp.sum(parts[...].astype(F32), axis=0)
    out[...] = jnp.broadcast_to(total.astype(BF16)[None], (PEERS, SLOT, 128))
    small[0:1, :] = total[41:42] + total[42:43]
    small[1:2, :] = total[43:44] + total[44:45]


def sum_call(parts):
    return pl.pallas_call(
        sum_kernel,
        out_shape=(jax.ShapeDtypeStruct((PEERS, SLOT, 128), BF16), jax.ShapeDtypeStruct((2, 128), F32)),
        in_specs=[pl.BlockSpec(memory_space=pltpu.VMEM)],
        out_specs=(pl.BlockSpec(memory_space=pltpu.VMEM),) * 2,
        name="sums",
    )(parts)


def final_kernel(every, feats, w_proj, grad_proj, grad_conv, grad_feats):
    me = lax.axis_index("band") * 2 + lax.axis_index("off")
    gproj = every[:, 0:32, :].reshape(1024, 128)
    grad_proj[...] = lax.dot_general(
        feats[...], gproj, (((0,), (0,)), ((), ())), preferred_element_type=F32
    )
    conv = every[:, 32:48, :].astype(F32)
    conv = jnp.concatenate([conv[:, 0:8].reshape(256, 128), conv[:, 8]], axis=0)
    grad_conv[0:288, :] = conv[:, 0:64]
    grad_conv[288:576, :] = conv[:, 64:128]
    mine = every[me, 0:32, :]
    grad_feats[...] = lax.dot_general(
        mine, w_proj[...], (((1,), (1,)), ((), ())), preferred_element_type=F32
    ).astype(BF16)


def final_call(every, feats, w_proj):
    return pl.pallas_call(
        final_kernel,
        out_shape=(
            jax.ShapeDtypeStruct((1024, 128), F32),
            jax.ShapeDtypeStruct((576, 64), F32),
            jax.ShapeDtypeStruct((32, 1024), BF16),
        ),
        in_specs=[pl.BlockSpec(memory_space=pltpu.VMEM)] * 3,
        out_specs=(pl.BlockSpec(memory_space=pltpu.VMEM),) * 3,
        compiler_params=pltpu.CompilerParams(vmem_limit_bytes=40 * 2**20),
        name="outputs",
    )(every, feats, w_proj)


def body(feats, w_proj, conv_w, conv_b, w_out, target, mask):
    bands = lax.axis_size("band")
    gathered = lax.all_gather(feats, "band", tiled=True)
    proj = dot(feats, w_proj).astype(BF16)

    def moved(x, by, offs=(0, 1)):
        pairs = [(2 * i + o, 2 * (i - by) + o) for i in range(bands) for o in offs if 0 <= i - by < bands]
        return lax.ppermute(x, GROUP, pairs)

    before = moved(proj[48:64], -1)
    after1 = moved(proj, 1)
    after2 = moved(proj, 2)
    after3 = moved(proj, 3, (1,))
    after4 = moved(proj[0:16], 4, (1,))

    def toeplitz(taps):
        low = jnp.pad(taps, ((0, 0), (0, 64), (0, 0)))
        high = jnp.pad(taps, ((0, 0), (64, 0), (0, 0)))
        return jnp.concatenate([low, high], axis=2).reshape(768, 128)

    fwd_w = toeplitz(conv_w.reshape(3, 192, 64))
    turned = conv_w.reshape(3, 3, 64, 64)[:, ::-1].transpose(0, 1, 3, 2)
    bwd_w = toeplitz(turned.reshape(3, 192, 64))
    twice = jnp.concatenate([w_out, w_out])
    at = jnp.arange(128, dtype=jnp.int32)
    spread = jnp.where((at[:, None] < 64) == (at[None, :] < 64), twice[:, None], 0.0)
    spread_hi = spread.astype(BF16)
    pred_w = jnp.concatenate([spread_hi, (spread - spread_hi.astype(F32)).astype(BF16)], axis=0)
    sent = tile_call(
        proj, before, after1, after2, after3, after4,
        mask.reshape(8, 128), target.reshape(64, 128), fwd_w, bwd_w,
        jnp.concatenate([conv_b, conv_b]).reshape(1, 128), twice.reshape(1, 128), pred_w,
    )
    parts = lax.all_to_all(sent, GROUP, 0, 0, tiled=True)
    sums, small = sum_call(parts)
    every = lax.all_to_all(sums, GROUP, 0, 0, tiled=True)
    grad_proj, grad_conv, grad_feats = final_call(every, gathered, w_proj)
    return (small[1, 0:1], grad_proj, grad_conv, small[0, 0:64], small[0, 64:128], grad_feats)


def solution(mesh):
    placed = (
        P(("rep", "band"), None),
        P(),
        P(),
        P(),
        P(),
        P(("rep", "band"), "off", None),
        P("rep"),
    )
    return jax.shard_map(
        body,
        mesh=mesh,
        in_specs=placed,
        out_specs=(
            P("rep"),
            P("rep", None),
            P("rep", None),
            P("rep"),
            P("rep"),
            P(("rep", "band", "off"), None),
        ),
        check_vma=False,
    )
```

profile of v0, /device:TPU:1, one launch (start us, length us, event | category | flops | bytes accessed | tf_op | source)
XLA Modules:
  0.0 89.0 jit_solution(6235980228251812181)
XLA Ops:
  7.2 0.0 all-gather.2.cloned.1.call-start
  7.2 0.7 all-gather.2.cloned.1.call-update
  7.9 1.2 %convolution_convert_fusion.own = bf16[64,128]{1,0:T(8,128)(2,1)S(1)} fusion(bf16[64,1024]{1,0:T(8,128)(2,1)} %param.7, bf16[1024,128]{1,0:T(8,128)(2,1)} %w_proj.1), kind=kOutput, calls=%fused_computation | convolution fusion | flops 16785408 | bytes 409600 | tf_op jit(solution)/shard_map/dot_general | solution.py:36
  9.1 3.3 %collective-permute-start.1 = (bf16[64,128]{1,0:T(8,128)(2,1)S(1)}, bf16[64,128]{1,0:T(8,128)(2,1)S(1)}, u32[]{:S(2)}, u32[]{:S(2)}) collective-permute-start(bf16[64,128]{1,0:T(8,128)(2,1)S(1)} %convolution_convert_fusion.own), channel_id=1, source_target_pairs={{8,0},{12,4},{16,8},{20,12},{24,16},{28,20},{32,24},{36,28},{40,32... | collective-permute-start | bytes 49160 | tf_op jit(solution)/shard_map/ppermute | solution.py:309
  12.5 1.3 %collective-permute-start.2 = (bf16[64,128]{1,0:T(8,128)(2,1)S(1)}, bf16[64,128]{1,0:T(8,128)(2,1)S(1)}, u32[]{:S(2)}, u32[]{:S(2)}) collective-permute-start(bf16[64,128]{1,0:T(8,128)(2,1)S(1)} %convolution_convert_fusion.own), channel_id=1, source_target_pairs={{16,0},{20,4},{24,8},{28,12},{32,16},{36,20},{40,24},{44,28},{48,3... | collective-permute-start | bytes 49160 | tf_op jit(solution)/shard_map/ppermute | solution.py:309
  13.8 0.7 collective-permute-start.3
  14.5 3.7 %collective-permute-start = (bf16[16,128]{1,0:T(8,128)(2,1)S(1)}, bf16[16,128]{1,0:T(8,128)(2,1)S(1)}, u32[]{:S(2)}, u32[]{:S(2)}) collective-permute-start(bf16[16,128]{1,0:T(8,128)(2,1)S(1)} %get-tuple-element.35), channel_id=1, source_target_pairs={{0,8},{4,12},{8,16},{12,20},{16,24},{20,28},{24,32},{28,36},{32,40... | collective-permute-start | bytes 12296 | tf_op jit(solution)/shard_map/ppermute | solution.py:309
  18.2 0.7 collective-permute-start.4
  18.9 1.0 %copy.21 = bf16[576,64]{1,0:T(8,128)(2,1)S(1)} copy(bf16[576,64]{0,1:T(8,128)(2,1)} %param.9) | data formatting | bytes 147456 | tf_op args[2]
  19.9 1.0 %reshape.52 = bf16[3,192,64]{1,0,2:T(4,128)(2,1)S(1)} reshape(bf16[576,64]{0,1:T(8,128)(2,1)} %param.9) | data formatting | bytes 147456 | tf_op jit(solution)/shard_map/reshape | solution.py:322
  20.9 0.1 copy.22
  21.1 0.8 pad_maximum_fusion.1
  21.9 0.1 fusion.6
  22.0 0.1 select_convert_fusion
  22.1 0.1 fusion.5
  22.2 0.2 fusion.4
  22.4 0.1 maximum_bitcast_fusion.conv_b2
  22.5 0.2 copy.20
  22.7 0.1 reshape.51.target
  22.8 0.0 collective-permute-done.before
  22.8 0.0 collective-permute-done.2.after2
  22.9 15.4 %tiles.1 = bf16[32,48,128]{2,1,0:T(8,128)(2,1)S(1)} custom-call(bf16[64,128]{1,0:T(8,128)(2,1)S(1)} %convolution_convert_fusion.own, bf16[16,128]{1,0:T(8,128)(2,1)S(1)} %collective-permute-done.before, bf16[64,128]{1,0:T(8,128)(2,1)S(1)} %collective-permute-done.1.after1, bf16[64,128]{1,0:T(8,128)(2,1)S(1)} %collective-permute-done.2.after2, ...), custom_call_target="tpu_custom_call" | custom-call | flops 2000000000 | bytes 1000000 | tf_op jit(solution)/shard_map/tiles/pallas_call | solution.py:242
  38.3 0.0 copy-start.1
  38.3 23.8 %all_to_all.10.parts = bf16[32,48,128]{2,1,0:T(8,128)(2,1)} all-to-all(bf16[32,48,128]{2,1,0:T(8,128)(2,1)S(1)} %tiles.1), channel_id=1, replica_groups=mesh['band'=16,'off'=2,'rep'=4] {'band','off'}, dimensions={0} | all-to-all | bytes 786432 | tf_op jit(solution)/shard_map/all_to_all | solution.py:335
  62.0 1.8 %sums.1 = (bf16[32,48,128]{2,1,0:T(8,128)(2,1)}, f32[2,128]{1,0:T(2,128)}) custom-call(bf16[32,48,128]{2,1,0:T(8,128)(2,1)} %all_to_all.10.parts), custom_call_target="tpu_custom_call" | custom-call | tf_op jit(solution)/shard_map/sums/pallas_call | solution.py:262
  63.9 4.1 %all-to-all-start.1 = ((bf16[32,48,128]{2,1,0:T(8,128)(2,1)}), bf16[32,48,128]{2,1,0:T(8,128)(2,1)S(1)}, u32[]{:S(2)}, u32[]{:S(2)}) async-start(bf16[32,48,128]{2,1,0:T(8,128)(2,1)} %get-tuple-element.12), calls=%async_computation.1 | async-start | bytes 786432 | tf_op jit(solution)/shard_map/all_to_all | solution.py:337
  67.9 1.2 %slice.17 = f32[1,1]{1,0:T(1,128)} slice(f32[2,128]{1,0:T(2,128)} %get-tuple-element.11), slice={[1:2], [0:1]} | slice | bytes 8 | tf_op jit(solution)/shard_map/slice | solution.py:339
  69.1 1.3 %slice_bitcast_fusion = (f32[64]{0:T(128)}, f32[64]{0:T(128)}) fusion(f32[2,128]{1,0:T(2,128)} %get-tuple-element.11), kind=kLoop, calls=%fused_computation.18 | loop fusion | bytes 1024 | tf_op jit(solution)/shard_map/squeeze | solution.py:339
  70.5 7.6 %all-to-all-done.1.every = bf16[32,48,128]{2,1,0:T(8,128)(2,1)S(1)} async-done(((bf16[32,48,128]{2,1,0:T(8,128)(2,1)}), bf16[32,48,128]{2,1,0:T(8,128)(2,1)S(1)}, u32[]{:S(2)}, u32[]{:S(2)}) %all-to-all-start.1) | async-done | bytes 393248 | tf_op jit(solution)/shard_map/all_to_all | solution.py:337
  78.1 1.6 %copy-done = bf16[1024,1024]{1,0:T(8,128)(2,1)S(1)} copy-done((bf16[1024,1024]{1,0:T(8,128)(2,1)S(1)}, bf16[1024,1024]{1,0:T(8,128)(2,1)}, u32[]{:S(2)}) %copy-start) | copy-done | bytes 2097176
  79.7 1.6 %outputs.1 = (f32[1024,128]{1,0:T(8,128)}, f32[576,64]{1,0:T(8,128)S(1)}, bf16[32,1024]{1,0:T(8,128)(2,1)}) custom-call(bf16[32,48,128]{2,1,0:T(8,128)(2,1)S(1)} %all-to-all-done.1.every, bf16[1024,1024]{1,0:T(8,128)(2,1)S(1)} %copy-done, bf16[1024,128]{1,0:T(8,128)(2,1)S(1)} %copy-done.1), custom_call_target="tpu_custom_call" | custom-call | tf_op jit(solution)/shard_map/outputs/pallas_call | solution.py:288
  81.3 0.8 copy.23
  (16 shorter events, 0.1 us)
Async XLA Ops:
  7.2 15.2 %copy-start.4 = (f32[64]{0:T(128)S(1)}, f32[64]{0:T(128)}, u32[]{:S(2)}) copy-start(f32[64]{0:T(128)} %param.10) | copy-start | bytes 772
  7.2 15.5 %copy-start.3 = (f32[64,2,64]{2,1,0:T(2,128)S(1)}, f32[64,2,64]{2,1,0:T(2,128)}, u32[]{:S(2)}) copy-start(f32[64,2,64]{2,1,0:T(2,128)} %param.12) | copy-start | bytes 98308
  7.2 15.7 %copy-start.2 = (s32[1024]{0:T(1024)S(1)}, s32[1024]{0:T(1024)}, u32[]{:S(2)}) copy-start(s32[1024]{0:T(1024)} %param.13) | copy-start | bytes 12292
  7.2 70.9 %all-gather.2.cloned.1.call-start = ((), (), s32[]{:S(2)}) async-start(), calls=%async_computation.2 | async-start | bytes 2228224 | tf_op jit(solution)/shard_map/all_gather | solution.py:304
  9.1 13.7 %collective-permute-start.1 = (bf16[64,128]{1,0:T(8,128)(2,1)S(1)}, bf16[64,128]{1,0:T(8,128)(2,1)S(1)}, u32[]{:S(2)}, u32[]{:S(2)}) collective-permute-start(bf16[64,128]{1,0:T(8,128)(2,1)S(1)} %convolution_convert_fusion.own), channel_id=1, source_target_pairs={{8,0},{12,4},{16,8},{20,12},{24,16},{28,20},{32,24},{36,28},{40,32... | collective-permute-start | bytes 49160 | tf_op jit(solution)/shard_map/ppermute | solution.py:309
  12.5 10.4 %collective-permute-start.2 = (bf16[64,128]{1,0:T(8,128)(2,1)S(1)}, bf16[64,128]{1,0:T(8,128)(2,1)S(1)}, u32[]{:S(2)}, u32[]{:S(2)}) collective-permute-start(bf16[64,128]{1,0:T(8,128)(2,1)S(1)} %convolution_convert_fusion.own), channel_id=1, source_target_pairs={{16,0},{20,4},{24,8},{28,12},{32,16},{36,20},{40,24},{44,28},{48,3... | collective-permute-start | bytes 49160 | tf_op jit(solution)/shard_map/ppermute | solution.py:309
  13.8 9.1 %collective-permute-start.3 = (bf16[64,128]{1,0:T(8,128)(2,1)S(1)}, bf16[64,128]{1,0:T(8,128)(2,1)S(1)}, u32[]{:S(2)}, u32[]{:S(2)}) collective-permute-start(bf16[64,128]{1,0:T(8,128)(2,1)S(1)} %convolution_convert_fusion.own), channel_id=1, source_target_pairs={{28,4},{36,12},{44,20},{52,28},{60,36},{68,44},{76,52},{84,60},{92... | collective-permute-start | bytes 49160 | tf_op jit(solution)/shard_map/ppermute | solution.py:309
  14.5 8.4 %collective-permute-start = (bf16[16,128]{1,0:T(8,128)(2,1)S(1)}, bf16[16,128]{1,0:T(8,128)(2,1)S(1)}, u32[]{:S(2)}, u32[]{:S(2)}) collective-permute-start(bf16[16,128]{1,0:T(8,128)(2,1)S(1)} %get-tuple-element.35), channel_id=1, source_target_pairs={{0,8},{4,12},{8,16},{12,20},{16,24},{20,28},{24,32},{28,36},{32,40... | collective-permute-start | bytes 12296 | tf_op jit(solution)/shard_map/ppermute | solution.py:309
  18.2 4.6 %collective-permute-start.4 = (bf16[16,128]{1,0:T(8,128)(2,1)S(1)}, bf16[16,128]{1,0:T(8,128)(2,1)S(1)}, u32[]{:S(2)}, u32[]{:S(2)}) collective-permute-start(bf16[16,128]{1,0:T(8,128)(2,1)S(1)} %get-tuple-element.34), channel_id=1, source_target_pairs={{36,4},{44,12},{52,20},{60,28},{68,36},{76,44},{84,52},{92,60},{10... | collective-permute-start | bytes 12296 | tf_op jit(solution)/shard_map/ppermute | solution.py:309
  38.3 39.8 %copy-start.1 = (bf16[1024,128]{1,0:T(8,128)(2,1)S(1)}, bf16[1024,128]{1,0:T(8,128)(2,1)}, u32[]{:S(2)}) copy-start(bf16[1024,128]{1,0:T(8,128)(2,1)} %w_proj.1) | copy-start | bytes 786436
  63.9 14.2 %all-to-all-start.1 = ((bf16[32,48,128]{2,1,0:T(8,128)(2,1)}), bf16[32,48,128]{2,1,0:T(8,128)(2,1)S(1)}, u32[]{:S(2)}, u32[]{:S(2)}) async-start(bf16[32,48,128]{2,1,0:T(8,128)(2,1)} %get-tuple-element.12), calls=%async_computation.1 | async-start | bytes 786432 | tf_op jit(solution)/shard_map/all_to_all | solution.py:337
  78.1 1.6 %copy-start = (bf16[1024,1024]{1,0:T(8,128)(2,1)S(1)}, bf16[1024,1024]{1,0:T(8,128)(2,1)}, u32[]{:S(2)}) copy-start(bf16[1024,1024]{1,0:T(8,128)(2,1)} %all-gather.2.cloned.1.call-done.feats) | copy-start | bytes 6291460
Sparse Core Ops, SparseCore 0:
  9.7 37.5 all-gather.1
where the time goes:
time: 89.6 us; the launch traced here: 89 us
  blocking collectives  23.8 us (27%)
  Pallas kernels  18.9 us (21%)
  between operations  14.2 us (16%)
  starting transfers between devices  13.8 us (15%)
  waiting for transfers between devices  8.32 us (9%)
  local copies, waits for them, and re-layouts  7.46 us (8%)
  other arithmetic  1.37 us (2%)
  matrix products  1.2 us (1%)
    all_to_all x1, blocking collectives, body(): parts = lax.all_to_all(sent, GROUP, 0, 0, tiled=True)  23.8 us
    pallas_call x1, Pallas kernels, tile_call(): pl.pallas_call(tile_kernel, out_shape=jax.ShapeDtypeStruct((PEERS, SLOT,...  15.4 us
    ppermute x5, starting transfers between devices, moved(): return lax.ppermute(x, GROUP, pairs)  9.67 us
    all_to_all x1, waiting for transfers between devices, body(): every = lax.all_to_all(sums, GROUP, 0, 0, tiled=True)  7.62 us
    all_to_all x1, starting transfers between devices, body(): every = lax.all_to_all(sums, GROUP, 0, 0, tiled=True)  4.07 us
    unnamed x12, local copies, waits for them, and re-layouts  3.45 us
    pallas_call x1, Pallas kernels, sum_call(): pl.pallas_call(sum_kernel, out_shape=(jax.ShapeDtypeStruct((PEERS, SLOT,...  1.82 us
  transfers between devices with their start and end apart: 7, of which 1 were waited for; matrix products, arithmetic and copies ran while one was open for 9% of the time, Pallas kernels for 19%

commit v1 on v0

v1 whole, which is shorter than its diff:
```python
import jax
import jax.numpy as jnp
from jax import lax
from jax.experimental import pallas as pl
from jax.experimental.pallas import tpu as pltpu
from jax.sharding import PartitionSpec as P

GELU_K = 0.7978845608028654
GELU_C = 0.044715
GROUP = ("band", "off")
PEERS = 32
SLOT = 48
F32 = jnp.float32
BF16 = jnp.bfloat16


def gelu_parts(x, half):
    square = x * x
    t = jnp.tanh(x * (GELU_K + (GELU_K * GELU_C) * square))
    one_plus = 1.0 + t
    scaled = x * half
    value = scaled * one_plus
    slope = one_plus * (half + (scaled * (1.0 - t)) * (GELU_K + (3.0 * GELU_K * GELU_C) * square))
    return value, slope


def lane_ids(shape):
    return lax.broadcasted_iota(jnp.int32, shape, len(shape) - 1)


def row_ids(shape):
    return lax.broadcasted_iota(jnp.int32, shape, len(shape) - 2)


def dot(a, b):
    return jnp.dot(a, b, preferred_element_type=F32)


def prep_kernel(
    mask, target, conv_t, conv_b, w_out, fwd_w, bwd_w, pred_w, goal, row_mask, col_mask, small
):
    band = lax.axis_index("band")
    first = band + 2 * lax.axis_index("off")
    half_lane = lane_ids((1, 128)) < 64

    blank = jnp.zeros((64, 64), F32)
    for ty in range(3):
        taps = [conv_t[:, (3 * ty + tx) * 64 : (3 * ty + tx + 1) * 64].astype(F32) for tx in range(3)]
        low = jnp.concatenate(taps + [blank], axis=1)
        high = jnp.concatenate([blank] + taps, axis=1)
        fwd_w[ty * 256 : ty * 256 + 256, :] = jnp.concatenate([low, high], axis=0).T.astype(BF16)
        left = taps[::-1] + [blank]
        right = [blank] + taps[::-1]
        for k in range(4):
            row = ty * 256 + k * 64
            bwd_w[row : row + 64, :] = jnp.concatenate([left[k], right[k]], axis=1).astype(BF16)

    bias2 = jnp.concatenate([conv_b[...], conv_b[...]], axis=1)
    twice = jnp.concatenate([w_out[...], w_out[...]], axis=1)
    small[...] = jnp.concatenate([bias2, twice, jnp.zeros((6, 128), F32)], axis=0)
    diagonal = row_ids((128, 128)) == lane_ids((128, 128))
    halves = (row_ids((128, 128)) < 64) == (lane_ids((128, 128)) < 64)
    twice_hi = twice.astype(BF16).astype(F32)
    halves_b = halves.astype(F32).astype(BF16)
    for k, part in enumerate((twice_hi, twice - twice_hi)):
        line = jnp.where(diagonal, part, 0.0).astype(BF16)
        pred_w[k * 128 : k * 128 + 128, :] = dot(line, halves_b).astype(BF16)

    mask_all = mask[...].astype(F32)
    mask_lane = lane_ids((8, 128))
    by_band = jnp.concatenate(
        [jnp.where(mask_lane < 64, mask_all, 0.0), jnp.where(mask_lane < 64, 0.0, mask_all)], axis=0
    ).astype(BF16)
    sums_row = dot(by_band, jnp.ones((128, 128), BF16))
    sums_col = lax.dot_general(
        jnp.ones((16, 128), BF16), by_band, (((1,), (1,)), ((), ())), preferred_element_type=F32
    )
    at = lax.broadcasted_iota(jnp.int32, (16, 16), 0)
    to = lax.broadcasted_iota(jnp.int32, (16, 16), 1)
    apart = (2 * (to % 8) + to // 8) - (2 * (at % 8) + at // 8)
    near_diagonal = (apart >= 0) & (apart < 4)
    count = jnp.sum(jnp.where(near_diagonal, sums_row[:, 0:16] * sums_col, 0.0))
    scale = 1.0 / count

    def mask_rows(which):
        inside = jnp.minimum(which, 15)
        line = mask[pl.ds(inside // 2, 1), :].astype(F32)
        line = jnp.where(which < 16, line, 0.0)
        spot = row_ids((64, 128)) + 64 * (inside % 2)
        spread = jnp.where(lane_ids((64, 128)) == spot, line, 0.0)
        return dot(spread.astype(BF16), jnp.ones((128, 128), BF16))

    row_mask[...] = (
        jnp.broadcast_to(mask_rows(band)[:, None, :] * (2.0 * scale), (64, 8, 128)).reshape(512, 128)
    )
    col_all = jnp.concatenate([mask_rows(first), mask_rows(first + 1)], axis=0).reshape(8, 2, 8, 128)
    col_mask[...] = jnp.where(half_lane, col_all[:, 0].reshape(64, 128), col_all[:, 1].reshape(64, 128))

    line = jnp.concatenate([target[:, 0, :], target[:, 1, :]], axis=1)
    lines = jnp.broadcast_to(line[:, None, :], (64, 8, 128)).reshape(512, 128)
    lines = jnp.where(lane_ids((512, 128)) % 8 == row_ids((512, 128)) % 8, lines, 0.0)
    lines_hi = lines.astype(BF16)
    lines_lo = (lines - lines_hi.astype(F32)).astype(BF16)
    spread = (
        (row_ids((128, 1024)) // 8 == lane_ids((128, 1024)) // 64).astype(F32).astype(BF16)
    )
    goal[...] = dot(
        jnp.concatenate([lines_hi, lines_lo], axis=1), jnp.concatenate([spread, spread], axis=0)
    )


def prep_call(*operands):
    shapes = [
        ((768, 128), BF16), ((768, 128), BF16), ((256, 128), BF16), ((512, 1024), F32), ((512, 128), F32),
        ((64, 128), F32), ((8, 128), F32),
    ]
    return pl.pallas_call(
        prep_kernel,
        out_shape=tuple(jax.ShapeDtypeStruct(shape, kind) for shape, kind in shapes),
        in_specs=[pl.BlockSpec(memory_space=pltpu.VMEM)] * len(operands),
        out_specs=(pl.BlockSpec(memory_space=pltpu.VMEM),) * len(shapes),
        compiler_params=pltpu.CompilerParams(vmem_limit_bytes=16 * 2**20),
        cost_estimate=pl.CostEstimate(flops=3 * 10**8, bytes_accessed=4 * 10**6, transcendentals=0),
        name="prepare",
    )(*operands)


def tile_kernel(
    own, before, after1, after2, after3, after4, w_proj, fwd_w, bwd_w, pred_w, goal, row_mask, col_mask, small,
    out,
    rows_u, cols_v, pair, slope, grads, pre, hid16, hid32, weighted, guess, grad_rows, grad_cols, grad_w, bins,
):
    band = lax.axis_index("band")
    off = lax.axis_index("off")
    first = band + 2 * off
    near = off == 0
    half_lane = lane_ids((1, 128)) < 64

    zero_rows = jnp.zeros((128, 1280), BF16)
    grads[0:128, :] = zero_rows
    grads[640:768, :] = zero_rows
    grads[128:640, 0:128] = jnp.zeros((512, 128), BF16)
    grads[128:640, 1152:1280] = jnp.zeros((512, 128), BF16)
    bins[...] = jnp.zeros(bins.shape, F32)

    feats = jnp.concatenate(
        [before[...], own[...], after1[...], after2[...], after3[...], after4[...]], axis=0
    )
    proj = dot(feats, w_proj[...]).astype(BF16).astype(F32)
    b_before, mine, b_1 = proj[0:16], proj[16:80], proj[80:144]
    b_2, b_3, b_4 = proj[144:208], proj[208:272], proj[272:288]
    u = jnp.concatenate([b_before[8:16], mine, b_1[0:8]], axis=0)
    rows_u[...] = jnp.where(half_lane, u, pltpu.roll(u, 64, 1))
    v = jnp.concatenate(
        [
            jnp.where(near, b_before[8:16], b_1[56:64]),
            jnp.where(near, mine, b_2),
            jnp.where(near, b_1, b_3),
            jnp.where(near, b_2[0:8], b_4[0:8]),
        ],
        axis=0,
    ).reshape(9, 2, 8, 128)
    v_low = v[:, 0].reshape(72, 128)
    v_high = v[:, 1].reshape(72, 128)
    cols_v[...] = jnp.where(half_lane, pltpu.roll(v_low, 64, 1), v_high)

    def pair_step(aq, carry):
        row = pl.multiple_of(aq * 64, 64)
        here = rows_u[pl.ds(pl.multiple_of(aq * 8, 8), 8), :]
        row_at = band * 8 + aq - 1
        row_in = (row_at >= 0) & (row_at < 128)
        for bp in range(9):
            block = first * 8 - 1 + 2 * bp
            spot = jnp.where(half_lane, block, block + 1)
            half = jnp.where((spot >= 0) & (spot < 128) & row_in, 0.5, 0.0)
            x = (here[:, None, :] + cols_v[bp * 8 : bp * 8 + 8, :][None, :, :]).reshape(64, 128)
            value, grade = gelu_parts(x, half)
            pair[pl.ds(row, 64), bp * 128 : bp * 128 + 128] = value.astype(BF16)
            slope[pl.ds(row, 64), bp * 128 : bp * 128 + 128] = grade
        return carry

    lax.fori_loop(0, 10, pair_step, 0)

    bias2 = small[0:1, :]
    out_w2 = small[1:2, :]
    zero8 = jnp.zeros((8, 128), F32)
    totals = (zero8, zero8, zero8)
    for bp in range(8):
        lane = bp * 128
        pre[...] = (
            dot(pair[0:512, lane : lane + 256], fwd_w[0:256, :])
            + dot(pair[64:576, lane : lane + 256], fwd_w[256:512, :])
            + dot(pair[128:640, lane : lane + 256], fwd_w[512:768, :])
        )

        def act_step(aq, carry):
            row = pl.ds(pl.multiple_of(aq * 64, 64), 64)
            value, grade = gelu_parts(pre[row, :] + bias2, 0.5)
            hid32[row, :] = value
            hid16[row, :] = value.astype(BF16)
            weighted[row, :] = grade * out_w2
            return carry

        lax.fori_loop(0, 8, act_step, 0)
        low = hid16[...]
        guess[...] = dot(jnp.concatenate([low, low], axis=1), pred_w[...])

        def loss_step(aq, carry):
            loss_sum, bias_sum, out_sum = carry
            start = pl.multiple_of(aq * 64, 64)
            row = pl.ds(start, 64)
            weight = (row_mask[row, :].reshape(8, 8, 128) * col_mask[bp * 8 : bp * 8 + 8, :][None]).reshape(64, 128)
            residue = guess[row, :] - goal[row, lane : lane + 128]
            grad_pred = weight * residue
            grad_pre = grad_pred * weighted[row, :]
            grads[pl.ds(pl.multiple_of(start + 128, 64), 64), lane + 128 : lane + 256] = grad_pre.astype(BF16)
            loss_sum = loss_sum + jnp.sum((grad_pred * residue).reshape(8, 8, 128), axis=0)
            bias_sum = bias_sum + jnp.sum(grad_pre.reshape(8, 8, 128), axis=0)
            out_sum = out_sum + jnp.sum((grad_pred * hid32[row, :]).reshape(8, 8, 128), axis=0)
            return loss_sum, bias_sum, out_sum

        totals = lax.fori_loop(0, 8, loss_step, totals)

    for bp in range(8):
        lane = bp * 128
        turned = grads[128:640, lane + 128 : lane + 256].T
        for ty in range(3):
            part = dot(turned, pair[ty * 64 : ty * 64 + 512, lane : lane + 256])
            if bp == 0:
                grad_w[:, ty * 256 : ty * 256 + 256] = part
            else:
                grad_w[:, ty * 256 : ty * 256 + 256] += part

    for bp in range(9):
        lane = bp * 128
        part = (
            dot(grads[128:768, lane : lane + 256], bwd_w[0:256, :])
            + dot(grads[64:704, lane : lane + 256], bwd_w[256:512, :])
            + dot(grads[0:640, lane : lane + 256], bwd_w[512:768, :])
        ) * slope[:, lane : lane + 128]
        if bp == 0:
            grad_rows[...] = part
        else:
            grad_rows[...] += part
        grad_cols[bp * 8 : bp * 8 + 8, :] = jnp.sum(part.reshape(80, 8, 128), axis=0)

    row_part = jnp.sum(grad_rows[...].reshape(80, 8, 128), axis=1)
    row_part = jnp.where(half_lane, row_part + pltpu.roll(row_part, 64, 1), 0.0)
    bins[pl.ds(pl.multiple_of(band * 64 + 56, 8), 80), :] += row_part
    col_part = grad_cols[...]
    col_low = pltpu.roll(col_part, 64, 1).reshape(9, 1, 8, 128)
    col_part = jnp.concatenate([col_low, col_part.reshape(9, 1, 8, 128)], axis=1).reshape(144, 128)
    col_part = jnp.where(half_lane, 0.0, col_part)
    bins[pl.ds(pl.multiple_of(first * 64 + 56, 8), 144), :] += col_part
    out[:, 0:32, :] = bins[64:1088, :].reshape(32, 32, 128).astype(BF16)

    none8 = jnp.zeros((8, 128), F32)
    none48 = jnp.zeros((48, 128), F32)

    def if_near(x):
        return jnp.where(near, x, 0.0)

    def if_far(x):
        return jnp.where(near, 0.0, x)

    rows = jnp.concatenate(
        [
            none8,
            row_part[0:8] + if_near(col_part[0:8]),
            row_part[8:72] + if_near(col_part[8:72]),
            row_part[72:80] + if_near(col_part[72:80]),
            if_near(col_part[80:128]),
            jnp.where(near, col_part[128:136], col_part[0:8]),
            jnp.where(near, col_part[136:144], col_part[8:16]),
            if_far(col_part[16:72]),
            if_far(col_part[72:136]),
            if_far(col_part[136:144]),
            none8,
        ],
        axis=0,
    )
    proj_part = dot(rows.T.astype(BF16), feats)
    for k in range(8):
        out[k * 4 : k * 4 + 4, 32:64, :] = (
            proj_part[:, k * 128 : k * 128 + 128].reshape(4, 32, 128).astype(BF16)
        )

    taps = []
    for ty in range(3):
        taps.append(
            grad_w[0:64, ty * 256 : ty * 256 + 192] + grad_w[64:128, ty * 256 + 64 : ty * 256 + 256]
        )
    conv_grad = jnp.concatenate(taps, axis=1)
    wide = jnp.concatenate([conv_grad[:, k * 128 : k * 128 + 128] for k in range(4)], axis=0)
    last = jnp.concatenate([conv_grad[0:32, 512:576], conv_grad[32:64, 512:576]], axis=1)

    loss_sum, bias_sum, out_sum = totals
    bias_row = jnp.sum(bias_sum, axis=0, keepdims=True)
    bias_row = bias_row + pltpu.roll(bias_row, 64, 1)
    out_row = jnp.sum(out_sum, axis=0, keepdims=True)
    out_row = out_row + pltpu.roll(out_row, 64, 1)
    small_row = jnp.where(half_lane, bias_row, out_row)
    loss_row = jnp.broadcast_to(jnp.sum(loss_sum, keepdims=True) * (0.5 / 64.0), (1, 128))
    small_hi = small_row.astype(BF16).astype(F32)
    loss_hi = loss_row.astype(BF16).astype(F32)
    tail = jnp.concatenate(
        [small_hi, small_row - small_hi, loss_hi, loss_row - loss_hi, jnp.zeros((3, 128), F32)], axis=0
    )
    tail = jnp.broadcast_to(tail[None], (PEERS, 7, 128))
    rest = jnp.concatenate([last.reshape(PEERS, 1, 128), tail], axis=1)
    out[:, 64:80, :] = jnp.concatenate([wide.reshape(PEERS, 8, 128), rest], axis=1).astype(BF16)


def tile_call(*operands):
    shapes = [
        ((80, 128), F32), ((72, 128), F32), ((640, 1152), BF16), ((640, 1152), F32), ((768, 1280), BF16),
        ((512, 128), F32), ((512, 128), BF16), ((512, 128), F32), ((512, 128), F32), ((512, 128), F32),
        ((640, 128), F32), ((72, 128), F32), ((128, 768), F32), ((1408, 128), F32),
    ]
    return pl.pallas_call(
        tile_kernel,
        out_shape=jax.ShapeDtypeStruct((PEERS, 80, 128), BF16),
        in_specs=[pl.BlockSpec(memory_space=pltpu.VMEM)] * len(operands),
        out_specs=pl.BlockSpec(memory_space=pltpu.VMEM),
        scratch_shapes=[pltpu.VMEM(shape, kind) for shape, kind in shapes],
        compiler_params=pltpu.CompilerParams(vmem_limit_bytes=40 * 2**20),
        cost_estimate=pl.CostEstimate(flops=2 * 10**9, bytes_accessed=10**6, transcendentals=10**6),
        name="tiles",
    )(*operands)


def sum_kernel(parts, out, mine, small):
    total = jnp.sum(parts[...].astype(F32), axis=0)
    out[...] = jnp.broadcast_to(total[32:80].astype(BF16)[None], (PEERS, SLOT, 128))
    mine[...] = total[0:32].astype(BF16)
    small[0:1, :] = total[73:74] + total[74:75]
    small[1:2, :] = total[75:76] + total[76:77]


def sum_call(parts):
    return pl.pallas_call(
        sum_kernel,
        out_shape=(
            jax.ShapeDtypeStruct((PEERS, SLOT, 128), BF16),
            jax.ShapeDtypeStruct((32, 128), BF16),
            jax.ShapeDtypeStruct((2, 128), F32),
        ),
        in_specs=[pl.BlockSpec(memory_space=pltpu.VMEM)],
        out_specs=(pl.BlockSpec(memory_space=pltpu.VMEM),) * 3,
        name="sums",
    )(parts)


def final_kernel(every, grad_proj, grad_conv_t):
    for k in range(8):
        block = every[k * 4 : k * 4 + 4, 0:32, :].astype(F32).reshape(128, 128)
        grad_proj[k * 128 : k * 128 + 128, :] = block.T
    conv = every[:, 32:48, :].astype(F32)
    wide = conv[:, 0:8].reshape(256, 128)
    for k in range(4):
        grad_conv_t[:, k * 128 : k * 128 + 128] = wide[k * 64 : k * 64 + 64]
    last = conv[:, 8]
    grad_conv_t[0:32, 512:576] = last[:, 0:64]
    grad_conv_t[32:64, 512:576] = last[:, 64:128]


def final_call(every):
    return pl.pallas_call(
        final_kernel,
        out_shape=(jax.ShapeDtypeStruct((1024, 128), F32), jax.ShapeDtypeStruct((64, 576), F32)),
        in_specs=[pl.BlockSpec(memory_space=pltpu.VMEM)],
        out_specs=(pl.BlockSpec(memory_space=pltpu.VMEM),) * 2,
        name="outputs",
    )(every)


def body(feats, w_proj, conv_w, conv_b, w_out, target, mask):
    bands = lax.axis_size("band")

    def moved(x, by, offs=(0, 1)):
        pairs = [(2 * i + o, 2 * (i - by) + o) for i in range(bands) for o in offs if 0 <= i - by < bands]
        return lax.ppermute(x, GROUP, pairs)

    before = moved(feats[48:64], -1)
    after1 = moved(feats, 1)
    after2 = moved(feats, 2)
    after3 = moved(feats, 3, (1,))
    after4 = moved(feats[0:16], 4, (1,))
    ready = prep_call(
        mask.reshape(8, 128), target, conv_w.T, conv_b.reshape(1, 64), w_out.reshape(1, 64)
    )
    sent = tile_call(feats, before, after1, after2, after3, after4, w_proj, *ready)
    parts = lax.all_to_all(sent, GROUP, 0, 0, tiled=True)
    sums, mine, small = sum_call(parts)
    every = lax.all_to_all(sums, GROUP, 0, 0, tiled=True)
    grad_feats = lax.dot_general(
        mine, w_proj, (((1,), (1,)), ((), ())), preferred_element_type=F32
    ).astype(BF16)
    grad_proj, grad_conv_t = final_call(every)
    return (small[1, 0:1], grad_proj, grad_conv_t.T, small[0, 0:64], small[0, 64:128], grad_feats)


def solution(mesh):
    placed = (
        P(("rep", "band"), None),
        P(),
        P(),
        P(),
        P(),
        P(("rep", "band"), "off", None),
        P("rep"),
    )
    return jax.shard_map(
        body,
        mesh=mesh,
        in_specs=placed,
        out_specs=(
            P("rep"),
            P("rep", None),
            P("rep", None),
            P("rep"),
            P("rep"),
            P(("rep", "band", "off"), None),
        ),
        check_vma=False,
    )
```

time: 89.6 us -> 80.8 us (0.902)
  between operations: 14.2 us -> 0.76 us
  blocking collectives: 23.8 us -> 26.2 us
  local copies, waits for them, and re-layouts: 7.46 us -> 9.64 us
  other arithmetic: 1.37 us -> 0 us
  Pallas kernels: 18.9 us -> 20.2 us
  waiting for transfers between devices: 8.32 us -> 7.3 us
    unnamed x12 -> x18, local copies, waits for them, and re-layouts: 3.45 us -> 6.32 us
    all_to_all x1, blocking collectives: 23.8 us -> 26.2 us  [body(): parts = lax.all_to_all(sent, GROUP, 0, 0, tiled=True)]
    reshape x2 -> x0, local copies, waits for them, and re-layouts: 1.11 us -> none  [the longest x1 1 us: body(): fwd_w = toeplitz(conv_w.reshape(3, 192, 64))]
    concatenate x4 -> x0, other arithmetic: 1.09 us -> none  [the longest x1 0.81 us: body(): twice = jnp.concatenate([w_out, w_out])]
    pallas_call x1 -> x2, Pallas kernels: 15.4 us -> 16.3 us  [the longest x1 15.7 us: tile_call(): pl.pallas_call(tile_kernel, out_shape=jax.ShapeDtypeStruct((PEERS, 80, 12...]
  transfers between devices with their start and end apart: 7 -> 6, of which waited for: 1 -> 1; matrix products, arithmetic and copies ran while one was open for 9% -> 5% of each run, Pallas kernels for 19% -> 1%
where the time goes in v1:
time: 80.8 us; the launch traced here: 80.1 us
  blocking collectives  26.2 us (32%)
  Pallas kernels  20.2 us (25%)
  starting transfers between devices  14.5 us (18%)
  local copies, waits for them, and re-layouts  9.64 us (12%)
  waiting for transfers between devices  7.3 us (9%)
  matrix products  1.53 us (2%)
    all_to_all x1, blocking collectives, body(): parts = lax.all_to_all(sent, GROUP, 0, 0, tiled=True)  26.2 us
    pallas_call x1, Pallas kernels, tile_call(): pl.pallas_call(tile_kernel, out_shape=jax.ShapeDtypeStruct((PEERS, 80, 12...  15.7 us
    ppermute x5, starting transfers between devices, moved(): return lax.ppermute(x, GROUP, pairs)  10.1 us
    all_to_all x1, waiting for transfers between devices, body(): every = lax.all_to_all(sums, GROUP, 0, 0, tiled=True)  7.29 us
    unnamed x18, local copies, waits for them, and re-layouts  6.32 us
    all_to_all x1, starting transfers between devices, body(): every = lax.all_to_all(sums, GROUP, 0, 0, tiled=True)  4.34 us
    pallas_call x1, Pallas kernels, final_call(): pl.pallas_call(final_kernel, out_shape=(jax.ShapeDtypeStruct((1024, 128),...  1.97 us
    pallas_call x1, Pallas kernels, sum_call(): pl.pallas_call(sum_kernel, out_shape=(jax.ShapeDtypeStruct((PEERS, SLOT,...  1.94 us
  transfers between devices with their start and end apart: 6, of which 1 were waited for; matrix products, arithmetic and copies ran while one was open for 5% of the time, Pallas kernels for 1%

profile of v1, /device:TPU:1, one launch (start us, length us, event | category | flops | bytes accessed | tf_op | source)
XLA Modules:
  0.0 80.1 jit_solution(3123846866401018249)
XLA Ops:
  0.6 1.3 %collective-permute-start.2 = (bf16[64,1024]{1,0:T(8,128)(2,1)}, bf16[64,1024]{1,0:T(8,128)(2,1)S(1)}, u32[]{:S(2)}, u32[]{:S(2)}) collective-permute-start(bf16[64,1024]{1,0:T(8,128)(2,1)} %own.1), channel_id=1, source_target_pairs={{16,0},{20,4},{24,8},{28,12},{32,16},{36,20},{40,24},{44,28},{48,3... | collective-permute-start | bytes 393224 | tf_op jit(solution)/shard_map/ppermute | solution.py:382
  1.9 3.3 %collective-permute-start.1 = (bf16[64,1024]{1,0:T(8,128)(2,1)}, bf16[64,1024]{1,0:T(8,128)(2,1)S(1)}, u32[]{:S(2)}, u32[]{:S(2)}) collective-permute-start(bf16[64,1024]{1,0:T(8,128)(2,1)} %own.1), channel_id=1, source_target_pairs={{8,0},{12,4},{16,8},{20,12},{24,16},{28,20},{32,24},{36,28},{40,32... | collective-permute-start | bytes 393224 | tf_op jit(solution)/shard_map/ppermute | solution.py:382
  5.3 0.7 collective-permute-start.3
  5.9 0.8 fusion
  6.7 0.7 collective-permute-start.4
  7.4 4.2 %collective-permute-start = (bf16[16,1024]{1,0:T(8,128)(2,1)S(1)}, bf16[16,1024]{1,0:T(8,128)(2,1)S(1)}, u32[]{:S(2)}, u32[]{:S(2)}) collective-permute-start(bf16[16,1024]{1,0:T(8,128)(2,1)S(1)} %get-tuple-element.31), channel_id=1, source_target_pairs={{0,8},{4,12},{8,16},{12,20},{16,24},{20,28},{24,32},{28,36},{32,40... | collective-permute-start | bytes 98312 | tf_op jit(solution)/shard_map/ppermute | solution.py:382
  11.6 0.0 copy-start.3
  11.6 0.9 %copy-done.3 = bf16[576,64]{0,1:T(8,128)(2,1)S(1)} copy-done((bf16[576,64]{0,1:T(8,128)(2,1)S(1)}, bf16[576,64]{0,1:T(8,128)(2,1)}, u32[]{:S(2)}) %copy-start.3) | copy-done | bytes 73752
  12.5 0.8 %copy-done.4 = f32[64,2,64]{2,1,0:T(2,128)S(1)} copy-done((f32[64,2,64]{2,1,0:T(2,128)S(1)}, f32[64,2,64]{2,1,0:T(2,128)}, u32[]{:S(2)}) %copy-start.4) | copy-done | bytes 32792
  13.3 0.7 copy-done.5
  14.0 0.7 copy-done.6
  14.7 0.7 copy-done.7
  15.3 0.6 prepare.1
  15.9 0.0 collective-permute-done.4.after4
  15.9 0.0 collective-permute-done.before
  15.9 0.0 collective-permute-done.2.after2
  16.0 0.0 collective-permute-done.1.after1
  16.0 0.0 collective-permute-done.3.after3
  16.0 0.0 copy-start
  16.0 0.9 %copy-done = bf16[1024,128]{1,0:T(8,128)(2,1)S(1)} copy-done((bf16[1024,128]{1,0:T(8,128)(2,1)S(1)}, bf16[1024,128]{1,0:T(8,128)(2,1)}, u32[]{:S(2)}) %copy-start) | copy-done | bytes 262168
  16.9 0.9 %copy-done.2 = bf16[64,1024]{1,0:T(8,128)(2,1)S(1)} copy-done((bf16[64,1024]{1,0:T(8,128)(2,1)S(1)}, bf16[64,1024]{1,0:T(8,128)(2,1)}, u32[]{:S(2)}) %copy-start.2) | copy-done | bytes 131096
  17.8 15.7 %tiles.1 = bf16[32,80,128]{2,1,0:T(8,128)(2,1)S(1)} custom-call(bf16[64,1024]{1,0:T(8,128)(2,1)S(1)} %copy-done.2, bf16[16,1024]{1,0:T(8,128)(2,1)S(1)} %collective-permute-done.before, bf16[64,1024]{1,0:T(8,128)(2,1)S(1)} %collective-permute-done.1.after1, bf16[64,1024]{1,0:T(8,128)(2,1)S(1)} %collective-permute-done.2.after2, ...), custom_call_target="tpu_custom_call" | custom-call | flops 2000000000 | bytes 1000000 | tf_op jit(solution)/shard_map/tiles/pallas_call | solution.py:320
  33.5 0.0 copy-start.1
  33.5 26.2 %all_to_all.10.parts = bf16[32,80,128]{2,1,0:T(8,128)(2,1)} all-to-all(bf16[32,80,128]{2,1,0:T(8,128)(2,1)S(1)} %tiles.1), channel_id=1, replica_groups=mesh['band'=16,'off'=2,'rep'=4] {'band','off'}, dimensions={0} | all-to-all | bytes 1310720 | tf_op jit(solution)/shard_map/all_to_all | solution.py:393
  59.7 1.9 %sums.1 = (bf16[32,48,128]{2,1,0:T(8,128)(2,1)}, bf16[32,128]{1,0:T(8,128)(2,1)}, f32[2,128]{1,0:T(2,128)}) custom-call(bf16[32,80,128]{2,1,0:T(8,128)(2,1)} %all_to_all.10.parts), custom_call_target="tpu_custom_call" | custom-call | tf_op jit(solution)/shard_map/sums/pallas_call | solution.py:341
  61.7 1.2 %slice.17 = f32[1,1]{1,0:T(1,128)} slice(f32[2,128]{1,0:T(2,128)} %get-tuple-element.25), slice={[1:2], [0:1]} | slice | bytes 8 | tf_op jit(solution)/shard_map/slice | solution.py:400
  62.9 4.3 %all-to-all-start.1 = ((bf16[32,48,128]{2,1,0:T(8,128)(2,1)}), bf16[32,48,128]{2,1,0:T(8,128)(2,1)S(1)}, u32[]{:S(2)}, u32[]{:S(2)}) async-start(bf16[32,48,128]{2,1,0:T(8,128)(2,1)} %get-tuple-element.26), calls=%async_computation.1 | async-start | bytes 786432 | tf_op jit(solution)/shard_map/all_to_all | solution.py:395
  67.2 1.3 %slice_bitcast_fusion = (f32[64]{0:T(128)}, f32[64]{0:T(128)}) fusion(f32[2,128]{1,0:T(2,128)} %get-tuple-element.25), kind=kLoop, calls=%fused_computation.1 | loop fusion | bytes 1024 | tf_op jit(solution)/shard_map/squeeze | solution.py:400
  68.5 1.5 %convolution_convert_fusion = bf16[32,1024]{1,0:T(8,128)(2,1)} fusion(bf16[32,128]{1,0:T(8,128)(2,1)} %get-tuple-element.29, bf16[1024,128]{1,0:T(8,128)(2,1)S(1)} %copy-done.1), kind=kOutput, calls=%fused_computation | convolution fusion | flops 8421376 | bytes 335872 | tf_op jit(solution)/shard_map/dot_general | solution.py:396
  70.1 7.3 %all-to-all-done.1.every = bf16[32,48,128]{2,1,0:T(8,128)(2,1)S(1)} async-done(((bf16[32,48,128]{2,1,0:T(8,128)(2,1)}), bf16[32,48,128]{2,1,0:T(8,128)(2,1)S(1)}, u32[]{:S(2)}, u32[]{:S(2)}) %all-to-all-start.1) | async-done | bytes 393248 | tf_op jit(solution)/shard_map/all_to_all | solution.py:395
  77.4 0.8 copy-done.8
  78.1 2.0 %outputs.1 = (f32[1024,128]{1,0:T(8,128)}, f32[64,576]{1,0:T(8,128)}) custom-call(bf16[32,48,128]{2,1,0:T(8,128)(2,1)} %copy-done.8), custom_call_target="tpu_custom_call" | custom-call | tf_op jit(solution)/shard_map/outputs/pallas_call | solution.py:368
  (7 shorter events, 0.0 us)
Async XLA Ops:
  0.6 15.3 %collective-permute-start.2 = (bf16[64,1024]{1,0:T(8,128)(2,1)}, bf16[64,1024]{1,0:T(8,128)(2,1)S(1)}, u32[]{:S(2)}, u32[]{:S(2)}) collective-permute-start(bf16[64,1024]{1,0:T(8,128)(2,1)} %own.1), channel_id=1, source_target_pairs={{16,0},{20,4},{24,8},{28,12},{32,16},{36,20},{40,24},{44,28},{48,3... | collective-permute-start | bytes 393224 | tf_op jit(solution)/shard_map/ppermute | solution.py:382
  1.9 14.0 %collective-permute-start.1 = (bf16[64,1024]{1,0:T(8,128)(2,1)}, bf16[64,1024]{1,0:T(8,128)(2,1)S(1)}, u32[]{:S(2)}, u32[]{:S(2)}) collective-permute-start(bf16[64,1024]{1,0:T(8,128)(2,1)} %own.1), channel_id=1, source_target_pairs={{8,0},{12,4},{16,8},{20,12},{24,16},{28,20},{32,24},{36,28},{40,32... | collective-permute-start | bytes 393224 | tf_op jit(solution)/shard_map/ppermute | solution.py:382
  5.3 10.7 %collective-permute-start.3 = (bf16[64,1024]{1,0:T(8,128)(2,1)}, bf16[64,1024]{1,0:T(8,128)(2,1)S(1)}, u32[]{:S(2)}, u32[]{:S(2)}) collective-permute-start(bf16[64,1024]{1,0:T(8,128)(2,1)} %own.1), channel_id=1, source_target_pairs={{28,4},{36,12},{44,20},{52,28},{60,36},{68,44},{76,52},{84,60},{92... | collective-permute-start | bytes 393224 | tf_op jit(solution)/shard_map/ppermute | solution.py:382
  6.7 9.2 %collective-permute-start.4 = (bf16[16,1024]{1,0:T(8,128)(2,1)S(1)}, bf16[16,1024]{1,0:T(8,128)(2,1)S(1)}, u32[]{:S(2)}, u32[]{:S(2)}) collective-permute-start(bf16[16,1024]{1,0:T(8,128)(2,1)S(1)} %get-tuple-element.30), channel_id=1, source_target_pairs={{36,4},{44,12},{52,20},{60,28},{68,36},{76,44},{84,52},{92,60},{10... | collective-permute-start | bytes 98312 | tf_op jit(solution)/shard_map/ppermute | solution.py:382
  7.4 8.5 %collective-permute-start = (bf16[16,1024]{1,0:T(8,128)(2,1)S(1)}, bf16[16,1024]{1,0:T(8,128)(2,1)S(1)}, u32[]{:S(2)}, u32[]{:S(2)}) collective-permute-start(bf16[16,1024]{1,0:T(8,128)(2,1)S(1)} %get-tuple-element.31), channel_id=1, source_target_pairs={{0,8},{4,12},{8,16},{12,20},{16,24},{20,28},{24,32},{28,36},{32,40... | collective-permute-start | bytes 98312 | tf_op jit(solution)/shard_map/ppermute | solution.py:382
  11.6 0.9 %copy-start.3 = (bf16[576,64]{0,1:T(8,128)(2,1)S(1)}, bf16[576,64]{0,1:T(8,128)(2,1)}, u32[]{:S(2)}) copy-start(bf16[576,64]{0,1:T(8,128)(2,1)} %param.9) | copy-start | bytes 221188
  12.5 0.8 %copy-start.4 = (f32[64,2,64]{2,1,0:T(2,128)S(1)}, f32[64,2,64]{2,1,0:T(2,128)}, u32[]{:S(2)}) copy-start(f32[64,2,64]{2,1,0:T(2,128)} %target.1) | copy-start | bytes 98308
  13.3 0.7 copy-start.5
  14.0 0.7 copy-start.6
  14.7 0.7 copy-start.7
  16.0 1.0 %copy-start = (bf16[1024,128]{1,0:T(8,128)(2,1)S(1)}, bf16[1024,128]{1,0:T(8,128)(2,1)}, u32[]{:S(2)}) copy-start(bf16[1024,128]{1,0:T(8,128)(2,1)} %w_proj.1) | copy-start | bytes 786436
  16.9 0.9 %copy-start.2 = (bf16[64,1024]{1,0:T(8,128)(2,1)S(1)}, bf16[64,1024]{1,0:T(8,128)(2,1)}, u32[]{:S(2)}) copy-start(bf16[64,1024]{1,0:T(8,128)(2,1)} %own.1) | copy-start | bytes 393220
  33.5 35.0 %copy-start.1 = (bf16[1024,128]{1,0:T(8,128)(2,1)S(1)}, bf16[1024,128]{1,0:T(8,128)(2,1)}, u32[]{:S(2)}) copy-start(bf16[1024,128]{1,0:T(8,128)(2,1)} %w_proj.1) | copy-start | bytes 786436
  62.9 14.5 %all-to-all-start.1 = ((bf16[32,48,128]{2,1,0:T(8,128)(2,1)}), bf16[32,48,128]{2,1,0:T(8,128)(2,1)S(1)}, u32[]{:S(2)}, u32[]{:S(2)}) async-start(bf16[32,48,128]{2,1,0:T(8,128)(2,1)} %get-tuple-element.26), calls=%async_computation.1 | async-start | bytes 786432 | tf_op jit(solution)/shard_map/all_to_all | solution.py:395
  77.4 0.8 copy-start.8

commit v2 on v1

--- a/solution.py
+++ b/solution.py
@@ -9,7 +9,7 @@
 GELU_C = 0.044715
 GROUP = ("band", "off")
 PEERS = 32
-SLOT = 48
+BANDS = 16
 F32 = jnp.float32
 BF16 = jnp.bfloat16
 
@@ -34,6 +34,33 @@
 
 def dot(a, b):
     return jnp.dot(a, b, preferred_element_type=F32)
+
+
+def front_kernel(feats, w_proj, out):
+    off = lax.axis_index("off")
+    proj = dot(feats[...], w_proj[...]).astype(BF16)
+    out[:, 0:64, :] = jnp.broadcast_to(proj[None], (BANDS, 64, 128))
+    group = lane_ids((16, 128)) // 32
+    for q in range(8):
+        block = feats[:, q * 128 : q * 128 + 128].astype(F32)
+        for half in range(2):
+            piece = 2 * half + off
+            packed = jnp.zeros((16, 128), F32)
+            for g in range(4):
+                turned = pltpu.roll(block[g * 16 : g * 16 + 16], lax.rem(g - piece + 4, 4) * 32, 1)
+                packed = jnp.where(group == g, turned, packed)
+            out[2 * q + half, 64:80, :] = packed.astype(BF16)
+
+
+def front_call(feats, w_proj):
+    return pl.pallas_call(
+        front_kernel,
+        out_shape=jax.ShapeDtypeStruct((BANDS, 80, 128), BF16),
+        in_specs=[pl.BlockSpec(memory_space=pltpu.VMEM)] * 2,
+        out_specs=pl.BlockSpec(memory_space=pltpu.VMEM),
+        compiler_params=pltpu.CompilerParams(vmem_limit_bytes=16 * 2**20),
+        name="front",
+    )(feats, w_proj)
 
 
 def prep_kernel(
@@ -126,14 +153,12 @@
 
 
 def tile_kernel(
-    own, before, after1, after2, after3, after4, w_proj, fwd_w, bwd_w, pred_w, goal, row_mask, col_mask, small,
+    proj, fwd_w, bwd_w, pred_w, goal, row_mask, col_mask, small,
     out,
-    rows_u, cols_v, pair, slope, grads, pre, hid16, hid32, weighted, guess, grad_rows, grad_cols, grad_w, bins,
+    rows_u, cols_v, pair, slope, grads, pre, hid16, hid32, weighted, guess, grad_rows, grad_cols, grad_w,
 ):
     band = lax.axis_index("band")
-    off = lax.axis_index("off")
-    first = band + 2 * off
-    near = off == 0
+    first = band + 2 * lax.axis_index("off")
     half_lane = lane_ids((1, 128)) < 64
 
     zero_rows = jnp.zeros((128, 1280), BF16)
@@ -141,24 +166,20 @@
     grads[640:768, :] = zero_rows
     grads[128:640, 0:128] = jnp.zeros((512, 128), BF16)
     grads[128:640, 1152:1280] = jnp.zeros((512, 128), BF16)
-    bins[...] = jnp.zeros(bins.shape, F32)
-
-    feats = jnp.concatenate(
-        [before[...], own[...], after1[...], after2[...], after3[...], after4[...]], axis=0
-    )
-    proj = dot(feats, w_proj[...]).astype(BF16).astype(F32)
-    b_before, mine, b_1 = proj[0:16], proj[16:80], proj[80:144]
-    b_2, b_3, b_4 = proj[144:208], proj[208:272], proj[272:288]
-    u = jnp.concatenate([b_before[8:16], mine, b_1[0:8]], axis=0)
+
+    def ending(which):
+        return proj[jnp.clip(which, 0, BANDS - 1), 48:64, :].astype(F32)[8:16]
+
+    def whole(which):
+        return proj[jnp.minimum(which, BANDS - 1), 0:64, :].astype(F32)
+
+    def opening(which):
+        return proj[jnp.minimum(which, BANDS - 1), 0:16, :].astype(F32)[0:8]
+
+    u = jnp.concatenate([ending(band - 1), whole(band), opening(band + 1)], axis=0)
     rows_u[...] = jnp.where(half_lane, u, pltpu.roll(u, 64, 1))
     v = jnp.concatenate(
-        [
-            jnp.where(near, b_before[8:16], b_1[56:64]),
-            jnp.where(near, mine, b_2),
-            jnp.where(near, b_1, b_3),
-            jnp.where(near, b_2[0:8], b_4[0:8]),
-        ],
-        axis=0,
+        [ending(first - 1), whole(first), whole(first + 1), opening(first + 2)], axis=0
     ).reshape(9, 2, 8, 128)
     v_low = v[:, 0].reshape(72, 128)
     v_high = v[:, 1].reshape(72, 128)
@@ -245,45 +266,13 @@
         grad_cols[bp * 8 : bp * 8 + 8, :] = jnp.sum(part.reshape(80, 8, 128), axis=0)
 
     row_part = jnp.sum(grad_rows[...].reshape(80, 8, 128), axis=1)
-    row_part = jnp.where(half_lane, row_part + pltpu.roll(row_part, 64, 1), 0.0)
-    bins[pl.ds(pl.multiple_of(band * 64 + 56, 8), 80), :] += row_part
+    row_part = row_part + pltpu.roll(row_part, 64, 1)
     col_part = grad_cols[...]
     col_low = pltpu.roll(col_part, 64, 1).reshape(9, 1, 8, 128)
     col_part = jnp.concatenate([col_low, col_part.reshape(9, 1, 8, 128)], axis=1).reshape(144, 128)
-    col_part = jnp.where(half_lane, 0.0, col_part)
-    bins[pl.ds(pl.multiple_of(first * 64 + 56, 8), 144), :] += col_part
-    out[:, 0:32, :] = bins[64:1088, :].reshape(32, 32, 128).astype(BF16)
-
-    none8 = jnp.zeros((8, 128), F32)
-    none48 = jnp.zeros((48, 128), F32)
-
-    def if_near(x):
-        return jnp.where(near, x, 0.0)
-
-    def if_far(x):
-        return jnp.where(near, 0.0, x)
-
-    rows = jnp.concatenate(
-        [
-            none8,
-            row_part[0:8] + if_near(col_part[0:8]),
-            row_part[8:72] + if_near(col_part[8:72]),
-            row_part[72:80] + if_near(col_part[72:80]),
-            if_near(col_part[80:128]),
-            jnp.where(near, col_part[128:136], col_part[0:8]),
-            jnp.where(near, col_part[136:144], col_part[8:16]),
-            if_far(col_part[16:72]),
-            if_far(col_part[72:136]),
-            if_far(col_part[136:144]),
-            none8,
-        ],
-        axis=0,
-    )
-    proj_part = dot(rows.T.astype(BF16), feats)
-    for k in range(8):
-        out[k * 4 : k * 4 + 4, 32:64, :] = (
-            proj_part[:, k * 128 : k * 128 + 128].reshape(4, 32, 128).astype(BF16)
-        )
+    spare = pltpu.roll(col_part[112:144], 64, 1)
+    packed = jnp.where(half_lane, jnp.concatenate([row_part, spare], axis=0), col_part[0:112])
+    out[:, 0:112, :] = jnp.broadcast_to(packed.astype(BF16)[None], (PEERS, 112, 128))
 
     taps = []
     for ty in range(3):
@@ -308,18 +297,18 @@
     )
     tail = jnp.broadcast_to(tail[None], (PEERS, 7, 128))
     rest = jnp.concatenate([last.reshape(PEERS, 1, 128), tail], axis=1)
-    out[:, 64:80, :] = jnp.concatenate([wide.reshape(PEERS, 8, 128), rest], axis=1).astype(BF16)
+    out[:, 112:128, :] = jnp.concatenate([wide.reshape(PEERS, 8, 128), rest], axis=1).astype(BF16)
 
 
 def tile_call(*operands):
     shapes = [
         ((80, 128), F32), ((72, 128), F32), ((640, 1152), BF16), ((640, 1152), F32), ((768, 1280), BF16),
         ((512, 128), F32), ((512, 128), BF16), ((512, 128), F32), ((512, 128), F32), ((512, 128), F32),
-        ((640, 128), F32), ((72, 128), F32), ((128, 768), F32), ((1408, 128), F32),
+        ((640, 128), F32), ((72, 128), F32), ((128, 768), F32),
     ]
     return pl.pallas_call(
         tile_kernel,
-        out_shape=jax.ShapeDtypeStruct((PEERS, 80, 128), BF16),
+        out_shape=jax.ShapeDtypeStruct((PEERS, 128, 128), BF16),
         in_specs=[pl.BlockSpec(memory_space=pltpu.VMEM)] * len(operands),
         out_specs=pl.BlockSpec(memory_space=pltpu.VMEM),
         scratch_shapes=[pltpu.VMEM(shape, kind) for shape, kind in shapes],
@@ -329,32 +318,52 @@
     )(*operands)
 
 
-def sum_kernel(parts, out, mine, small):
-    total = jnp.sum(parts[...].astype(F32), axis=0)
-    out[...] = jnp.broadcast_to(total[32:80].astype(BF16)[None], (PEERS, SLOT, 128))
-    mine[...] = total[0:32].astype(BF16)
-    small[0:1, :] = total[73:74] + total[74:75]
-    small[1:2, :] = total[75:76] + total[76:77]
-
-
-def sum_call(parts):
+def sum_kernel(parts, cols, out, mine, small, bins):
+    me = 2 * lax.axis_index("band") + lax.axis_index("off")
+    half_lane = lane_ids((1, 128)) < 64
+    bins[...] = jnp.zeros(bins.shape, F32)
+    for band in range(BANDS):
+        for off in range(2):
+            piece = parts[2 * band + off, 0:112, :].astype(F32)
+            bins[band * 64 + 56 : band * 64 + 136, :] += jnp.where(half_lane, piece[0:80], 0.0)
+            start = (band + 2 * off) * 64 + 56
+            bins[start : start + 112, :] += jnp.where(half_lane, 0.0, piece)
+            spare = pltpu.roll(piece[80:112], 64, 1)
+            bins[start + 112 : start + 144, :] += jnp.where(half_lane, 0.0, spare)
+    gproj = bins[64:1088, :].astype(BF16).reshape(BANDS, 4, 16, 128)
+    mine[...] = bins[pl.ds(pl.multiple_of(64 + 32 * me, 32), 32), :].astype(BF16)
+    wide = jnp.concatenate([gproj[:, g].reshape(256, 128) for g in range(4)], axis=1)
+    product = lax.dot_general(
+        cols[:, 64:80, :].reshape(256, 128), wide, (((0,), (0,)), ((), ())), preferred_element_type=F32
+    )
+    rows = product[0:32, 0:128]
+    for g in range(1, 4):
+        rows = rows + product[g * 32 : g * 32 + 32, g * 128 : g * 128 + 128]
+    total = jnp.sum(parts[:, 112:128, :].astype(F32), axis=0)
+    out[:, 0:32, :] = jnp.broadcast_to(rows.astype(BF16)[None], (PEERS, 32, 128))
+    out[:, 32:48, :] = jnp.broadcast_to(total.astype(BF16)[None], (PEERS, 16, 128))
+    small[0:1, :] = total[9:10] + total[10:11]
+    small[1:2, :] = total[11:12] + total[12:13]
+
+
+def sum_call(parts, cols):
     return pl.pallas_call(
         sum_kernel,
         out_shape=(
-            jax.ShapeDtypeStruct((PEERS, SLOT, 128), BF16),
+            jax.ShapeDtypeStruct((PEERS, 48, 128), BF16),
             jax.ShapeDtypeStruct((32, 128), BF16),
             jax.ShapeDtypeStruct((2, 128), F32),
         ),
-        in_specs=[pl.BlockSpec(memory_space=pltpu.VMEM)],
+        in_specs=[pl.BlockSpec(memory_space=pltpu.VMEM)] * 2,
         out_specs=(pl.BlockSpec(memory_space=pltpu.VMEM),) * 3,
+        scratch_shapes=[pltpu.VMEM((1408, 128), F32)],
+        compiler_params=pltpu.CompilerParams(vmem_limit_bytes=16 * 2**20),
         name="sums",
-    )(parts)
+    )(parts, cols)
 
 
 def final_kernel(every, grad_proj, grad_conv_t):
-    for k in range(8):
-        block = every[k * 4 : k * 4 + 4, 0:32, :].astype(F32).reshape(128, 128)
-        grad_proj[k * 128 : k * 128 + 128, :] = block.T
+    grad_proj[...] = every[:, 0:32, :].astype(F32).reshape(1024, 128)
     conv = every[:, 32:48, :].astype(F32)
     wide = conv[:, 0:8].reshape(256, 128)
     for k in range(4):
@@ -375,23 +384,12 @@
 
 
 def body(feats, w_proj, conv_w, conv_b, w_out, target, mask):
-    bands = lax.axis_size("band")
-
-    def moved(x, by, offs=(0, 1)):
-        pairs = [(2 * i + o, 2 * (i - by) + o) for i in range(bands) for o in offs if 0 <= i - by < bands]
-        return lax.ppermute(x, GROUP, pairs)
-
-    before = moved(feats[48:64], -1)
-    after1 = moved(feats, 1)
-    after2 = moved(feats, 2)
-    after3 = moved(feats, 3, (1,))
-    after4 = moved(feats[0:16], 4, (1,))
+    spread = lax.all_to_all(front_call(feats, w_proj), "band", 0, 0, tiled=True)
     ready = prep_call(
         mask.reshape(8, 128), target, conv_w.T, conv_b.reshape(1, 64), w_out.reshape(1, 64)
     )
-    sent = tile_call(feats, before, after1, after2, after3, after4, w_proj, *ready)
-    parts = lax.all_to_all(sent, GROUP, 0, 0, tiled=True)
-    sums, mine, small = sum_call(parts)
+    parts = lax.all_to_all(tile_call(spread, *ready), GROUP, 0, 0, tiled=True)
+    sums, mine, small = sum_call(parts, spread)
     every = lax.all_to_all(sums, GROUP, 0, 0, tiled=True)
     grad_feats = lax.dot_general(
         mine, w_proj, (((1,), (1,)), ((), ())), preferred_element_type=F32

time: 80.8 us -> 75 us (0.928)
  waiting for transfers between devices: 7.3 us -> 12 us
  blocking collectives: 26.2 us -> 22.7 us
  starting transfers between devices: 14.5 us -> 11.2 us
  local copies, waits for them, and re-layouts: 9.64 us -> 7.43 us
    ppermute x5 -> x0, starting transfers between devices: 10.1 us -> none  [moved(): return lax.ppermute(x, GROUP, pairs)]
    all_to_all x0 -> x1, starting transfers between devices: none -> 6.83 us  [body(): spread = lax.all_to_all(front_call(feats, w_proj), 'band', 0, 0, tiled=True)]
    all_to_all x1, blocking collectives: 26.2 us -> 22.7 us  [body(): parts = lax.all_to_all(tile_call(spread, *ready), GROUP, 0, 0, tiled=True)]
    all_to_all x0 -> x1, waiting for transfers between devices: none -> 3.29 us  [body(): spread = lax.all_to_all(front_call(feats, w_proj), 'band', 0, 0, tiled=True)]
    all_to_all x1, waiting for transfers between devices: 7.29 us -> 8.74 us  [body(): every = lax.all_to_all(sums, GROUP, 0, 0, tiled=True)]
    pallas_call x2 -> x3, Pallas kernels: 17.6 us -> 17.2 us  [the longest x1 15 us: tile_call(): pl.pallas_call(tile_kernel, out_shape=jax.ShapeDtypeStruct((PEERS, 128, 1...]
  transfers between devices with their start and end apart: 6 -> 2, of which waited for: 1 -> 2; matrix products, arithmetic and copies ran while one was open for 5% -> 2% of each run, Pallas kernels for 1% -> 1%
where the time goes in v2:
time: 75 us; the launch traced here: 74.5 us
  blocking collectives  22.7 us (30%)
  Pallas kernels  19.7 us (26%)
  waiting for transfers between devices  12 us (16%)
  starting transfers between devices  11.2 us (15%)
  local copies, waits for them, and re-layouts  7.43 us (10%)
  matrix products  0.83 us (1%)
    all_to_all x1, blocking collectives, body(): parts = lax.all_to_all(tile_call(spread, *ready), GROUP, 0, 0, tiled=True)  22.7 us
    pallas_call x1, Pallas kernels, tile_call(): pl.pallas_call(tile_kernel, out_shape=jax.ShapeDtypeStruct((PEERS, 128, 1...  15 us
    all_to_all x1, waiting for transfers between devices, body(): every = lax.all_to_all(sums, GROUP, 0, 0, tiled=True)  8.74 us
    all_to_all x1, starting transfers between devices, body(): spread = lax.all_to_all(front_call(feats, w_proj), 'band', 0, 0, tiled=True)  6.83 us
    unnamed x18, local copies, waits for them, and re-layouts  6.33 us
    all_to_all x1, starting transfers between devices, body(): every = lax.all_to_all(sums, GROUP, 0, 0, tiled=True)  4.36 us
    all_to_all x1, waiting for transfers between devices, body(): spread = lax.all_to_all(front_call(feats, w_proj), 'band', 0, 0, tiled=True)  3.29 us
    pallas_call x1, Pallas kernels, final_call(): pl.pallas_call(final_kernel, out_shape=(jax.ShapeDtypeStruct((1024, 128),...  1.88 us
  transfers between devices with their start and end apart: 2, of which 2 were waited for; matrix products, arithmetic and copies ran while one was open for 2% of the time, Pallas kernels for 1%

profile of v2, /device:TPU:1, one launch (start us, length us, event | category | flops | bytes accessed | tf_op | source)
XLA Modules:
  0.0 74.5 jit_solution(4184566802203236417)
XLA Ops:
  0.6 0.0 copy-start
  0.6 0.9 %copy-done = bf16[1024,128]{1,0:T(8,128)(2,1)S(1)} copy-done((bf16[1024,128]{1,0:T(8,128)(2,1)S(1)}, bf16[1024,128]{1,0:T(8,128)(2,1)}, u32[]{:S(2)}) %copy-start) | copy-done | bytes 262168
  1.6 0.0 copy-start.2
  1.6 0.9 %copy-done.2 = bf16[64,1024]{1,0:T(8,128)(2,1)S(1)} copy-done((bf16[64,1024]{1,0:T(8,128)(2,1)S(1)}, bf16[64,1024]{1,0:T(8,128)(2,1)}, u32[]{:S(2)}) %copy-start.2) | copy-done | bytes 131096
  2.5 0.9 %front.1 = bf16[16,80,128]{2,1,0:T(8,128)(2,1)} custom-call(bf16[64,1024]{1,0:T(8,128)(2,1)S(1)} %copy-done.2, bf16[1024,128]{1,0:T(8,128)(2,1)S(1)} %copy-done), custom_call_target="tpu_custom_call" | custom-call | tf_op jit(solution)/shard_map/front/pallas_call | solution.py:56
  3.4 6.8 %all-to-all-start = ((bf16[16,80,128]{2,1,0:T(8,128)(2,1)}), bf16[16,80,128]{2,1,0:T(8,128)(2,1)S(1)}, u32[]{:S(2)}, u32[]{:S(2)}) async-start(bf16[16,80,128]{2,1,0:T(8,128)(2,1)} %front.1), calls=%async_computation | async-start | bytes 655360 | tf_op jit(solution)/shard_map/all_to_all | solution.py:387
  10.2 0.0 copy-start.3
  10.2 0.9 %copy-done.3 = bf16[576,64]{0,1:T(8,128)(2,1)S(1)} copy-done((bf16[576,64]{0,1:T(8,128)(2,1)S(1)}, bf16[576,64]{0,1:T(8,128)(2,1)}, u32[]{:S(2)}) %copy-start.3) | copy-done | bytes 73752
  11.1 0.0 copy-start.4
  11.1 0.8 %copy-done.4 = f32[64,2,64]{2,1,0:T(2,128)S(1)} copy-done((f32[64,2,64]{2,1,0:T(2,128)S(1)}, f32[64,2,64]{2,1,0:T(2,128)}, u32[]{:S(2)}) %copy-start.4) | copy-done | bytes 32792
  12.0 0.0 copy-start.5
  12.0 0.7 copy-done.5
  12.6 0.0 copy-start.6
  12.7 0.7 copy-done.6
  13.3 0.0 copy-start.7
  13.3 0.7 copy-done.7
  14.0 0.6 prepare.1
  14.6 3.3 %all-to-all-done.proj.cols = bf16[16,80,128]{2,1,0:T(8,128)(2,1)S(1)} async-done(((bf16[16,80,128]{2,1,0:T(8,128)(2,1)}), bf16[16,80,128]{2,1,0:T(8,128)(2,1)S(1)}, u32[]{:S(2)}, u32[]{:S(2)}) %all-to-all-start) | async-done | bytes 327712 | tf_op jit(solution)/shard_map/all_to_all | solution.py:387
  17.9 15.0 %tiles.1 = bf16[32,128,128]{2,1,0:T(8,128)(2,1)S(1)} custom-call(bf16[16,80,128]{2,1,0:T(8,128)(2,1)S(1)} %all-to-all-done.proj.cols, bf16[768,128]{1,0:T(8,128)(2,1)S(1)} %get-tuple-element.18.fwd_w, bf16[768,128]{1,0:T(8,128)(2,1)S(1)} %get-tuple-element.19.bwd_w, bf16[256,128]{1,0:T(8,128)(2,1)S(1)} %get-tuple-element.20.pred_w, ...), custom_call_target="tpu_custom_call" | custom-call | flops 2000000000 | bytes 1000000 | tf_op jit(solution)/shard_map/tiles/pallas_call | solution.py:309
  32.9 0.0 copy-start.1
  32.9 22.7 %all_to_all.15.parts = bf16[32,128,128]{2,1,0:T(8,128)(2,1)S(1)} all-to-all(bf16[32,128,128]{2,1,0:T(8,128)(2,1)S(1)} %tiles.1), channel_id=1, replica_groups=mesh['band'=16,'off'=2,'rep'=4] {'band','off'}, dimensions={0} | all-to-all | bytes 2097152 | tf_op jit(solution)/shard_map/all_to_all | solution.py:391
  55.6 1.3 %sums.1 = (bf16[32,48,128]{2,1,0:T(8,128)(2,1)}, bf16[32,128]{1,0:T(8,128)(2,1)S(1)}, f32[2,128]{1,0:T(2,128)S(1)}) custom-call(bf16[32,128,128]{2,1,0:T(8,128)(2,1)S(1)} %all_to_all.15.parts, bf16[16,80,128]{2,1,0:T(8,128)(2,1)S(1)} %all-to-all-done.proj.cols), custom_call_target="tpu_custom_call" | custom-call | tf_op jit(solution)/shard_map/sums/pallas_call | solution.py:350
  56.8 0.5 slice.9
  57.3 4.4 %all-to-all-start.2 = ((bf16[32,48,128]{2,1,0:T(8,128)(2,1)}), bf16[32,48,128]{2,1,0:T(8,128)(2,1)S(1)}, u32[]{:S(2)}, u32[]{:S(2)}) async-start(bf16[32,48,128]{2,1,0:T(8,128)(2,1)} %get-tuple-element.26), calls=%async_computation.2 | async-start | bytes 786432 | tf_op jit(solution)/shard_map/all_to_all | solution.py:393
  61.7 0.6 slice_bitcast_fusion
  62.3 0.0 copy-done.1
  62.3 0.8 %convolution_convert_fusion = bf16[32,1024]{1,0:T(8,128)(2,1)} fusion(bf16[32,128]{1,0:T(8,128)(2,1)S(1)} %get-tuple-element.29, bf16[1024,128]{1,0:T(8,128)(2,1)S(1)} %copy-done.1), kind=kOutput, calls=%fused_computation | convolution fusion | flops 8421376 | bytes 335872 | tf_op jit(solution)/shard_map/dot_general | solution.py:394
  63.1 8.7 %all-to-all-done.2.every = bf16[32,48,128]{2,1,0:T(8,128)(2,1)S(1)} async-done(((bf16[32,48,128]{2,1,0:T(8,128)(2,1)}), bf16[32,48,128]{2,1,0:T(8,128)(2,1)S(1)}, u32[]{:S(2)}, u32[]{:S(2)}) %all-to-all-start.2) | async-done | bytes 393248 | tf_op jit(solution)/shard_map/all_to_all | solution.py:393
  71.9 0.0 copy-start.8
  71.9 0.8 %copy-done.8 = bf16[32,48,128]{2,1,0:T(8,128)(2,1)} copy-done((bf16[32,48,128]{2,1,0:T(8,128)(2,1)}, bf16[32,48,128]{2,1,0:T(8,128)(2,1)S(1)}, u32[]{:S(2)}) %copy-start.8) | copy-done | bytes 393240
  72.6 1.9 %outputs.1 = (f32[1024,128]{1,0:T(8,128)}, f32[64,576]{1,0:T(8,128)}) custom-call(bf16[32,48,128]{2,1,0:T(8,128)(2,1)} %copy-done.8), custom_call_target="tpu_custom_call" | custom-call | tf_op jit(solution)/shard_map/outputs/pallas_call | solution.py:377
Async XLA Ops:
  0.6 1.0 %copy-start = (bf16[1024,128]{1,0:T(8,128)(2,1)S(1)}, bf16[1024,128]{1,0:T(8,128)(2,1)}, u32[]{:S(2)}) copy-start(bf16[1024,128]{1,0:T(8,128)(2,1)} %w_proj.1) | copy-start | bytes 786436
  1.6 0.9 %copy-start.2 = (bf16[64,1024]{1,0:T(8,128)(2,1)S(1)}, bf16[64,1024]{1,0:T(8,128)(2,1)}, u32[]{:S(2)}) copy-start(bf16[64,1024]{1,0:T(8,128)(2,1)} %feats.1) | copy-start | bytes 393220
  3.4 14.4 %all-to-all-start = ((bf16[16,80,128]{2,1,0:T(8,128)(2,1)}), bf16[16,80,128]{2,1,0:T(8,128)(2,1)S(1)}, u32[]{:S(2)}, u32[]{:S(2)}) async-start(bf16[16,80,128]{2,1,0:T(8,128)(2,1)} %front.1), calls=%async_computation | async-start | bytes 655360 | tf_op jit(solution)/shard_map/all_to_all | solution.py:387
  10.2 0.9 %copy-start.3 = (bf16[576,64]{0,1:T(8,128)(2,1)S(1)}, bf16[576,64]{0,1:T(8,128)(2,1)}, u32[]{:S(2)}) copy-start(bf16[576,64]{0,1:T(8,128)(2,1)} %param.9) | copy-start | bytes 221188
  11.1 0.8 %copy-start.4 = (f32[64,2,64]{2,1,0:T(2,128)S(1)}, f32[64,2,64]{2,1,0:T(2,128)}, u32[]{:S(2)}) copy-start(f32[64,2,64]{2,1,0:T(2,128)} %target.1) | copy-start | bytes 98308
  12.0 0.7 copy-start.5
  12.6 0.7 copy-start.6
  13.3 0.7 copy-start.7
  32.9 29.4 %copy-start.1 = (bf16[1024,128]{1,0:T(8,128)(2,1)S(1)}, bf16[1024,128]{1,0:T(8,128)(2,1)}, u32[]{:S(2)}) copy-start(bf16[1024,128]{1,0:T(8,128)(2,1)} %w_proj.1) | copy-start | bytes 786436
  57.3 14.5 %all-to-all-start.2 = ((bf16[32,48,128]{2,1,0:T(8,128)(2,1)}), bf16[32,48,128]{2,1,0:T(8,128)(2,1)S(1)}, u32[]{:S(2)}, u32[]{:S(2)}) async-start(bf16[32,48,128]{2,1,0:T(8,128)(2,1)} %get-tuple-element.26), calls=%async_computation.2 | async-start | bytes 786432 | tf_op jit(solution)/shard_map/all_to_all | solution.py:393
  71.9 0.8 %copy-start.8 = (bf16[32,48,128]{2,1,0:T(8,128)(2,1)}, bf16[32,48,128]{2,1,0:T(8,128)(2,1)S(1)}, u32[]{:S(2)}) copy-start(bf16[32,48,128]{2,1,0:T(8,128)(2,1)S(1)} %all-to-all-done.2.every) | copy-start | bytes 1179652

commit v3 on v2

--- a/solution.py
+++ b/solution.py
@@ -202,45 +202,53 @@
 
     lax.fori_loop(0, 10, pair_step, 0)
 
-    bias2 = small[0:1, :]
-    out_w2 = small[1:2, :]
-    zero8 = jnp.zeros((8, 128), F32)
-    totals = (zero8, zero8, zero8)
     for bp in range(8):
         lane = bp * 128
-        pre[...] = (
+        pre[:, lane : lane + 128] = (
             dot(pair[0:512, lane : lane + 256], fwd_w[0:256, :])
             + dot(pair[64:576, lane : lane + 256], fwd_w[256:512, :])
             + dot(pair[128:640, lane : lane + 256], fwd_w[512:768, :])
         )
 
-        def act_step(aq, carry):
-            row = pl.ds(pl.multiple_of(aq * 64, 64), 64)
-            value, grade = gelu_parts(pre[row, :] + bias2, 0.5)
-            hid32[row, :] = value
-            hid16[row, :] = value.astype(BF16)
-            weighted[row, :] = grade * out_w2
-            return carry
-
-        lax.fori_loop(0, 8, act_step, 0)
-        low = hid16[...]
-        guess[...] = dot(jnp.concatenate([low, low], axis=1), pred_w[...])
-
-        def loss_step(aq, carry):
-            loss_sum, bias_sum, out_sum = carry
-            start = pl.multiple_of(aq * 64, 64)
-            row = pl.ds(start, 64)
-            weight = (row_mask[row, :].reshape(8, 8, 128) * col_mask[bp * 8 : bp * 8 + 8, :][None]).reshape(64, 128)
-            residue = guess[row, :] - goal[row, lane : lane + 128]
+    bias2 = small[0:1, :]
+    out_w2 = small[1:2, :]
+
+    def act_step(aq, carry):
+        row = pl.ds(pl.multiple_of(aq * 64, 64), 64)
+        for bp in range(8):
+            lane = slice(bp * 128, bp * 128 + 128)
+            value, grade = gelu_parts(pre[row, lane] + bias2, 0.5)
+            hid32[row, lane] = value
+            hid16[row, lane] = value.astype(BF16)
+            weighted[row, lane] = grade * out_w2
+        return carry
+
+    lax.fori_loop(0, 8, act_step, 0)
+
+    for bp in range(8):
+        lane = slice(bp * 128, bp * 128 + 128)
+        low = hid16[:, lane]
+        guess[:, lane] = dot(jnp.concatenate([low, low], axis=1), pred_w[...])
+
+    def loss_step(aq, carry):
+        loss_sum, bias_sum, out_sum = carry
+        start = pl.multiple_of(aq * 64, 64)
+        row = pl.ds(start, 64)
+        row_weight = row_mask[row, :].reshape(8, 8, 128)
+        for bp in range(8):
+            lane = slice(bp * 128, bp * 128 + 128)
+            weight = (row_weight * col_mask[bp * 8 : bp * 8 + 8, :][None]).reshape(64, 128)
+            residue = guess[row, lane] - goal[row, lane]
             grad_pred = weight * residue
-            grad_pre = grad_pred * weighted[row, :]
-            grads[pl.ds(pl.multiple_of(start + 128, 64), 64), lane + 128 : lane + 256] = grad_pre.astype(BF16)
+            grad_pre = grad_pred * weighted[row, lane]
+            grads[pl.ds(pl.multiple_of(start + 128, 64), 64), bp * 128 + 128 : bp * 128 + 256] = grad_pre.astype(BF16)
             loss_sum = loss_sum + jnp.sum((grad_pred * residue).reshape(8, 8, 128), axis=0)
             bias_sum = bias_sum + jnp.sum(grad_pre.reshape(8, 8, 128), axis=0)
-            out_sum = out_sum + jnp.sum((grad_pred * hid32[row, :]).reshape(8, 8, 128), axis=0)
-            return loss_sum, bias_sum, out_sum
-
-        totals = lax.fori_loop(0, 8, loss_step, totals)
+            out_sum = out_sum + jnp.sum((grad_pred * hid32[row, lane]).reshape(8, 8, 128), axis=0)
+        return loss_sum, bias_sum, out_sum
+
+    zero8 = jnp.zeros((8, 128), F32)
+    totals = lax.fori_loop(0, 8, loss_step, (zero8, zero8, zero8))
 
     for bp in range(8):
         lane = bp * 128
@@ -303,7 +311,7 @@
 def tile_call(*operands):
     shapes = [
         ((80, 128), F32), ((72, 128), F32), ((640, 1152), BF16), ((640, 1152), F32), ((768, 1280), BF16),
-        ((512, 128), F32), ((512, 128), BF16), ((512, 128), F32), ((512, 128), F32), ((512, 128), F32),
+        ((512, 1024), F32), ((512, 1024), BF16), ((512, 1024), F32), ((512, 1024), F32), ((512, 1024), F32),
         ((640, 128), F32), ((72, 128), F32), ((128, 768), F32),
     ]
     return pl.pallas_call(

time: 75 us -> 70.1 us (0.935)
  Pallas kernels: 19.7 us -> 14.7 us
    pallas_call x1, Pallas kernels: 15 us -> 10 us  [tile_call(): pl.pallas_call(tile_kernel, out_shape=jax.ShapeDtypeStruct((PEERS, 128, 1...]
where the time goes in v3:
time: 70.1 us; the launch traced here: 69.5 us
  blocking collectives  22.7 us (32%)
  Pallas kernels  14.7 us (21%)
  waiting for transfers between devices  12 us (17%)
  starting transfers between devices  11.2 us (16%)
  local copies, waits for them, and re-layouts  7.43 us (11%)
  matrix products  0.83 us (1%)
    all_to_all x1, blocking collectives, body(): parts = lax.all_to_all(tile_call(spread, *ready), GROUP, 0, 0, tiled=True)  22.7 us
    pallas_call x1, Pallas kernels, tile_call(): pl.pallas_call(tile_kernel, out_shape=jax.ShapeDtypeStruct((PEERS, 128, 1...  10 us
    all_to_all x1, waiting for transfers between devices, body(): every = lax.all_to_all(sums, GROUP, 0, 0, tiled=True)  8.74 us
    all_to_all x1, starting transfers between devices, body(): spread = lax.all_to_all(front_call(feats, w_proj), 'band', 0, 0, tiled=True)  6.83 us
    unnamed x18, local copies, waits for them, and re-layouts  6.33 us
    all_to_all x1, starting transfers between devices, body(): every = lax.all_to_all(sums, GROUP, 0, 0, tiled=True)  4.36 us
    all_to_all x1, waiting for transfers between devices, body(): spread = lax.all_to_all(front_call(feats, w_proj), 'band', 0, 0, tiled=True)  3.29 us
    pallas_call x1, Pallas kernels, final_call(): pl.pallas_call(final_kernel, out_shape=(jax.ShapeDtypeStruct((1024, 128),...  1.88 us
  transfers between devices with their start and end apart: 2, of which 2 were waited for; matrix products, arithmetic and copies ran while one was open for 2% of the time, Pallas kernels for 1%

profile of v3, /device:TPU:1, one launch (start us, length us, event | category | flops | bytes accessed | tf_op | source)
XLA Modules:
  0.0 69.5 jit_solution(8116812808259816397)
XLA Ops:
  0.6 0.0 copy-start
  0.6 0.9 %copy-done = bf16[1024,128]{1,0:T(8,128)(2,1)S(1)} copy-done((bf16[1024,128]{1,0:T(8,128)(2,1)S(1)}, bf16[1024,128]{1,0:T(8,128)(2,1)}, u32[]{:S(2)}) %copy-start) | copy-done | bytes 262168
  1.6 0.0 copy-start.2
  1.6 0.9 %copy-done.2 = bf16[64,1024]{1,0:T(8,128)(2,1)S(1)} copy-done((bf16[64,1024]{1,0:T(8,128)(2,1)S(1)}, bf16[64,1024]{1,0:T(8,128)(2,1)}, u32[]{:S(2)}) %copy-start.2) | copy-done | bytes 131096
  2.5 0.9 %front.1 = bf16[16,80,128]{2,1,0:T(8,128)(2,1)} custom-call(bf16[64,1024]{1,0:T(8,128)(2,1)S(1)} %copy-done.2, bf16[1024,128]{1,0:T(8,128)(2,1)S(1)} %copy-done), custom_call_target="tpu_custom_call" | custom-call | tf_op jit(solution)/shard_map/front/pallas_call | solution.py:56
  3.4 6.8 %all-to-all-start = ((bf16[16,80,128]{2,1,0:T(8,128)(2,1)}), bf16[16,80,128]{2,1,0:T(8,128)(2,1)S(1)}, u32[]{:S(2)}, u32[]{:S(2)}) async-start(bf16[16,80,128]{2,1,0:T(8,128)(2,1)} %front.1), calls=%async_computation | async-start | bytes 655360 | tf_op jit(solution)/shard_map/all_to_all | solution.py:395
  10.2 0.0 copy-start.3
  10.2 0.9 %copy-done.3 = bf16[576,64]{0,1:T(8,128)(2,1)S(1)} copy-done((bf16[576,64]{0,1:T(8,128)(2,1)S(1)}, bf16[576,64]{0,1:T(8,128)(2,1)}, u32[]{:S(2)}) %copy-start.3) | copy-done | bytes 73752
  11.1 0.0 copy-start.4
  11.1 0.8 %copy-done.4 = f32[64,2,64]{2,1,0:T(2,128)S(1)} copy-done((f32[64,2,64]{2,1,0:T(2,128)S(1)}, f32[64,2,64]{2,1,0:T(2,128)}, u32[]{:S(2)}) %copy-start.4) | copy-done | bytes 32792
  12.0 0.0 copy-start.5
  12.0 0.7 copy-done.5
  12.6 0.0 copy-start.6
  12.7 0.7 copy-done.6
  13.3 0.0 copy-start.7
  13.3 0.7 copy-done.7
  14.0 0.6 prepare.1
  14.6 3.3 %all-to-all-done.proj.cols = bf16[16,80,128]{2,1,0:T(8,128)(2,1)S(1)} async-done(((bf16[16,80,128]{2,1,0:T(8,128)(2,1)}), bf16[16,80,128]{2,1,0:T(8,128)(2,1)S(1)}, u32[]{:S(2)}, u32[]{:S(2)}) %all-to-all-start) | async-done | bytes 327712 | tf_op jit(solution)/shard_map/all_to_all | solution.py:395
  17.9 10.0 %tiles.1 = bf16[32,128,128]{2,1,0:T(8,128)(2,1)S(1)} custom-call(bf16[16,80,128]{2,1,0:T(8,128)(2,1)S(1)} %all-to-all-done.proj.cols, bf16[768,128]{1,0:T(8,128)(2,1)S(1)} %get-tuple-element.18.fwd_w, bf16[768,128]{1,0:T(8,128)(2,1)S(1)} %get-tuple-element.19.bwd_w, bf16[256,128]{1,0:T(8,128)(2,1)S(1)} %get-tuple-element.20.pred_w, ...), custom_call_target="tpu_custom_call" | custom-call | flops 2000000000 | bytes 1000000 | tf_op jit(solution)/shard_map/tiles/pallas_call | solution.py:317
  27.9 0.0 copy-start.1
  27.9 22.7 %all_to_all.15.parts = bf16[32,128,128]{2,1,0:T(8,128)(2,1)S(1)} all-to-all(bf16[32,128,128]{2,1,0:T(8,128)(2,1)S(1)} %tiles.1), channel_id=1, replica_groups=mesh['band'=16,'off'=2,'rep'=4] {'band','off'}, dimensions={0} | all-to-all | bytes 2097152 | tf_op jit(solution)/shard_map/all_to_all | solution.py:399
  50.6 1.3 %sums.1 = (bf16[32,48,128]{2,1,0:T(8,128)(2,1)}, bf16[32,128]{1,0:T(8,128)(2,1)S(1)}, f32[2,128]{1,0:T(2,128)S(1)}) custom-call(bf16[32,128,128]{2,1,0:T(8,128)(2,1)S(1)} %all_to_all.15.parts, bf16[16,80,128]{2,1,0:T(8,128)(2,1)S(1)} %all-to-all-done.proj.cols), custom_call_target="tpu_custom_call" | custom-call | tf_op jit(solution)/shard_map/sums/pallas_call | solution.py:358
  51.8 0.5 slice.9
  52.3 4.4 %all-to-all-start.2 = ((bf16[32,48,128]{2,1,0:T(8,128)(2,1)}), bf16[32,48,128]{2,1,0:T(8,128)(2,1)S(1)}, u32[]{:S(2)}, u32[]{:S(2)}) async-start(bf16[32,48,128]{2,1,0:T(8,128)(2,1)} %get-tuple-element.26), calls=%async_computation.2 | async-start | bytes 786432 | tf_op jit(solution)/shard_map/all_to_all | solution.py:401
  56.7 0.6 slice_bitcast_fusion
  57.3 0.0 copy-done.1
  57.3 0.8 %convolution_convert_fusion = bf16[32,1024]{1,0:T(8,128)(2,1)} fusion(bf16[32,128]{1,0:T(8,128)(2,1)S(1)} %get-tuple-element.29, bf16[1024,128]{1,0:T(8,128)(2,1)S(1)} %copy-done.1), kind=kOutput, calls=%fused_computation | convolution fusion | flops 8421376 | bytes 335872 | tf_op jit(solution)/shard_map/dot_general | solution.py:402
  58.1 8.7 %all-to-all-done.2.every = bf16[32,48,128]{2,1,0:T(8,128)(2,1)S(1)} async-done(((bf16[32,48,128]{2,1,0:T(8,128)(2,1)}), bf16[32,48,128]{2,1,0:T(8,128)(2,1)S(1)}, u32[]{:S(2)}, u32[]{:S(2)}) %all-to-all-start.2) | async-done | bytes 393248 | tf_op jit(solution)/shard_map/all_to_all | solution.py:401
  66.9 0.0 copy-start.8
  66.9 0.8 %copy-done.8 = bf16[32,48,128]{2,1,0:T(8,128)(2,1)} copy-done((bf16[32,48,128]{2,1,0:T(8,128)(2,1)}, bf16[32,48,128]{2,1,0:T(8,128)(2,1)S(1)}, u32[]{:S(2)}) %copy-start.8) | copy-done | bytes 393240
  67.6 1.9 %outputs.1 = (f32[1024,128]{1,0:T(8,128)}, f32[64,576]{1,0:T(8,128)}) custom-call(bf16[32,48,128]{2,1,0:T(8,128)(2,1)} %copy-done.8), custom_call_target="tpu_custom_call" | custom-call | tf_op jit(solution)/shard_map/outputs/pallas_call | solution.py:385
Async XLA Ops:
  0.6 1.0 %copy-start = (bf16[1024,128]{1,0:T(8,128)(2,1)S(1)}, bf16[1024,128]{1,0:T(8,128)(2,1)}, u32[]{:S(2)}) copy-start(bf16[1024,128]{1,0:T(8,128)(2,1)} %w_proj.1) | copy-start | bytes 786436
  1.6 0.9 %copy-start.2 = (bf16[64,1024]{1,0:T(8,128)(2,1)S(1)}, bf16[64,1024]{1,0:T(8,128)(2,1)}, u32[]{:S(2)}) copy-start(bf16[64,1024]{1,0:T(8,128)(2,1)} %feats.1) | copy-start | bytes 393220
  3.4 14.4 %all-to-all-start = ((bf16[16,80,128]{2,1,0:T(8,128)(2,1)}), bf16[16,80,128]{2,1,0:T(8,128)(2,1)S(1)}, u32[]{:S(2)}, u32[]{:S(2)}) async-start(bf16[16,80,128]{2,1,0:T(8,128)(2,1)} %front.1), calls=%async_computation | async-start | bytes 655360 | tf_op jit(solution)/shard_map/all_to_all | solution.py:395
  10.2 0.9 %copy-start.3 = (bf16[576,64]{0,1:T(8,128)(2,1)S(1)}, bf16[576,64]{0,1:T(8,128)(2,1)}, u32[]{:S(2)}) copy-start(bf16[576,64]{0,1:T(8,128)(2,1)} %param.9) | copy-start | bytes 221188
  11.1 0.8 %copy-start.4 = (f32[64,2,64]{2,1,0:T(2,128)S(1)}, f32[64,2,64]{2,1,0:T(2,128)}, u32[]{:S(2)}) copy-start(f32[64,2,64]{2,1,0:T(2,128)} %target.1) | copy-start | bytes 98308
  12.0 0.7 copy-start.5
  12.6 0.7 copy-start.6
  13.3 0.7 copy-start.7
  27.9 29.4 %copy-start.1 = (bf16[1024,128]{1,0:T(8,128)(2,1)S(1)}, bf16[1024,128]{1,0:T(8,128)(2,1)}, u32[]{:S(2)}) copy-start(bf16[1024,128]{1,0:T(8,128)(2,1)} %w_proj.1) | copy-start | bytes 786436
  52.3 14.5 %all-to-all-start.2 = ((bf16[32,48,128]{2,1,0:T(8,128)(2,1)}), bf16[32,48,128]{2,1,0:T(8,128)(2,1)S(1)}, u32[]{:S(2)}, u32[]{:S(2)}) async-start(bf16[32,48,128]{2,1,0:T(8,128)(2,1)} %get-tuple-element.26), calls=%async_computation.2 | async-start | bytes 786432 | tf_op jit(solution)/shard_map/all_to_all | solution.py:401
  66.9 0.8 %copy-start.8 = (bf16[32,48,128]{2,1,0:T(8,128)(2,1)}, bf16[32,48,128]{2,1,0:T(8,128)(2,1)S(1)}, u32[]{:S(2)}) copy-start(bf16[32,48,128]{2,1,0:T(8,128)(2,1)S(1)} %all-to-all-done.2.every) | copy-start | bytes 1179652

commit v4 on v3

--- a/solution.py
+++ b/solution.py
@@ -36,10 +36,13 @@
     return jnp.dot(a, b, preferred_element_type=F32)
 
 
-def front_kernel(feats, w_proj, out):
+def front_kernel(feats_hbm, w_proj_hbm, out, feats, w_proj, sems):
     off = lax.axis_index("off")
-    proj = dot(feats[...], w_proj[...]).astype(BF16)
-    out[:, 0:64, :] = jnp.broadcast_to(proj[None], (BANDS, 64, 128))
+    get_feats = pltpu.make_async_copy(feats_hbm, feats, sems.at[0])
+    get_w = pltpu.make_async_copy(w_proj_hbm, w_proj, sems.at[1])
+    get_feats.start()
+    get_w.start()
+    get_feats.wait()
     group = lane_ids((16, 128)) // 32
     for q in range(8):
         block = feats[:, q * 128 : q * 128 + 128].astype(F32)
@@ -50,15 +53,23 @@
                 turned = pltpu.roll(block[g * 16 : g * 16 + 16], lax.rem(g - piece + 4, 4) * 32, 1)
                 packed = jnp.where(group == g, turned, packed)
             out[2 * q + half, 64:80, :] = packed.astype(BF16)
+    get_w.wait()
+    proj = dot(feats[...], w_proj[...]).astype(BF16)
+    out[:, 0:64, :] = jnp.broadcast_to(proj[None], (BANDS, 64, 128))
 
 
 def front_call(feats, w_proj):
     return pl.pallas_call(
         front_kernel,
         out_shape=jax.ShapeDtypeStruct((BANDS, 80, 128), BF16),
-        in_specs=[pl.BlockSpec(memory_space=pltpu.VMEM)] * 2,
+        in_specs=[pl.BlockSpec(memory_space=pltpu.HBM)] * 2,
         out_specs=pl.BlockSpec(memory_space=pltpu.VMEM),
-        compiler_params=pltpu.CompilerParams(vmem_limit_bytes=16 * 2**20),
+        scratch_shapes=[
+            pltpu.VMEM((64, 1024), BF16),
+            pltpu.VMEM((1024, 128), BF16),
+            pltpu.SemaphoreType.DMA((2,)),
+        ],
+        compiler_params=pltpu.CompilerParams(vmem_limit_bytes=60 * 2**20),
         name="front",
     )(feats, w_proj)
 
@@ -185,24 +196,27 @@
     v_high = v[:, 1].reshape(72, 128)
     cols_v[...] = jnp.where(half_lane, pltpu.roll(v_low, 64, 1), v_high)
 
-    def pair_step(aq, carry):
-        row = pl.multiple_of(aq * 64, 64)
-        here = rows_u[pl.ds(pl.multiple_of(aq * 8, 8), 8), :]
-        row_at = band * 8 + aq - 1
-        row_in = (row_at >= 0) & (row_at < 128)
-        for bp in range(9):
-            block = first * 8 - 1 + 2 * bp
-            spot = jnp.where(half_lane, block, block + 1)
-            half = jnp.where((spot >= 0) & (spot < 128) & row_in, 0.5, 0.0)
-            x = (here[:, None, :] + cols_v[bp * 8 : bp * 8 + 8, :][None, :, :]).reshape(64, 128)
+    bias2 = small[0:1, :]
+    out_w2 = small[1:2, :]
+
+    def pair_stage(bp):
+        lane = slice(bp * 128, bp * 128 + 128)
+        block = first * 8 - 1 + 2 * bp
+        spot = jnp.where(half_lane, block, block + 1)
+        col_in = jnp.where((spot >= 0) & (spot < 128), 0.5, 0.0)
+        v_here = cols_v[bp * 8 : bp * 8 + 8, :][None]
+        for aq in range(10):
+            half = col_in
+            if aq == 0:
+                half = jnp.where(band == 0, 0.0, col_in)
+            if aq == 9:
+                half = jnp.where(band == BANDS - 1, 0.0, col_in)
+            x = (rows_u[aq * 8 : aq * 8 + 8, :][:, None, :] + v_here).reshape(64, 128)
             value, grade = gelu_parts(x, half)
-            pair[pl.ds(row, 64), bp * 128 : bp * 128 + 128] = value.astype(BF16)
-            slope[pl.ds(row, 64), bp * 128 : bp * 128 + 128] = grade
-        return carry
-
-    lax.fori_loop(0, 10, pair_step, 0)
-
-    for bp in range(8):
+            pair[aq * 64 : aq * 64 + 64, lane] = value.astype(BF16)
+            slope[aq * 64 : aq * 64 + 64, lane] = grade
+
+    def conv_stage(bp):
         lane = bp * 128
         pre[:, lane : lane + 128] = (
             dot(pair[0:512, lane : lane + 256], fwd_w[0:256, :])
@@ -210,47 +224,37 @@
             + dot(pair[128:640, lane : lane + 256], fwd_w[512:768, :])
         )
 
-    bias2 = small[0:1, :]
-    out_w2 = small[1:2, :]
-
-    def act_step(aq, carry):
-        row = pl.ds(pl.multiple_of(aq * 64, 64), 64)
-        for bp in range(8):
-            lane = slice(bp * 128, bp * 128 + 128)
+    def act_stage(bp):
+        lane = slice(bp * 128, bp * 128 + 128)
+        for aq in range(8):
+            row = slice(aq * 64, aq * 64 + 64)
             value, grade = gelu_parts(pre[row, lane] + bias2, 0.5)
             hid32[row, lane] = value
             hid16[row, lane] = value.astype(BF16)
             weighted[row, lane] = grade * out_w2
-        return carry
-
-    lax.fori_loop(0, 8, act_step, 0)
-
-    for bp in range(8):
+
+    def pred_stage(bp):
         lane = slice(bp * 128, bp * 128 + 128)
         low = hid16[:, lane]
         guess[:, lane] = dot(jnp.concatenate([low, low], axis=1), pred_w[...])
 
-    def loss_step(aq, carry):
-        loss_sum, bias_sum, out_sum = carry
-        start = pl.multiple_of(aq * 64, 64)
-        row = pl.ds(start, 64)
-        row_weight = row_mask[row, :].reshape(8, 8, 128)
-        for bp in range(8):
-            lane = slice(bp * 128, bp * 128 + 128)
-            weight = (row_weight * col_mask[bp * 8 : bp * 8 + 8, :][None]).reshape(64, 128)
+    def loss_stage(bp, sums):
+        loss_sum, bias_sum, out_sum = sums
+        lane = slice(bp * 128, bp * 128 + 128)
+        col_weight = col_mask[bp * 8 : bp * 8 + 8, :][None]
+        for aq in range(8):
+            row = slice(aq * 64, aq * 64 + 64)
+            weight = (row_mask[row, :].reshape(8, 8, 128) * col_weight).reshape(64, 128)
             residue = guess[row, lane] - goal[row, lane]
             grad_pred = weight * residue
             grad_pre = grad_pred * weighted[row, lane]
-            grads[pl.ds(pl.multiple_of(start + 128, 64), 64), bp * 128 + 128 : bp * 128 + 256] = grad_pre.astype(BF16)
+            grads[128 + aq * 64 : 192 + aq * 64, bp * 128 + 128 : bp * 128 + 256] = grad_pre.astype(BF16)
             loss_sum = loss_sum + jnp.sum((grad_pred * residue).reshape(8, 8, 128), axis=0)
             bias_sum = bias_sum + jnp.sum(grad_pre.reshape(8, 8, 128), axis=0)
             out_sum = out_sum + jnp.sum((grad_pred * hid32[row, lane]).reshape(8, 8, 128), axis=0)
         return loss_sum, bias_sum, out_sum
 
-    zero8 = jnp.zeros((8, 128), F32)
-    totals = lax.fori_loop(0, 8, loss_step, (zero8, zero8, zero8))
-
-    for bp in range(8):
+    def weights_stage(bp):
         lane = bp * 128
         turned = grads[128:640, lane + 128 : lane + 256].T
         for ty in range(3):
@@ -260,7 +264,7 @@
             else:
                 grad_w[:, ty * 256 : ty * 256 + 256] += part
 
-    for bp in range(9):
+    def back_stage(bp):
         lane = bp * 128
         part = (
             dot(grads[128:768, lane : lane + 256], bwd_w[0:256, :])
@@ -272,6 +276,24 @@
         else:
             grad_rows[...] += part
         grad_cols[bp * 8 : bp * 8 + 8, :] = jnp.sum(part.reshape(80, 8, 128), axis=0)
+
+    zero8 = jnp.zeros((8, 128), F32)
+    totals = (zero8, zero8, zero8)
+    for step in range(15):
+        if 6 <= step:
+            back_stage(step - 6)
+        if 6 <= step < 14:
+            weights_stage(step - 6)
+        if 5 <= step < 13:
+            totals = loss_stage(step - 5, totals)
+        if 4 <= step < 12:
+            pred_stage(step - 4)
+        if 3 <= step < 11:
+            act_stage(step - 3)
+        if 2 <= step < 10:
+            conv_stage(step - 2)
+        if step < 9:
+            pair_stage(step)
 
     row_part = jnp.sum(grad_rows[...].reshape(80, 8, 128), axis=1)
     row_part = row_part + pltpu.roll(row_part, 64, 1)
@@ -326,7 +348,7 @@
     )(*operands)
 
 
-def sum_kernel(parts, cols, out, mine, small, bins):
+def sum_kernel(parts, cols, out, mine, bias, w_out, loss, bins):
     me = 2 * lax.axis_index("band") + lax.axis_index("off")
     half_lane = lane_ids((1, 128)) < 64
     bins[...] = jnp.zeros(bins.shape, F32)
@@ -350,8 +372,10 @@
     total = jnp.sum(parts[:, 112:128, :].astype(F32), axis=0)
     out[:, 0:32, :] = jnp.broadcast_to(rows.astype(BF16)[None], (PEERS, 32, 128))
     out[:, 32:48, :] = jnp.broadcast_to(total.astype(BF16)[None], (PEERS, 16, 128))
-    small[0:1, :] = total[9:10] + total[10:11]
-    small[1:2, :] = total[11:12] + total[12:13]
+    small = total[9:10] + total[10:11]
+    bias[...] = small[:, 0:64]
+    w_out[...] = small[:, 64:128]
+    loss[...] = (total[11:12] + total[12:13])[:, 0:1]
 
 
 def sum_call(parts, cols):
@@ -360,18 +384,27 @@
         out_shape=(
             jax.ShapeDtypeStruct((PEERS, 48, 128), BF16),
             jax.ShapeDtypeStruct((32, 128), BF16),
-            jax.ShapeDtypeStruct((2, 128), F32),
+            jax.ShapeDtypeStruct((1, 64), F32),
+            jax.ShapeDtypeStruct((1, 64), F32),
+            jax.ShapeDtypeStruct((1, 1), F32),
         ),
         in_specs=[pl.BlockSpec(memory_space=pltpu.VMEM)] * 2,
-        out_specs=(pl.BlockSpec(memory_space=pltpu.VMEM),) * 3,
+        out_specs=(pl.BlockSpec(memory_space=pltpu.VMEM),) * 5,
         scratch_shapes=[pltpu.VMEM((1408, 128), F32)],
         compiler_params=pltpu.CompilerParams(vmem_limit_bytes=16 * 2**20),
         name="sums",
     )(parts, cols)
 
 
-def final_kernel(every, grad_proj, grad_conv_t):
-    grad_proj[...] = every[:, 0:32, :].astype(F32).reshape(1024, 128)
+def final_kernel(every, grad_proj_hbm, grad_conv_hbm, grad_proj, grad_conv_t, sems):
+    puts = []
+    for k in range(4):
+        rows = pl.ds(k * 256, 256)
+        grad_proj[k * 256 : k * 256 + 256, :] = (
+            every[k * 8 : k * 8 + 8, 0:32, :].astype(F32).reshape(256, 128)
+        )
+        puts.append(pltpu.make_async_copy(grad_proj.at[rows], grad_proj_hbm.at[rows], sems.at[k]))
+        puts[k].start()
     conv = every[:, 32:48, :].astype(F32)
     wide = conv[:, 0:8].reshape(256, 128)
     for k in range(4):
@@ -379,6 +412,10 @@
     last = conv[:, 8]
     grad_conv_t[0:32, 512:576] = last[:, 0:64]
     grad_conv_t[32:64, 512:576] = last[:, 64:128]
+    puts.append(pltpu.make_async_copy(grad_conv_t, grad_conv_hbm, sems.at[4]))
+    puts[4].start()
+    for put in puts:
+        put.wait()
 
 
 def final_call(every):
@@ -386,7 +423,13 @@
         final_kernel,
         out_shape=(jax.ShapeDtypeStruct((1024, 128), F32), jax.ShapeDtypeStruct((64, 576), F32)),
         in_specs=[pl.BlockSpec(memory_space=pltpu.VMEM)],
-        out_specs=(pl.BlockSpec(memory_space=pltpu.VMEM),) * 2,
+        out_specs=(pl.BlockSpec(memory_space=pltpu.HBM),) * 2,
+        scratch_shapes=[
+            pltpu.VMEM((1024, 128), F32),
+            pltpu.VMEM((64, 576), F32),
+            pltpu.SemaphoreType.DMA((5,)),
+        ],
+        compiler_params=pltpu.CompilerParams(vmem_limit_bytes=8 * 2**20),
         name="outputs",
     )(every)
 
@@ -397,13 +440,13 @@
         mask.reshape(8, 128), target, conv_w.T, conv_b.reshape(1, 64), w_out.reshape(1, 64)
     )
     parts = lax.all_to_all(tile_call(spread, *ready), GROUP, 0, 0, tiled=True)
-    sums, mine, small = sum_call(parts, spread)
+    sums, mine, bias, w_out, loss = sum_call(parts, spread)
     every = lax.all_to_all(sums, GROUP, 0, 0, tiled=True)
     grad_feats = lax.dot_general(
         mine, w_proj, (((1,), (1,)), ((), ())), preferred_element_type=F32
     ).astype(BF16)
     grad_proj, grad_conv_t = final_call(every)
-    return (small[1, 0:1], grad_proj, grad_conv_t.T, small[0, 0:64], small[0, 64:128], grad_feats)
+    return (loss.reshape(1), grad_proj, grad_conv_t.T, bias.reshape(64), w_out.reshape(64), grad_feats)
 
 
 def solution(mesh):

time: 70.1 us -> 64.2 us (0.916)
  local copies, waits for them, and re-layouts: 7.43 us -> 3.72 us
  Pallas kernels: 14.7 us -> 12 us
    pallas_call x1, Pallas kernels: 10 us -> 7.3 us  [tile_call(): pl.pallas_call(tile_kernel, out_shape=jax.ShapeDtypeStruct((PEERS, 128, 1...]
    unnamed x18 -> x12, local copies, waits for them, and re-layouts: 6.33 us -> 3.72 us
    pallas_call x1, Pallas kernels: 0.91 us -> 1.97 us  [front_call(): pl.pallas_call(front_kernel, out_shape=jax.ShapeDtypeStruct((BANDS, 80, 1...]
    pallas_call x1, Pallas kernels: 1.88 us -> 0.91 us  [final_call(): pl.pallas_call(final_kernel, out_shape=(jax.ShapeDtypeStruct((1024, 128),...]
  transfers between devices with their start and end apart: 2 -> 2, of which waited for: 2 -> 2; matrix products, arithmetic and copies ran while one was open for 2% -> 1% of each run, Pallas kernels for 1% -> 1%
where the time goes in v4:
time: 64.2 us; the launch traced here: 63.7 us
  blocking collectives  22.7 us (35%)
  waiting for transfers between devices  12.6 us (20%)
  Pallas kernels  12 us (19%)
  starting transfers between devices  11.2 us (17%)
  local copies, waits for them, and re-layouts  3.72 us (6%)
  matrix products  0.83 us (1%)
  between operations  0.69 us (1%)
    all_to_all x1, blocking collectives, body(): parts = lax.all_to_all(tile_call(spread, *ready), GROUP, 0, 0, tiled=True)  22.7 us
    all_to_all x1, waiting for transfers between devices, body(): every = lax.all_to_all(sums, GROUP, 0, 0, tiled=True)  9.31 us
    pallas_call x1, Pallas kernels, tile_call(): pl.pallas_call(tile_kernel, out_shape=jax.ShapeDtypeStruct((PEERS, 128, 1...  7.3 us
    all_to_all x1, starting transfers between devices, body(): spread = lax.all_to_all(front_call(feats, w_proj), 'band', 0, 0, tiled=True)  6.84 us
    all_to_all x1, starting transfers between devices, body(): every = lax.all_to_all(sums, GROUP, 0, 0, tiled=True)  4.36 us
    unnamed x12, local copies, waits for them, and re-layouts  3.72 us
    all_to_all x1, waiting for transfers between devices, body(): spread = lax.all_to_all(front_call(feats, w_proj), 'band', 0, 0, tiled=True)  3.29 us
    pallas_call x1, Pallas kernels, front_call(): pl.pallas_call(front_kernel, out_shape=jax.ShapeDtypeStruct((BANDS, 80, 1...  1.97 us
  transfers between devices with their start and end apart: 2, of which 2 were waited for; matrix products, arithmetic and copies ran while one was open for 1% of the time, Pallas kernels for 1%

profile of v4, /device:TPU:1, one launch (start us, length us, event | category | flops | bytes accessed | tf_op | source)
XLA Modules:
  0.0 63.7 jit_solution(16666820654617338415)
XLA Ops:
  0.6 2.0 %front.1 = bf16[16,80,128]{2,1,0:T(8,128)(2,1)} custom-call(bf16[64,1024]{1,0:T(8,128)(2,1)} %feats_hbm.1, bf16[1024,128]{1,0:T(8,128)(2,1)} %w_proj_hbm.1), custom_call_target="tpu_custom_call" | custom-call | tf_op jit(solution)/shard_map/front/pallas_call | solution.py:62
  2.6 6.8 %all-to-all-start = ((bf16[16,80,128]{2,1,0:T(8,128)(2,1)}), bf16[16,80,128]{2,1,0:T(8,128)(2,1)S(1)}, u32[]{:S(2)}, u32[]{:S(2)}) async-start(bf16[16,80,128]{2,1,0:T(8,128)(2,1)} %front.1), calls=%async_computation | async-start | bytes 655360 | tf_op jit(solution)/shard_map/all_to_all | solution.py:438
  9.5 0.0 copy-start
  9.5 0.9 %copy-done = bf16[576,64]{0,1:T(8,128)(2,1)S(1)} copy-done((bf16[576,64]{0,1:T(8,128)(2,1)S(1)}, bf16[576,64]{0,1:T(8,128)(2,1)}, u32[]{:S(2)}) %copy-start) | copy-done | bytes 73752
  10.3 0.0 copy-start.1
  10.3 0.8 %copy-done.1 = f32[64,2,64]{2,1,0:T(2,128)S(1)} copy-done((f32[64,2,64]{2,1,0:T(2,128)S(1)}, f32[64,2,64]{2,1,0:T(2,128)}, u32[]{:S(2)}) %copy-start.1) | copy-done | bytes 32792
  11.2 0.0 copy-start.2
  11.2 0.7 %copy-done.2 = s32[1024]{0:T(1024)S(1)} copy-done((s32[1024]{0:T(1024)S(1)}, s32[1024]{0:T(1024)}, u32[]{:S(2)}) %copy-start.2) | copy-done | bytes 4120
  11.9 0.0 copy-start.3
  11.9 0.7 %copy-done.3 = f32[64]{0:T(128)S(1)} copy-done((f32[64]{0:T(128)S(1)}, f32[64]{0:T(128)}, u32[]{:S(2)}) %copy-start.3) | copy-done | bytes 280
  12.5 0.0 copy-start.4
  12.5 0.7 %copy-done.4 = f32[64]{0:T(128)S(1)} copy-done((f32[64]{0:T(128)S(1)}, f32[64]{0:T(128)}, u32[]{:S(2)}) %copy-start.4) | copy-done | bytes 280
  13.2 0.6 prepare.1
  13.8 3.3 %all-to-all-done.proj.cols = bf16[16,80,128]{2,1,0:T(8,128)(2,1)S(1)} async-done(((bf16[16,80,128]{2,1,0:T(8,128)(2,1)}), bf16[16,80,128]{2,1,0:T(8,128)(2,1)S(1)}, u32[]{:S(2)}, u32[]{:S(2)}) %all-to-all-start) | async-done | bytes 327712 | tf_op jit(solution)/shard_map/all_to_all | solution.py:438
  17.1 7.3 %tiles.1 = bf16[32,128,128]{2,1,0:T(8,128)(2,1)S(1)} custom-call(bf16[16,80,128]{2,1,0:T(8,128)(2,1)S(1)} %all-to-all-done.proj.cols, bf16[768,128]{1,0:T(8,128)(2,1)S(1)} %get-tuple-element.20.fwd_w, bf16[768,128]{1,0:T(8,128)(2,1)S(1)} %get-tuple-element.21.bwd_w, bf16[256,128]{1,0:T(8,128)(2,1)S(1)} %get-tuple-element.22.pred_w, ...), custom_call_target="tpu_custom_call" | custom-call | flops 2000000000 | bytes 1000000 | tf_op jit(solution)/shard_map/tiles/pallas_call | solution.py:339
  24.4 0.0 copy-start.5
  24.4 22.7 %all_to_all.15.parts = bf16[32,128,128]{2,1,0:T(8,128)(2,1)S(1)} all-to-all(bf16[32,128,128]{2,1,0:T(8,128)(2,1)S(1)} %tiles.1), channel_id=1, replica_groups=mesh['band'=16,'off'=2,'rep'=4] {'band','off'}, dimensions={0} | all-to-all | bytes 2097152 | tf_op jit(solution)/shard_map/all_to_all | solution.py:442
  47.0 1.3 %sums.1 = (bf16[32,48,128]{2,1,0:T(8,128)(2,1)}, bf16[32,128]{1,0:T(8,128)(2,1)S(1)}, f32[1,64]{1,0:T(1,128)}, f32[1,64]{1,0:T(1,128)}, f32[1,1]{1,0:T(1,128)}) custom-call(bf16[32,128,128]{2,1,0:T(8,128)(2,1)S(1)} %all_to_all.15.parts, bf16[16,80,128]{2,1,0:T(8,128)(2,1)S(1)} %all-to-all-done.proj.cols), custom_call_target="tpu_custom_call" | custom-call | tf_op jit(solution)/shard_map/sums/pallas_call | solution.py:382
  48.3 4.4 %all-to-all-start.2 = ((bf16[32,48,128]{2,1,0:T(8,128)(2,1)}), bf16[32,48,128]{2,1,0:T(8,128)(2,1)S(1)}, u32[]{:S(2)}, u32[]{:S(2)}) async-start(bf16[32,48,128]{2,1,0:T(8,128)(2,1)} %get-tuple-element.28), calls=%async_computation.2 | async-start | bytes 786432 | tf_op jit(solution)/shard_map/all_to_all | solution.py:444
  52.7 0.0 copy-done.5
  52.7 0.8 %convolution_convert_fusion = bf16[32,1024]{1,0:T(8,128)(2,1)} fusion(bf16[32,128]{1,0:T(8,128)(2,1)S(1)} %get-tuple-element.33, bf16[1024,128]{1,0:T(8,128)(2,1)S(1)} %copy-done.5), kind=kOutput, calls=%fused_computation | convolution fusion | flops 8421376 | bytes 335872 | tf_op jit(solution)/shard_map/dot_general | solution.py:445
  53.5 9.3 %all-to-all-done.2.every = bf16[32,48,128]{2,1,0:T(8,128)(2,1)S(1)} async-done(((bf16[32,48,128]{2,1,0:T(8,128)(2,1)}), bf16[32,48,128]{2,1,0:T(8,128)(2,1)S(1)}, u32[]{:S(2)}, u32[]{:S(2)}) %all-to-all-start.2) | async-done | bytes 393248 | tf_op jit(solution)/shard_map/all_to_all | solution.py:444
  62.8 0.9 %outputs.1 = (f32[1024,128]{1,0:T(8,128)}, f32[64,576]{1,0:T(8,128)}) custom-call(bf16[32,48,128]{2,1,0:T(8,128)(2,1)S(1)} %all-to-all-done.2.every), custom_call_target="tpu_custom_call" | custom-call | tf_op jit(solution)/shard_map/outputs/pallas_call | solution.py:422
Async XLA Ops:
  2.6 14.5 %all-to-all-start = ((bf16[16,80,128]{2,1,0:T(8,128)(2,1)}), bf16[16,80,128]{2,1,0:T(8,128)(2,1)S(1)}, u32[]{:S(2)}, u32[]{:S(2)}) async-start(bf16[16,80,128]{2,1,0:T(8,128)(2,1)} %front.1), calls=%async_computation | async-start | bytes 655360 | tf_op jit(solution)/shard_map/all_to_all | solution.py:438
  9.5 0.9 %copy-start = (bf16[576,64]{0,1:T(8,128)(2,1)S(1)}, bf16[576,64]{0,1:T(8,128)(2,1)}, u32[]{:S(2)}) copy-start(bf16[576,64]{0,1:T(8,128)(2,1)} %param.9) | copy-start | bytes 221188
  10.3 0.8 %copy-start.1 = (f32[64,2,64]{2,1,0:T(2,128)S(1)}, f32[64,2,64]{2,1,0:T(2,128)}, u32[]{:S(2)}) copy-start(f32[64,2,64]{2,1,0:T(2,128)} %target.1) | copy-start | bytes 98308
  11.2 0.7 %copy-start.2 = (s32[1024]{0:T(1024)S(1)}, s32[1024]{0:T(1024)}, u32[]{:S(2)}) copy-start(s32[1024]{0:T(1024)} %param.13) | copy-start | bytes 12292
  11.9 0.7 %copy-start.3 = (f32[64]{0:T(128)S(1)}, f32[64]{0:T(128)}, u32[]{:S(2)}) copy-start(f32[64]{0:T(128)} %param.10) | copy-start | bytes 772
  12.5 0.7 %copy-start.4 = (f32[64]{0:T(128)S(1)}, f32[64]{0:T(128)}, u32[]{:S(2)}) copy-start(f32[64]{0:T(128)} %param.11) | copy-start | bytes 772
  24.4 28.3 %copy-start.5 = (bf16[1024,128]{1,0:T(8,128)(2,1)S(1)}, bf16[1024,128]{1,0:T(8,128)(2,1)}, u32[]{:S(2)}) copy-start(bf16[1024,128]{1,0:T(8,128)(2,1)} %w_proj_hbm.1) | copy-start | bytes 786436
  48.3 14.5 %all-to-all-start.2 = ((bf16[32,48,128]{2,1,0:T(8,128)(2,1)}), bf16[32,48,128]{2,1,0:T(8,128)(2,1)S(1)}, u32[]{:S(2)}, u32[]{:S(2)}) async-start(bf16[32,48,128]{2,1,0:T(8,128)(2,1)} %get-tuple-element.28), calls=%async_computation.2 | async-start | bytes 786432 | tf_op jit(solution)/shard_map/all_to_all | solution.py:444

commit v5 on v4

--- a/solution.py
+++ b/solution.py
@@ -9,6 +9,7 @@
 GELU_C = 0.044715
 GROUP = ("band", "off")
 PEERS = 32
+CHIPS = 16
 BANDS = 16
 F32 = jnp.float32
 BF16 = jnp.bfloat16
@@ -43,16 +44,15 @@
     get_feats.start()
     get_w.start()
     get_feats.wait()
-    group = lane_ids((16, 128)) // 32
+    half_lane = lane_ids((1, 128)) < 64
     for q in range(8):
         block = feats[:, q * 128 : q * 128 + 128].astype(F32)
-        for half in range(2):
-            piece = 2 * half + off
-            packed = jnp.zeros((16, 128), F32)
-            for g in range(4):
-                turned = pltpu.roll(block[g * 16 : g * 16 + 16], lax.rem(g - piece + 4, 4) * 32, 1)
-                packed = jnp.where(group == g, turned, packed)
-            out[2 * q + half, 64:80, :] = packed.astype(BF16)
+        top, bottom = block[0:32], block[32:64]
+        low = jnp.where(half_lane, top, pltpu.roll(bottom, 64, 1))
+        high = jnp.where(half_lane, pltpu.roll(top, 64, 1), bottom)
+        packed = jnp.where(off == 0, low, high).astype(BF16)
+        out[2 * q, 64:96, :] = packed
+        out[2 * q + 1, 64:96, :] = packed
     get_w.wait()
     proj = dot(feats[...], w_proj[...]).astype(BF16)
     out[:, 0:64, :] = jnp.broadcast_to(proj[None], (BANDS, 64, 128))
@@ -61,7 +61,7 @@
 def front_call(feats, w_proj):
     return pl.pallas_call(
         front_kernel,
-        out_shape=jax.ShapeDtypeStruct((BANDS, 80, 128), BF16),
+        out_shape=jax.ShapeDtypeStruct((BANDS, 96, 128), BF16),
         in_specs=[pl.BlockSpec(memory_space=pltpu.HBM)] * 2,
         out_specs=pl.BlockSpec(memory_space=pltpu.VMEM),
         scratch_shapes=[
@@ -165,8 +165,9 @@
 
 def tile_kernel(
     proj, fwd_w, bwd_w, pred_w, goal, row_mask, col_mask, small,
-    out,
+    keep, send,
     rows_u, cols_v, pair, slope, grads, pre, hid16, hid32, weighted, guess, grad_rows, grad_cols, grad_w,
+    place_u, place_v,
 ):
     band = lax.axis_index("band")
     first = band + 2 * lax.axis_index("off")
@@ -296,13 +297,17 @@
             pair_stage(step)
 
     row_part = jnp.sum(grad_rows[...].reshape(80, 8, 128), axis=1)
-    row_part = row_part + pltpu.roll(row_part, 64, 1)
+    core = band % 2
+    place_u[...] = jnp.zeros(place_u.shape, F32)
+    place_v[...] = jnp.zeros(place_v.shape, F32)
+    place_u[pl.ds(pl.multiple_of(core * 64, 64), 80), :] = row_part + pltpu.roll(row_part, 64, 1)
     col_part = grad_cols[...]
-    col_low = pltpu.roll(col_part, 64, 1).reshape(9, 1, 8, 128)
-    col_part = jnp.concatenate([col_low, col_part.reshape(9, 1, 8, 128)], axis=1).reshape(144, 128)
-    spare = pltpu.roll(col_part[112:144], 64, 1)
-    packed = jnp.where(half_lane, jnp.concatenate([row_part, spare], axis=0), col_part[0:112])
-    out[:, 0:112, :] = jnp.broadcast_to(packed.astype(BF16)[None], (PEERS, 112, 128))
+    col_high = pltpu.roll(col_part, 64, 1).reshape(9, 1, 8, 128)
+    place_v[pl.ds(pl.multiple_of(core * 64, 64), 144), :] = jnp.concatenate(
+        [col_part.reshape(9, 1, 8, 128), col_high], axis=1
+    ).reshape(144, 128)
+    packed_u = jnp.where(half_lane, place_u[0:72, :], pltpu.roll(place_u[72:144, :], 64, 1))
+    packed_v = jnp.where(half_lane, place_v[0:104, :], pltpu.roll(place_v[104:208, :], 64, 1))
 
     taps = []
     for ty in range(3):
@@ -310,7 +315,7 @@
             grad_w[0:64, ty * 256 : ty * 256 + 192] + grad_w[64:128, ty * 256 + 64 : ty * 256 + 256]
         )
     conv_grad = jnp.concatenate(taps, axis=1)
-    wide = jnp.concatenate([conv_grad[:, k * 128 : k * 128 + 128] for k in range(4)], axis=0)
+    blocks = [conv_grad[:, k * 128 : k * 128 + 128] for k in range(4)]
     last = jnp.concatenate([conv_grad[0:32, 512:576], conv_grad[32:64, 512:576]], axis=1)
 
     loss_sum, bias_sum, out_sum = totals
@@ -323,24 +328,25 @@
     small_hi = small_row.astype(BF16).astype(F32)
     loss_hi = loss_row.astype(BF16).astype(F32)
     tail = jnp.concatenate(
-        [small_hi, small_row - small_hi, loss_hi, loss_row - loss_hi, jnp.zeros((3, 128), F32)], axis=0
-    )
-    tail = jnp.broadcast_to(tail[None], (PEERS, 7, 128))
-    rest = jnp.concatenate([last.reshape(PEERS, 1, 128), tail], axis=1)
-    out[:, 112:128, :] = jnp.concatenate([wide.reshape(PEERS, 8, 128), rest], axis=1).astype(BF16)
+        [small_hi, small_row - small_hi, loss_hi, loss_row - loss_hi, jnp.zeros((4, 128), F32)], axis=0
+    )
+    first_core = jnp.concatenate([packed_u, last, blocks[2], blocks[3], tail], axis=0)
+    second_core = jnp.concatenate([packed_v, blocks[0], blocks[1], tail], axis=0)
+    keep[...] = jnp.where(core == 0, first_core, second_core)
+    send[...] = jnp.where(core == 0, second_core, first_core).astype(BF16)
 
 
 def tile_call(*operands):
     shapes = [
         ((80, 128), F32), ((72, 128), F32), ((640, 1152), BF16), ((640, 1152), F32), ((768, 1280), BF16),
         ((512, 1024), F32), ((512, 1024), BF16), ((512, 1024), F32), ((512, 1024), F32), ((512, 1024), F32),
-        ((640, 128), F32), ((72, 128), F32), ((128, 768), F32),
+        ((640, 128), F32), ((72, 128), F32), ((128, 768), F32), ((208, 128), F32), ((208, 128), F32),
     ]
     return pl.pallas_call(
         tile_kernel,
-        out_shape=jax.ShapeDtypeStruct((PEERS, 128, 128), BF16),
+        out_shape=(jax.ShapeDtypeStruct((240, 128), F32), jax.ShapeDtypeStruct((240, 128), BF16)),
         in_specs=[pl.BlockSpec(memory_space=pltpu.VMEM)] * len(operands),
-        out_specs=pl.BlockSpec(memory_space=pltpu.VMEM),
+        out_specs=(pl.BlockSpec(memory_space=pltpu.VMEM),) * 2,
         scratch_shapes=[pltpu.VMEM(shape, kind) for shape, kind in shapes],
         compiler_params=pltpu.CompilerParams(vmem_limit_bytes=40 * 2**20),
         cost_estimate=pl.CostEstimate(flops=2 * 10**9, bytes_accessed=10**6, transcendentals=10**6),
@@ -348,34 +354,90 @@
     )(*operands)
 
 
-def sum_kernel(parts, cols, out, mine, bias, w_out, loss, bins):
-    me = 2 * lax.axis_index("band") + lax.axis_index("off")
+def join_kernel(kept, received, out):
+    first_core = lax.axis_index("band") % 2 == 0
+    total = kept[...] + received[...].astype(F32)
+    small = total[232:233] + total[233:234]
+    loss = total[234:235] + total[235:236]
+    small_hi = small.astype(BF16).astype(F32)
+    loss_hi = loss.astype(BF16).astype(F32)
+    tail = jnp.concatenate(
+        [small_hi, small - small_hi, loss_hi, loss - loss_hi, jnp.zeros((2, 128), F32)], axis=0
+    )
+
+    def to_all(rows):
+        return jnp.broadcast_to(rows[None], (CHIPS, rows.shape[0], 128))
+
+    extra = jnp.concatenate(
+        [total[72:88].reshape(CHIPS, 1, 128), total[88:104].reshape(CHIPS, 1, 128), to_all(tail)], axis=1
+    )
+    out[...] = jnp.concatenate(
+        [
+            to_all(total[0:72]),
+            jnp.where(first_core, extra, to_all(total[72:80])),
+            to_all(total[80:104]),
+            total[104:232].reshape(CHIPS, 8, 128),
+        ],
+        axis=1,
+    ).astype(BF16)
+
+
+def join_call(kept, received):
+    return pl.pallas_call(
+        join_kernel,
+        out_shape=jax.ShapeDtypeStruct((CHIPS, 112, 128), BF16),
+        in_specs=[pl.BlockSpec(memory_space=pltpu.VMEM)] * 2,
+        out_specs=pl.BlockSpec(memory_space=pltpu.VMEM),
+        compiler_params=pltpu.CompilerParams(vmem_limit_bytes=16 * 2**20),
+        name="join",
+    )(kept, received)
+
+
+def sum_kernel(parts, cols, out, mine, theirs, bins):
+    band = lax.axis_index("band")
+    off = lax.axis_index("off")
+    core = band % 2
     half_lane = lane_ids((1, 128)) < 64
     bins[...] = jnp.zeros(bins.shape, F32)
-    for band in range(BANDS):
-        for off in range(2):
-            piece = parts[2 * band + off, 0:112, :].astype(F32)
-            bins[band * 64 + 56 : band * 64 + 136, :] += jnp.where(half_lane, piece[0:80], 0.0)
-            start = (band + 2 * off) * 64 + 56
-            bins[start : start + 112, :] += jnp.where(half_lane, 0.0, piece)
-            spare = pltpu.roll(piece[80:112], 64, 1)
-            bins[start + 112 : start + 144, :] += jnp.where(half_lane, 0.0, spare)
-    gproj = bins[64:1088, :].astype(BF16).reshape(BANDS, 4, 16, 128)
-    mine[...] = bins[pl.ds(pl.multiple_of(64 + 32 * me, 32), 32), :].astype(BF16)
-    wide = jnp.concatenate([gproj[:, g].reshape(256, 128) for g in range(4)], axis=1)
+    split = jnp.where(core == 0, 72, 104)
+    used = row_ids((104, 128)) < split
+    for chip in range(CHIPS):
+        piece = jnp.where(used, parts[chip].astype(F32)[0:104], 0.0)
+        start = pl.multiple_of(chip // 2 * 128 + core * (chip % 2 * 128) + 56, 8)
+        bins[pl.ds(start, 104), :] += piece
+        bins[pl.ds(pl.multiple_of(start + split, 8), 104), :] += pltpu.roll(piece, 64, 1)
+
+    def own_half(x):
+        return jnp.where(
+            core == 0, jnp.where(half_lane, x, 0.0), jnp.where(half_lane, 0.0, pltpu.roll(x, 64, 1))
+        ).astype(BF16)
+
+    other = band + 1 - 2 * core
+    mine[...] = own_half(bins[pl.ds(pl.multiple_of(64 + 64 * band + 32 * off, 32), 32), :])
+    theirs[...] = own_half(bins[pl.ds(pl.multiple_of(64 + 64 * other + 32 * off, 32), 32), :])
+    halves = bins[64:1088, :].reshape(BANDS, 2, 32, 128)
+    dense = jnp.where(
+        half_lane, halves[:, 0].reshape(512, 128), pltpu.roll(halves[:, 1].reshape(512, 128), 64, 1)
+    ).astype(BF16)
     product = lax.dot_general(
-        cols[:, 64:80, :].reshape(256, 128), wide, (((0,), (0,)), ((), ())), preferred_element_type=F32
-    )
-    rows = product[0:32, 0:128]
-    for g in range(1, 4):
-        rows = rows + product[g * 32 : g * 32 + 32, g * 128 : g * 128 + 128]
-    total = jnp.sum(parts[:, 112:128, :].astype(F32), axis=0)
-    out[:, 0:32, :] = jnp.broadcast_to(rows.astype(BF16)[None], (PEERS, 32, 128))
-    out[:, 32:48, :] = jnp.broadcast_to(total.astype(BF16)[None], (PEERS, 16, 128))
-    small = total[9:10] + total[10:11]
-    bias[...] = small[:, 0:64]
-    w_out[...] = small[:, 64:128]
-    loss[...] = (total[11:12] + total[12:13])[:, 0:1]
+        cols[:, 64:96, :].reshape(512, 128), dense, (((0,), (0,)), ((), ())), preferred_element_type=F32
+    )
+    rows = product[0:64] + pltpu.roll(product[64:128], 64, 1)
+    rows = jnp.where(half_lane, rows[0:32], pltpu.roll(rows[32:64], 64, 1))
+    weights = jnp.sum(parts[:, 96:112, :].astype(F32), axis=0)[8:16]
+    extra = jnp.sum(parts[:, 64:80, :].astype(F32), axis=0)[8:16]
+    small = extra[2:3] + extra[3:4]
+    loss = extra[4:5] + extra[5:6]
+    small_hi = small.astype(BF16).astype(F32)
+    loss_hi = loss.astype(BF16).astype(F32)
+    whole = jnp.concatenate(
+        [
+            rows, weights, extra[0:2], small_hi, small - small_hi, loss_hi, loss - loss_hi,
+            jnp.zeros((2, 128), F32),
+        ],
+        axis=0,
+    )
+    out[...] = jnp.broadcast_to(whole.astype(BF16)[None], (PEERS, 48, 128))
 
 
 def sum_call(parts, cols):
@@ -384,46 +446,62 @@
         out_shape=(
             jax.ShapeDtypeStruct((PEERS, 48, 128), BF16),
             jax.ShapeDtypeStruct((32, 128), BF16),
+            jax.ShapeDtypeStruct((32, 128), BF16),
+        ),
+        in_specs=[pl.BlockSpec(memory_space=pltpu.VMEM)] * 2,
+        out_specs=(pl.BlockSpec(memory_space=pltpu.VMEM),) * 3,
+        scratch_shapes=[pltpu.VMEM((1408, 128), F32)],
+        compiler_params=pltpu.CompilerParams(vmem_limit_bytes=16 * 2**20),
+        name="sums",
+    )(parts, cols)
+
+
+def final_kernel(every, grad_proj_hbm, grad_conv_hbm, bias, w_out, loss, grad_proj, grad_conv_t, sems):
+    half_lane = lane_ids((1, 128)) < 64
+    puts = []
+    for k in range(4):
+        for chip in range(4 * k, 4 * k + 4):
+            source = chip // 2 * 4 + chip % 2
+            left = every[source, 0:32, :].astype(F32)
+            right = every[source + 2, 0:32, :].astype(F32)
+            row = chip * 64
+            grad_proj[row : row + 32, :] = jnp.where(half_lane, left, pltpu.roll(right, 64, 1))
+            grad_proj[row + 32 : row + 64, :] = jnp.where(half_lane, pltpu.roll(left, 64, 1), right)
+        rows = pl.ds(k * 256, 256)
+        puts.append(pltpu.make_async_copy(grad_proj.at[rows], grad_proj_hbm.at[rows], sems.at[k]))
+        puts[k].start()
+    conv = every[:, 32:48, :].astype(F32).reshape(8, 2, 2, 16, 128)
+    for core in range(2):
+        wide = conv[:, core, :, 0:8].reshape(128, 128)
+        for k in range(2):
+            lane = (2 - 2 * core + k) * 128
+            grad_conv_t[:, lane : lane + 128] = wide[k * 64 : k * 64 + 64]
+    first = conv[:, 0].reshape(CHIPS, 16, 128)
+    last = jnp.concatenate([first[:, 8], first[:, 9]], axis=0)
+    grad_conv_t[0:32, 512:576] = last[:, 0:64]
+    grad_conv_t[32:64, 512:576] = last[:, 64:128]
+    puts.append(pltpu.make_async_copy(grad_conv_t, grad_conv_hbm, sems.at[4]))
+    puts[4].start()
+    small = first[0, 10:11] + first[0, 11:12]
+    bias[...] = small[:, 0:64]
+    w_out[...] = small[:, 64:128]
+    loss[...] = (first[0, 12:13] + first[0, 13:14])[:, 0:1]
+    for put in puts:
+        put.wait()
+
+
+def final_call(every):
+    return pl.pallas_call(
+        final_kernel,
+        out_shape=(
+            jax.ShapeDtypeStruct((1024, 128), F32),
+            jax.ShapeDtypeStruct((64, 576), F32),
             jax.ShapeDtypeStruct((1, 64), F32),
             jax.ShapeDtypeStruct((1, 64), F32),
             jax.ShapeDtypeStruct((1, 1), F32),
         ),
-        in_specs=[pl.BlockSpec(memory_space=pltpu.VMEM)] * 2,
-        out_specs=(pl.BlockSpec(memory_space=pltpu.VMEM),) * 5,
-        scratch_shapes=[pltpu.VMEM((1408, 128), F32)],
-        compiler_params=pltpu.CompilerParams(vmem_limit_bytes=16 * 2**20),
-        name="sums",
-    )(parts, cols)
-
-
-def final_kernel(every, grad_proj_hbm, grad_conv_hbm, grad_proj, grad_conv_t, sems):
-    puts = []
-    for k in range(4):
-        rows = pl.ds(k * 256, 256)
-        grad_proj[k * 256 : k * 256 + 256, :] = (
-            every[k * 8 : k * 8 + 8, 0:32, :].astype(F32).reshape(256, 128)
-        )
-        puts.append(pltpu.make_async_copy(grad_proj.at[rows], grad_proj_hbm.at[rows], sems.at[k]))
-        puts[k].start()
-    conv = every[:, 32:48, :].astype(F32)
-    wide = conv[:, 0:8].reshape(256, 128)
-    for k in range(4):
-        grad_conv_t[:, k * 128 : k * 128 + 128] = wide[k * 64 : k * 64 + 64]
-    last = conv[:, 8]
-    grad_conv_t[0:32, 512:576] = last[:, 0:64]
-    grad_conv_t[32:64, 512:576] = last[:, 64:128]
-    puts.append(pltpu.make_async_copy(grad_conv_t, grad_conv_hbm, sems.at[4]))
-    puts[4].start()
-    for put in puts:
-        put.wait()
-
-
-def final_call(every):
-    return pl.pallas_call(
-        final_kernel,
-        out_shape=(jax.ShapeDtypeStruct((1024, 128), F32), jax.ShapeDtypeStruct((64, 576), F32)),
         in_specs=[pl.BlockSpec(memory_space=pltpu.VMEM)],
-        out_specs=(pl.BlockSpec(memory_space=pltpu.HBM),) * 2,
+        out_specs=(pl.BlockSpec(memory_space=pltpu.HBM),) * 2 + (pl.BlockSpec(memory_space=pltpu.VMEM),) * 3,
         scratch_shapes=[
             pltpu.VMEM((1024, 128), F32),
             pltpu.VMEM((64, 576), F32),
@@ -439,13 +517,18 @@
     ready = prep_call(
         mask.reshape(8, 128), target, conv_w.T, conv_b.reshape(1, 64), w_out.reshape(1, 64)
     )
-    parts = lax.all_to_all(tile_call(spread, *ready), GROUP, 0, 0, tiled=True)
-    sums, mine, bias, w_out, loss = sum_call(parts, spread)
+    swap = [(2 * i + o, 2 * (i + 1 - 2 * (i % 2)) + o) for i in range(BANDS) for o in range(2)]
+    same_core = [[2 * i + o for i in range(core, BANDS, 2) for o in range(2)] for core in range(2)]
+    kept, given = tile_call(spread, *ready)
+    joined = join_call(kept, lax.ppermute(given, GROUP, swap))
+    parts = lax.all_to_all(joined, GROUP, 0, 0, tiled=True, axis_index_groups=same_core)
+    sums, mine, theirs = sum_call(parts, spread)
     every = lax.all_to_all(sums, GROUP, 0, 0, tiled=True)
+    own = mine + lax.ppermute(theirs, GROUP, swap)
     grad_feats = lax.dot_general(
-        mine, w_proj, (((1,), (1,)), ((), ())), preferred_element_type=F32
+        own, w_proj, (((1,), (1,)), ((), ())), preferred_element_type=F32
     ).astype(BF16)
-    grad_proj, grad_conv_t = final_call(every)
+    grad_proj, grad_conv_t, bias, w_out, loss = final_call(every)
     return (loss.reshape(1), grad_proj, grad_conv_t.T, bias.reshape(64), w_out.reshape(64), grad_feats)
 
 

time: 64.2 us -> 60.2 us (0.938)
  blocking collectives: 22.7 us -> 14.6 us
  starting transfers between devices: 11.2 us -> 13.4 us
  waiting for transfers between devices: 12.6 us -> 13.7 us
  Pallas kernels: 12 us -> 12.8 us
    all_to_all x1, blocking collectives: 22.7 us -> 14.6 us  [body(): lax.all_to_all(joined, GROUP, 0, 0, tiled=True, axis_index_groups=same_core)]
    ppermute x0 -> x2, waiting for transfers between devices: none -> 1.73 us  [the longest x1 0.9 us: body(): joined = join_call(kept, lax.ppermute(given, GROUP, swap))]
    ppermute x0 -> x2, starting transfers between devices: none -> 1.52 us  [the longest x1 1.1 us: body(): joined = join_call(kept, lax.ppermute(given, GROUP, swap))]
    all_to_all x1, waiting for transfers between devices: 9.31 us -> 8.07 us  [body(): every = lax.all_to_all(sums, GROUP, 0, 0, tiled=True)]
    all_to_all x1, starting transfers between devices: 4.36 us -> 5.08 us  [body(): every = lax.all_to_all(sums, GROUP, 0, 0, tiled=True)]
    all_to_all x1, waiting for transfers between devices: 3.29 us -> 3.95 us  [body(): spread = lax.all_to_all(front_call(feats, w_proj), 'band', 0, 0, tiled=True)]
    pallas_call x2 -> x3, Pallas kernels: 9.27 us -> 9.18 us  [the longest x1 7.17 us: tile_call(): pl.pallas_call(tile_kernel, out_shape=(jax.ShapeDtypeStruct((240, 128), F...]
  transfers between devices with their start and end apart: 2 -> 4, of which waited for: 2 -> 4; matrix products, arithmetic and copies ran while one was open for 1% -> 1% of each run, Pallas kernels for 1% -> 1%
where the time goes in v5:
time: 60.2 us; the launch traced here: 59.7 us
  blocking collectives  14.6 us (24%)
  waiting for transfers between devices  13.7 us (23%)
  starting transfers between devices  13.4 us (22%)
  Pallas kernels  12.8 us (21%)
  local copies, waits for them, and re-layouts  3.72 us (6%)
  matrix products  0.83 us (1%)
  between operations  0.67 us (1%)
    all_to_all x1, blocking collectives, body(): lax.all_to_all(joined, GROUP, 0, 0, tiled=True, axis_index_groups=same_core)  14.6 us
    all_to_all x1, waiting for transfers between devices, body(): every = lax.all_to_all(sums, GROUP, 0, 0, tiled=True)  8.07 us
    pallas_call x1, Pallas kernels, tile_call(): pl.pallas_call(tile_kernel, out_shape=(jax.ShapeDtypeStruct((240, 128), F...  7.17 us
    all_to_all x1, starting transfers between devices, body(): spread = lax.all_to_all(front_call(feats, w_proj), 'band', 0, 0, tiled=True)  6.84 us
    all_to_all x1, starting transfers between devices, body(): every = lax.all_to_all(sums, GROUP, 0, 0, tiled=True)  5.08 us
    all_to_all x1, waiting for transfers between devices, body(): spread = lax.all_to_all(front_call(feats, w_proj), 'band', 0, 0, tiled=True)  3.95 us
    unnamed x12, local copies, waits for them, and re-layouts  3.72 us
    pallas_call x1, Pallas kernels, front_call(): pl.pallas_call(front_kernel, out_shape=jax.ShapeDtypeStruct((BANDS, 96, 1...  1.97 us
  transfers between devices with their start and end apart: 4, of which 4 were waited for; matrix products, arithmetic and copies ran while one was open for 1% of the time, Pallas kernels for 1%

profile of v5, /device:TPU:1, one launch (start us, length us, event | category | flops | bytes accessed | tf_op | source)
XLA Modules:
  0.0 59.7 jit_solution(14010286013227804866)
XLA Ops:
  0.6 2.0 %front.1 = bf16[16,96,128]{2,1,0:T(8,128)(2,1)} custom-call(bf16[64,1024]{1,0:T(8,128)(2,1)} %feats_hbm.1, bf16[1024,128]{1,0:T(8,128)(2,1)} %w_proj_hbm.1), custom_call_target="tpu_custom_call" | custom-call | tf_op jit(solution)/shard_map/front/pallas_call | solution.py:62
  2.6 6.8 %all-to-all-start = ((bf16[16,96,128]{2,1,0:T(8,128)(2,1)}), bf16[16,96,128]{2,1,0:T(8,128)(2,1)S(1)}, u32[]{:S(2)}, u32[]{:S(2)}) async-start(bf16[16,96,128]{2,1,0:T(8,128)(2,1)} %front.1), calls=%async_computation | async-start | bytes 786432 | tf_op jit(solution)/shard_map/all_to_all | solution.py:516
  9.4 0.0 copy-start
  9.5 0.9 %copy-done = bf16[576,64]{0,1:T(8,128)(2,1)S(1)} copy-done((bf16[576,64]{0,1:T(8,128)(2,1)S(1)}, bf16[576,64]{0,1:T(8,128)(2,1)}, u32[]{:S(2)}) %copy-start) | copy-done | bytes 73752
  10.3 0.0 copy-start.1
  10.3 0.8 %copy-done.1 = f32[64,2,64]{2,1,0:T(2,128)S(1)} copy-done((f32[64,2,64]{2,1,0:T(2,128)S(1)}, f32[64,2,64]{2,1,0:T(2,128)}, u32[]{:S(2)}) %copy-start.1) | copy-done | bytes 32792
  11.2 0.0 copy-start.2
  11.2 0.7 %copy-done.2 = s32[1024]{0:T(1024)S(1)} copy-done((s32[1024]{0:T(1024)S(1)}, s32[1024]{0:T(1024)}, u32[]{:S(2)}) %copy-start.2) | copy-done | bytes 4120
  11.9 0.0 copy-start.3
  11.9 0.7 %copy-done.3 = f32[64]{0:T(128)S(1)} copy-done((f32[64]{0:T(128)S(1)}, f32[64]{0:T(128)}, u32[]{:S(2)}) %copy-start.3) | copy-done | bytes 280
  12.5 0.0 copy-start.4
  12.5 0.7 %copy-done.4 = f32[64]{0:T(128)S(1)} copy-done((f32[64]{0:T(128)S(1)}, f32[64]{0:T(128)}, u32[]{:S(2)}) %copy-start.4) | copy-done | bytes 280
  13.2 0.6 %prepare.1 = (bf16[768,128]{1,0:T(8,128)(2,1)S(1)}, bf16[768,128]{1,0:T(8,128)(2,1)S(1)}, bf16[256,128]{1,0:T(8,128)(2,1)S(1)}, f32[512,1024]{1,0:T(8,128)S(1)},...) custom-call(s32[8,128]{1,0:T(8,128)S(1)} %bitcast.10, f32[64,2,64]{2,1,0:T(2,128)S(1)} %copy-done.1, ...), custom_call_target="tpu_custom_call" | custom-call | flops 300000000 | bytes 4000000 | tf_op jit(solution)/shard_map/prepare/pallas_call | solution.py:155
  13.8 3.9 %all-to-all-done.proj.cols = bf16[16,96,128]{2,1,0:T(8,128)(2,1)S(1)} async-done(((bf16[16,96,128]{2,1,0:T(8,128)(2,1)}), bf16[16,96,128]{2,1,0:T(8,128)(2,1)S(1)}, u32[]{:S(2)}, u32[]{:S(2)}) %all-to-all-start) | async-done | bytes 393248 | tf_op jit(solution)/shard_map/all_to_all | solution.py:516
  17.7 7.2 %tiles.1 = (f32[240,128]{1,0:T(8,128)S(1)}, bf16[240,128]{1,0:T(8,128)(2,1)S(1)}) custom-call(bf16[16,96,128]{2,1,0:T(8,128)(2,1)S(1)} %all-to-all-done.proj.cols, bf16[768,128]{1,0:T(8,128)(2,1)S(1)} %get-tuple-element.23.fwd_w, bf16[768,128]{1,0:T(8,128)(2,1)S(1)} %get-tuple-element.24.bwd_w, bf16[256,128]{1,0:T(8,128)(2,1)S(1)} %get-tuple-element.25.pred_w, ...), custom_call_target="tpu_custom_call" | custom-call | flops 2000000000 | bytes 1000000 | tf_op jit(solution)/shard_map/tiles/pallas_call | solution.py:345
  24.9 0.0 copy-start.5
  24.9 1.1 %collective-permute-start = (bf16[240,128]{1,0:T(8,128)(2,1)S(1)}, bf16[240,128]{1,0:T(8,128)(2,1)S(1)}, u32[]{:S(2)}, u32[]{:S(2)}) collective-permute-start(bf16[240,128]{1,0:T(8,128)(2,1)S(1)} %get-tuple-element.31), channel_id=1, source_target_pairs={{0,8},{4,12},{8,0},{12,4},{16,24},{20,28},{24,16},{28,20},{32,40},... | collective-permute-start | bytes 184328 | tf_op jit(solution)/shard_map/ppermute | solution.py:523
  26.0 0.9 %collective-permute-done.received = bf16[240,128]{1,0:T(8,128)(2,1)S(1)} collective-permute-done((bf16[240,128]{1,0:T(8,128)(2,1)S(1)}, bf16[240,128]{1,0:T(8,128)(2,1)S(1)}, u32[]{:S(2)}, u32[]{:S(2)}) %collective-permute-start) | collective-permute-done | bytes 61472 | tf_op jit(solution)/shard_map/ppermute | solution.py:523
  26.9 14.6 %all_to_all.15.parts = bf16[16,112,128]{2,1,0:T(8,128)(2,1)S(1)} all-to-all(bf16[16,112,128]{2,1,0:T(8,128)(2,1)S(1)} %join.1), channel_id=1, replica_groups={{0,4,16,20,32,36,48,52,64,68,80,84,96,100,112,116},{8,12,24,28,40,44,56..., dimensions={0} | all-to-all | bytes 917504 | tf_op jit(solution)/shard_map/all_to_all | solution.py:524
  41.5 1.5 %sums.1 = (bf16[32,48,128]{2,1,0:T(8,128)(2,1)}, bf16[32,128]{1,0:T(8,128)(2,1)S(1)}, bf16[32,128]{1,0:T(8,128)(2,1)S(1)}) custom-call(bf16[16,112,128]{2,1,0:T(8,128)(2,1)S(1)} %all_to_all.15.parts, bf16[16,96,128]{2,1,0:T(8,128)(2,1)S(1)} %all-to-all-done.proj.cols), custom_call_target="tpu_custom_call" | custom-call | tf_op jit(solution)/shard_map/sums/pallas_call | solution.py:444
  43.0 5.1 %all-to-all-start.2 = ((bf16[32,48,128]{2,1,0:T(8,128)(2,1)}), bf16[32,48,128]{2,1,0:T(8,128)(2,1)S(1)}, u32[]{:S(2)}, u32[]{:S(2)}) async-start(bf16[32,48,128]{2,1,0:T(8,128)(2,1)} %get-tuple-element.32), calls=%async_computation.2 | async-start | bytes 786432 | tf_op jit(solution)/shard_map/all_to_all | solution.py:526
  48.1 0.4 collective-permute-start.1
  48.5 0.8 %collective-permute-done.1 = bf16[32,128]{1,0:T(8,128)(2,1)S(1)} collective-permute-done((bf16[32,128]{1,0:T(8,128)(2,1)S(1)}, bf16[32,128]{1,0:T(8,128)(2,1)S(1)}, u32[]{:S(2)}, u32[]{:S(2)}) %collective-permute-start.1) | collective-permute-done | bytes 8224 | tf_op jit(solution)/shard_map/ppermute | solution.py:527
  49.4 0.0 copy-done.5
  49.4 0.8 %convolution_convert_fusion = bf16[32,1024]{1,0:T(8,128)(2,1)} fusion(bf16[1024,128]{1,0:T(8,128)(2,1)S(1)} %copy-done.5, bf16[32,128]{1,0:T(8,128)(2,1)S(1)} %get-tuple-element.38, bf16[32,128]{1,0:T(8,128)(2,1)S(1)} %collective-permute-done.1), kind=kOutput, calls=%fused_computation | convolution fusion | flops 8425472 | bytes 344064 | tf_op jit(solution)/shard_map/dot_general | solution.py:528
  50.2 8.1 %all-to-all-done.2.every = bf16[32,48,128]{2,1,0:T(8,128)(2,1)S(1)} async-done(((bf16[32,48,128]{2,1,0:T(8,128)(2,1)}), bf16[32,48,128]{2,1,0:T(8,128)(2,1)S(1)}, u32[]{:S(2)}, u32[]{:S(2)}) %all-to-all-start.2) | async-done | bytes 393248 | tf_op jit(solution)/shard_map/all_to_all | solution.py:526
  58.3 1.5 %outputs.1 = (f32[1024,128]{1,0:T(8,128)}, f32[64,576]{1,0:T(8,128)}, f32[1,64]{1,0:T(1,128)}, f32[1,64]{1,0:T(1,128)}, f32[1,1]{1,0:T(1,128)}) custom-call(bf16[32,48,128]{2,1,0:T(8,128)(2,1)S(1)} %all-to-all-done.2.every), custom_call_target="tpu_custom_call" | custom-call | tf_op jit(solution)/shard_map/outputs/pallas_call | solution.py:494
  (1 shorter events, 0.0 us)
Async XLA Ops:
  2.6 15.1 %all-to-all-start = ((bf16[16,96,128]{2,1,0:T(8,128)(2,1)}), bf16[16,96,128]{2,1,0:T(8,128)(2,1)S(1)}, u32[]{:S(2)}, u32[]{:S(2)}) async-start(bf16[16,96,128]{2,1,0:T(8,128)(2,1)} %front.1), calls=%async_computation | async-start | bytes 786432 | tf_op jit(solution)/shard_map/all_to_all | solution.py:516
  9.4 0.9 %copy-start = (bf16[576,64]{0,1:T(8,128)(2,1)S(1)}, bf16[576,64]{0,1:T(8,128)(2,1)}, u32[]{:S(2)}) copy-start(bf16[576,64]{0,1:T(8,128)(2,1)} %param.9) | copy-start | bytes 221188
  10.3 0.8 %copy-start.1 = (f32[64,2,64]{2,1,0:T(2,128)S(1)}, f32[64,2,64]{2,1,0:T(2,128)}, u32[]{:S(2)}) copy-start(f32[64,2,64]{2,1,0:T(2,128)} %target.1) | copy-start | bytes 98308
  11.2 0.7 %copy-start.2 = (s32[1024]{0:T(1024)S(1)}, s32[1024]{0:T(1024)}, u32[]{:S(2)}) copy-start(s32[1024]{0:T(1024)} %param.13) | copy-start | bytes 12292
  11.9 0.7 %copy-start.3 = (f32[64]{0:T(128)S(1)}, f32[64]{0:T(128)}, u32[]{:S(2)}) copy-start(f32[64]{0:T(128)} %param.10) | copy-start | bytes 772
  12.5 0.7 %copy-start.4 = (f32[64]{0:T(128)S(1)}, f32[64]{0:T(128)}, u32[]{:S(2)}) copy-start(f32[64]{0:T(128)} %param.11) | copy-start | bytes 772
  24.9 24.5 %copy-start.5 = (bf16[1024,128]{1,0:T(8,128)(2,1)S(1)}, bf16[1024,128]{1,0:T(8,128)(2,1)}, u32[]{:S(2)}) copy-start(bf16[1024,128]{1,0:T(8,128)(2,1)} %w_proj_hbm.1) | copy-start | bytes 786436
  24.9 2.0 %collective-permute-start = (bf16[240,128]{1,0:T(8,128)(2,1)S(1)}, bf16[240,128]{1,0:T(8,128)(2,1)S(1)}, u32[]{:S(2)}, u32[]{:S(2)}) collective-permute-start(bf16[240,128]{1,0:T(8,128)(2,1)S(1)} %get-tuple-element.31), channel_id=1, source_target_pairs={{0,8},{4,12},{8,0},{12,4},{16,24},{20,28},{24,16},{28,20},{32,40},... | collective-permute-start | bytes 184328 | tf_op jit(solution)/shard_map/ppermute | solution.py:523
  43.0 15.2 %all-to-all-start.2 = ((bf16[32,48,128]{2,1,0:T(8,128)(2,1)}), bf16[32,48,128]{2,1,0:T(8,128)(2,1)S(1)}, u32[]{:S(2)}, u32[]{:S(2)}) async-start(bf16[32,48,128]{2,1,0:T(8,128)(2,1)} %get-tuple-element.32), calls=%async_computation.2 | async-start | bytes 786432 | tf_op jit(solution)/shard_map/all_to_all | solution.py:526
  48.1 1.3 %collective-permute-start.1 = (bf16[32,128]{1,0:T(8,128)(2,1)S(1)}, bf16[32,128]{1,0:T(8,128)(2,1)S(1)}, u32[]{:S(2)}, u32[]{:S(2)}) collective-permute-start(bf16[32,128]{1,0:T(8,128)(2,1)S(1)} %get-tuple-element.39), channel_id=1, source_target_pairs={{0,8},{4,12},{8,0},{12,4},{16,24},{20,28},{24,16},{28,20},{32,40},... | collective-permute-start | bytes 24584 | tf_op jit(solution)/shard_map/ppermute | solution.py:527

commit v6 on v5

--- a/solution.py
+++ b/solution.py
@@ -8,7 +8,6 @@
 GELU_K = 0.7978845608028654
 GELU_C = 0.044715
 GROUP = ("band", "off")
-PEERS = 32
 CHIPS = 16
 BANDS = 16
 F32 = jnp.float32
@@ -50,18 +49,16 @@
         top, bottom = block[0:32], block[32:64]
         low = jnp.where(half_lane, top, pltpu.roll(bottom, 64, 1))
         high = jnp.where(half_lane, pltpu.roll(top, 64, 1), bottom)
-        packed = jnp.where(off == 0, low, high).astype(BF16)
-        out[2 * q, 64:96, :] = packed
-        out[2 * q + 1, 64:96, :] = packed
+        out[q, 64:96, :] = jnp.where(off == 0, low, high).astype(BF16)
     get_w.wait()
     proj = dot(feats[...], w_proj[...]).astype(BF16)
-    out[:, 0:64, :] = jnp.broadcast_to(proj[None], (BANDS, 64, 128))
+    out[:, 0:64, :] = jnp.broadcast_to(proj[None], (8, 64, 128))
 
 
 def front_call(feats, w_proj):
     return pl.pallas_call(
         front_kernel,
-        out_shape=jax.ShapeDtypeStruct((BANDS, 96, 128), BF16),
+        out_shape=jax.ShapeDtypeStruct((8, 96, 128), BF16),
         in_specs=[pl.BlockSpec(memory_space=pltpu.HBM)] * 2,
         out_specs=pl.BlockSpec(memory_space=pltpu.VMEM),
         scratch_shapes=[
@@ -75,7 +72,7 @@
 
 
 def prep_kernel(
-    mask, target, conv_t, conv_b, w_out, fwd_w, bwd_w, pred_w, goal, row_mask, col_mask, small
+    mask, target, conv_t, fwd_w, bwd_w, goal, row_mask, col_mask
 ):
     band = lax.axis_index("band")
     first = band + 2 * lax.axis_index("off")
@@ -93,17 +90,6 @@
             row = ty * 256 + k * 64
             bwd_w[row : row + 64, :] = jnp.concatenate([left[k], right[k]], axis=1).astype(BF16)
 
-    bias2 = jnp.concatenate([conv_b[...], conv_b[...]], axis=1)
-    twice = jnp.concatenate([w_out[...], w_out[...]], axis=1)
-    small[...] = jnp.concatenate([bias2, twice, jnp.zeros((6, 128), F32)], axis=0)
-    diagonal = row_ids((128, 128)) == lane_ids((128, 128))
-    halves = (row_ids((128, 128)) < 64) == (lane_ids((128, 128)) < 64)
-    twice_hi = twice.astype(BF16).astype(F32)
-    halves_b = halves.astype(F32).astype(BF16)
-    for k, part in enumerate((twice_hi, twice - twice_hi)):
-        line = jnp.where(diagonal, part, 0.0).astype(BF16)
-        pred_w[k * 128 : k * 128 + 128, :] = dot(line, halves_b).astype(BF16)
-
     mask_all = mask[...].astype(F32)
     mask_lane = lane_ids((8, 128))
     by_band = jnp.concatenate(
@@ -149,8 +135,7 @@
 
 def prep_call(*operands):
     shapes = [
-        ((768, 128), BF16), ((768, 128), BF16), ((256, 128), BF16), ((512, 1024), F32), ((512, 128), F32),
-        ((64, 128), F32), ((8, 128), F32),
+        ((768, 128), BF16), ((768, 128), BF16), ((512, 1024), F32), ((512, 128), F32), ((64, 128), F32),
     ]
     return pl.pallas_call(
         prep_kernel,
@@ -164,12 +149,13 @@
 
 
 def tile_kernel(
-    proj, fwd_w, bwd_w, pred_w, goal, row_mask, col_mask, small,
+    same, other, conv_b, w_out, fwd_w, bwd_w, goal, row_mask, col_mask,
     keep, send,
     rows_u, cols_v, pair, slope, grads, pre, hid16, hid32, weighted, guess, grad_rows, grad_cols, grad_w,
     place_u, place_v,
 ):
     band = lax.axis_index("band")
+    core = band % 2
     first = band + 2 * lax.axis_index("off")
     half_lane = lane_ids((1, 128)) < 64
 
@@ -179,14 +165,21 @@
     grads[128:640, 0:128] = jnp.zeros((512, 128), BF16)
     grads[128:640, 1152:1280] = jnp.zeros((512, 128), BF16)
 
+    def channels(which, rows):
+        inside = jnp.clip(which, 0, BANDS - 1)
+        at = inside // 2
+        return jnp.where(
+            inside % 2 == core, same[at, rows, :].astype(F32), other[at, rows, :].astype(F32)
+        )
+
     def ending(which):
-        return proj[jnp.clip(which, 0, BANDS - 1), 48:64, :].astype(F32)[8:16]
+        return channels(which, slice(48, 64))[8:16]
 
     def whole(which):
-        return proj[jnp.minimum(which, BANDS - 1), 0:64, :].astype(F32)
+        return channels(which, slice(0, 64))
 
     def opening(which):
-        return proj[jnp.minimum(which, BANDS - 1), 0:16, :].astype(F32)[0:8]
+        return channels(which, slice(0, 16))[0:8]
 
     u = jnp.concatenate([ending(band - 1), whole(band), opening(band + 1)], axis=0)
     rows_u[...] = jnp.where(half_lane, u, pltpu.roll(u, 64, 1))
@@ -197,8 +190,9 @@
     v_high = v[:, 1].reshape(72, 128)
     cols_v[...] = jnp.where(half_lane, pltpu.roll(v_low, 64, 1), v_high)
 
-    bias2 = small[0:1, :]
-    out_w2 = small[1:2, :]
+    bias2 = jnp.concatenate([conv_b[...], conv_b[...]], axis=1)
+    out_w2 = jnp.concatenate([w_out[...], w_out[...]], axis=1)
+    halves = ((row_ids((128, 128)) < 64) == (lane_ids((128, 128)) < 64)).astype(F32).astype(BF16)
 
     def pair_stage(bp):
         lane = slice(bp * 128, bp * 128 + 128)
@@ -231,13 +225,12 @@
             row = slice(aq * 64, aq * 64 + 64)
             value, grade = gelu_parts(pre[row, lane] + bias2, 0.5)
             hid32[row, lane] = value
-            hid16[row, lane] = value.astype(BF16)
+            hid16[row, lane] = (value * out_w2).astype(BF16)
             weighted[row, lane] = grade * out_w2
 
     def pred_stage(bp):
         lane = slice(bp * 128, bp * 128 + 128)
-        low = hid16[:, lane]
-        guess[:, lane] = dot(jnp.concatenate([low, low], axis=1), pred_w[...])
+        guess[:, lane] = dot(hid16[:, lane], halves)
 
     def loss_stage(bp, sums):
         loss_sum, bias_sum, out_sum = sums
@@ -297,7 +290,6 @@
             pair_stage(step)
 
     row_part = jnp.sum(grad_rows[...].reshape(80, 8, 128), axis=1)
-    core = band % 2
     place_u[...] = jnp.zeros(place_u.shape, F32)
     place_v[...] = jnp.zeros(place_v.shape, F32)
     place_u[pl.ds(pl.multiple_of(core * 64, 64), 80), :] = row_part + pltpu.roll(row_part, 64, 1)
@@ -393,7 +385,7 @@
     )(kept, received)
 
 
-def sum_kernel(parts, cols, out, mine, theirs, bins):
+def sum_kernel(parts, same, other, out, mine, theirs, bins):
     band = lax.axis_index("band")
     off = lax.axis_index("off")
     core = band % 2
@@ -412,16 +404,25 @@
             core == 0, jnp.where(half_lane, x, 0.0), jnp.where(half_lane, 0.0, pltpu.roll(x, 64, 1))
         ).astype(BF16)
 
-    other = band + 1 - 2 * core
+    sibling = band + 1 - 2 * core
     mine[...] = own_half(bins[pl.ds(pl.multiple_of(64 + 64 * band + 32 * off, 32), 32), :])
-    theirs[...] = own_half(bins[pl.ds(pl.multiple_of(64 + 64 * other + 32 * off, 32), 32), :])
-    halves = bins[64:1088, :].reshape(BANDS, 2, 32, 128)
-    dense = jnp.where(
-        half_lane, halves[:, 0].reshape(512, 128), pltpu.roll(halves[:, 1].reshape(512, 128), 64, 1)
-    ).astype(BF16)
-    product = lax.dot_general(
-        cols[:, 64:96, :].reshape(512, 128), dense, (((0,), (0,)), ((), ())), preferred_element_type=F32
-    )
+    theirs[...] = own_half(bins[pl.ds(pl.multiple_of(64 + 64 * sibling + 32 * off, 32), 32), :])
+    halves = bins[64:1088, :].reshape(8, 2, 2, 32, 128)
+
+    def dense(bands):
+        return jnp.where(
+            half_lane, bands[:, 0].reshape(256, 128), pltpu.roll(bands[:, 1].reshape(256, 128), 64, 1)
+        )
+
+    even, odd = dense(halves[:, 0]), dense(halves[:, 1])
+    product = 0.0
+    for cols, bands in (
+        (same, jnp.where(core == 0, even, odd)), (other, jnp.where(core == 0, odd, even))
+    ):
+        product = product + lax.dot_general(
+            cols[:, 64:96, :].reshape(256, 128), bands.astype(BF16), (((0,), (0,)), ((), ())),
+            preferred_element_type=F32,
+        )
     rows = product[0:64] + pltpu.roll(product[64:128], 64, 1)
     rows = jnp.where(half_lane, rows[0:32], pltpu.roll(rows[32:64], 64, 1))
     weights = jnp.sum(parts[:, 96:112, :].astype(F32), axis=0)[8:16]
@@ -437,98 +438,111 @@
         ],
         axis=0,
     )
-    out[...] = jnp.broadcast_to(whole.astype(BF16)[None], (PEERS, 48, 128))
-
-
-def sum_call(parts, cols):
+    out[...] = jnp.broadcast_to(whole.astype(BF16)[None], (CHIPS, 48, 128))
+
+
+def sum_call(parts, same, other):
     return pl.pallas_call(
         sum_kernel,
         out_shape=(
-            jax.ShapeDtypeStruct((PEERS, 48, 128), BF16),
+            jax.ShapeDtypeStruct((CHIPS, 48, 128), BF16),
             jax.ShapeDtypeStruct((32, 128), BF16),
             jax.ShapeDtypeStruct((32, 128), BF16),
         ),
-        in_specs=[pl.BlockSpec(memory_space=pltpu.VMEM)] * 2,
+        in_specs=[pl.BlockSpec(memory_space=pltpu.VMEM)] * 3,
         out_specs=(pl.BlockSpec(memory_space=pltpu.VMEM),) * 3,
         scratch_shapes=[pltpu.VMEM((1408, 128), F32)],
         compiler_params=pltpu.CompilerParams(vmem_limit_bytes=16 * 2**20),
         name="sums",
-    )(parts, cols)
-
-
-def final_kernel(every, grad_proj_hbm, grad_conv_hbm, bias, w_out, loss, grad_proj, grad_conv_t, sems):
+    )(parts, same, other)
+
+
+def final_kernel(
+    same, other, mine, received, w_proj, grad_proj_hbm, grad_conv_hbm, grad_feats_hbm, bias, w_out, loss,
+    grad_proj, grad_conv_t, grad_feats, sems,
+):
+    is_first = lax.axis_index("band") % 2 == 0
     half_lane = lane_ids((1, 128)) < 64
+    firsts, seconds = [], []
     puts = []
+    gproj = mine[...] + received[...]
+    grad_feats[...] = lax.dot_general(
+        gproj, w_proj[...], (((1,), (1,)), ((), ())), preferred_element_type=F32
+    ).astype(BF16)
+    put_feats = pltpu.make_async_copy(grad_feats, grad_feats_hbm, sems.at[5])
+    put_feats.start()
     for k in range(4):
         for chip in range(4 * k, 4 * k + 4):
-            source = chip // 2 * 4 + chip % 2
-            left = every[source, 0:32, :].astype(F32)
-            right = every[source + 2, 0:32, :].astype(F32)
+            here = same[chip].astype(F32)
+            there = other[chip].astype(F32)
+            left = jnp.where(is_first, here, there)
+            right = jnp.where(is_first, there, here)
+            firsts.append(left[32:48])
+            seconds.append(right[32:40])
+            left, right = left[0:32], right[0:32]
             row = chip * 64
             grad_proj[row : row + 32, :] = jnp.where(half_lane, left, pltpu.roll(right, 64, 1))
             grad_proj[row + 32 : row + 64, :] = jnp.where(half_lane, pltpu.roll(left, 64, 1), right)
         rows = pl.ds(k * 256, 256)
         puts.append(pltpu.make_async_copy(grad_proj.at[rows], grad_proj_hbm.at[rows], sems.at[k]))
         puts[k].start()
-    conv = every[:, 32:48, :].astype(F32).reshape(8, 2, 2, 16, 128)
-    for core in range(2):
-        wide = conv[:, core, :, 0:8].reshape(128, 128)
-        for k in range(2):
-            lane = (2 - 2 * core + k) * 128
-            grad_conv_t[:, lane : lane + 128] = wide[k * 64 : k * 64 + 64]
-    first = conv[:, 0].reshape(CHIPS, 16, 128)
-    last = jnp.concatenate([first[:, 8], first[:, 9]], axis=0)
+    wide = jnp.concatenate(seconds + [first[0:8] for first in firsts], axis=0)
+    for k in range(4):
+        grad_conv_t[:, k * 128 : k * 128 + 128] = wide[k * 64 : k * 64 + 64]
+    last = jnp.concatenate([first[8:9] for first in firsts] + [first[9:10] for first in firsts], axis=0)
     grad_conv_t[0:32, 512:576] = last[:, 0:64]
     grad_conv_t[32:64, 512:576] = last[:, 64:128]
     puts.append(pltpu.make_async_copy(grad_conv_t, grad_conv_hbm, sems.at[4]))
     puts[4].start()
-    small = first[0, 10:11] + first[0, 11:12]
+    small = firsts[0][10:11] + firsts[0][11:12]
     bias[...] = small[:, 0:64]
     w_out[...] = small[:, 64:128]
-    loss[...] = (first[0, 12:13] + first[0, 13:14])[:, 0:1]
-    for put in puts:
+    loss[...] = (firsts[0][12:13] + firsts[0][13:14])[:, 0:1]
+    for put in puts + [put_feats]:
         put.wait()
 
 
-def final_call(every):
+def final_call(*operands):
     return pl.pallas_call(
         final_kernel,
         out_shape=(
             jax.ShapeDtypeStruct((1024, 128), F32),
             jax.ShapeDtypeStruct((64, 576), F32),
+            jax.ShapeDtypeStruct((32, 1024), BF16),
             jax.ShapeDtypeStruct((1, 64), F32),
             jax.ShapeDtypeStruct((1, 64), F32),
             jax.ShapeDtypeStruct((1, 1), F32),
         ),
-        in_specs=[pl.BlockSpec(memory_space=pltpu.VMEM)],
-        out_specs=(pl.BlockSpec(memory_space=pltpu.HBM),) * 2 + (pl.BlockSpec(memory_space=pltpu.VMEM),) * 3,
+        in_specs=[pl.BlockSpec(memory_space=pltpu.VMEM)] * len(operands),
+        out_specs=(pl.BlockSpec(memory_space=pltpu.HBM),) * 3 + (pl.BlockSpec(memory_space=pltpu.VMEM),) * 3,
         scratch_shapes=[
             pltpu.VMEM((1024, 128), F32),
             pltpu.VMEM((64, 576), F32),
-            pltpu.SemaphoreType.DMA((5,)),
+            pltpu.VMEM((32, 1024), BF16),
+            pltpu.SemaphoreType.DMA((6,)),
         ],
         compiler_params=pltpu.CompilerParams(vmem_limit_bytes=8 * 2**20),
         name="outputs",
-    )(every)
+    )(*operands)
 
 
 def body(feats, w_proj, conv_w, conv_b, w_out, target, mask):
-    spread = lax.all_to_all(front_call(feats, w_proj), "band", 0, 0, tiled=True)
-    ready = prep_call(
-        mask.reshape(8, 128), target, conv_w.T, conv_b.reshape(1, 64), w_out.reshape(1, 64)
-    )
     swap = [(2 * i + o, 2 * (i + 1 - 2 * (i % 2)) + o) for i in range(BANDS) for o in range(2)]
     same_core = [[2 * i + o for i in range(core, BANDS, 2) for o in range(2)] for core in range(2)]
-    kept, given = tile_call(spread, *ready)
+    same_row = [[2 * i + o for i in range(core, BANDS, 2)] for core in range(2) for o in range(2)]
+    same = lax.all_to_all(front_call(feats, w_proj), GROUP, 0, 0, tiled=True, axis_index_groups=same_row)
+    ready = prep_call(mask.reshape(8, 128), target, conv_w.T)
+    same, ready = lax.optimization_barrier((same, ready))
+    other = lax.ppermute(same, GROUP, swap)
+    kept, given = tile_call(same, other, conv_b.reshape(1, 64), w_out.reshape(1, 64), *ready)
     joined = join_call(kept, lax.ppermute(given, GROUP, swap))
     parts = lax.all_to_all(joined, GROUP, 0, 0, tiled=True, axis_index_groups=same_core)
-    sums, mine, theirs = sum_call(parts, spread)
-    every = lax.all_to_all(sums, GROUP, 0, 0, tiled=True)
-    own = mine + lax.ppermute(theirs, GROUP, swap)
-    grad_feats = lax.dot_general(
-        own, w_proj, (((1,), (1,)), ((), ())), preferred_element_type=F32
-    ).astype(BF16)
-    grad_proj, grad_conv_t, bias, w_out, loss = final_call(every)
+    sums, mine, theirs = sum_call(parts, same, other)
+    every = lax.all_to_all(sums, GROUP, 0, 0, tiled=True, axis_index_groups=same_core)
+    every, theirs = lax.optimization_barrier((every, theirs))
+    grad_proj, grad_conv_t, grad_feats, bias, w_out, loss = final_call(
+        every, lax.ppermute(every, GROUP, swap), mine, lax.ppermute(theirs, GROUP, swap), w_proj
+    )
     return (loss.reshape(1), grad_proj, grad_conv_t.T, bias.reshape(64), w_out.reshape(64), grad_feats)
 
 

time: 60.2 us -> 57.9 us (0.962)
  blocking collectives: 14.6 us -> 25.3 us
  waiting for transfers between devices: 13.7 us -> 6.23 us
  starting transfers between devices: 13.4 us -> 10.9 us
  local copies, waits for them, and re-layouts: 3.72 us -> 2.42 us
  matrix products: 0.83 us -> 0 us
  Pallas kernels: 12.8 us -> 12 us
    all_to_all x0 -> x1, blocking collectives: none -> 11.1 us  [body(): lax.all_to_all(sums, GROUP, 0, 0, tiled=True, axis_index_groups=same_core)]
    all_to_all x2 -> x1, waiting for transfers between devices: 12 us -> 3.09 us  [body(): lax.all_to_all(front_call(feats, w_proj), GROUP, 0, 0, tiled=True, axis_i...]
    all_to_all x2 -> x1, starting transfers between devices: 11.9 us -> 5.87 us  [body(): lax.all_to_all(front_call(feats, w_proj), GROUP, 0, 0, tiled=True, axis_i...]
    ppermute x1 -> x3, starting transfers between devices: 0.42 us -> 4.53 us  [the longest x1 2.72 us: body(): lax.ppermute(every, GROUP, swap)]
    ppermute x1 -> x3, waiting for transfers between devices: 0.83 us -> 2.24 us  [the longest x1 1.17 us: body(): lax.ppermute(theirs, GROUP, swap)]
    unnamed x12, local copies, waits for them, and re-layouts: 3.72 us -> 2.42 us
    dot_general x1 -> x0, matrix products: 0.83 us -> none  [body(): lax.dot_general(own, w_proj, (((1,), (1,)), ((), ())), preferred_element_...]
    pallas_call x2, Pallas kernels: 3.47 us -> 2.65 us  [the longest x1 1.9 us: front_call(): pl.pallas_call(front_kernel, out_shape=jax.ShapeDtypeStruct((8, 96, 128),...]
  transfers between devices with their start and end apart: 4 -> 5, of which waited for: 4 -> 4; matrix products, arithmetic and copies ran while one was open for 1% -> 0% of each run, Pallas kernels for 1% -> 1%
where the time goes in v6:
time: 57.9 us; the launch traced here: 57.5 us
  blocking collectives  25.3 us (44%)
  Pallas kernels  12 us (21%)
  starting transfers between devices  10.9 us (19%)
  waiting for transfers between devices  6.23 us (11%)
  local copies, waits for them, and re-layouts  2.42 us (4%)
  between operations  0.7 us (1%)
    all_to_all x1, blocking collectives, body(): lax.all_to_all(joined, GROUP, 0, 0, tiled=True, axis_index_groups=same_core)  14.1 us
    all_to_all x1, blocking collectives, body(): lax.all_to_all(sums, GROUP, 0, 0, tiled=True, axis_index_groups=same_core)  11.1 us
    pallas_call x1, Pallas kernels, tile_call(): pl.pallas_call(tile_kernel, out_shape=(jax.ShapeDtypeStruct((240, 128), F...  7.13 us
    all_to_all x1, starting transfers between devices, body(): lax.all_to_all(front_call(feats, w_proj), GROUP, 0, 0, tiled=True, axis_i...  5.87 us
    all_to_all x1, waiting for transfers between devices, body(): lax.all_to_all(front_call(feats, w_proj), GROUP, 0, 0, tiled=True, axis_i...  3.09 us
    ppermute x1, starting transfers between devices, body(): lax.ppermute(every, GROUP, swap)  2.72 us
    unnamed x12, local copies, waits for them, and re-layouts  2.42 us
    pallas_call x1, Pallas kernels, front_call(): pl.pallas_call(front_kernel, out_shape=jax.ShapeDtypeStruct((8, 96, 128),...  1.9 us
  transfers between devices with their start and end apart: 5, of which 4 were waited for; matrix products, arithmetic and copies ran while one was open for 0% of the time, Pallas kernels for 1%

profile of v6, /device:TPU:1, one launch (start us, length us, event | category | flops | bytes accessed | tf_op | source)
XLA Modules:
  0.0 57.5 jit_solution(14694045658291465396)
XLA Ops:
  0.6 0.0 copy-start.5
  0.6 0.0 copy-start.4
  0.7 1.9 %front.1 = bf16[8,96,128]{2,1,0:T(8,128)(2,1)} custom-call(bf16[64,1024]{1,0:T(8,128)(2,1)} %feats_hbm.1, bf16[1024,128]{1,0:T(8,128)(2,1)} %w_proj.1), custom_call_target="tpu_custom_call" | custom-call | tf_op jit(solution)/shard_map/front/pallas_call | solution.py:59
  2.6 5.9 %all-to-all-start = ((bf16[8,96,128]{2,1,0:T(8,128)(2,1)}), bf16[8,96,128]{2,1,0:T(8,128)(2,1)S(1)}, u32[]{:S(2)}, u32[]{:S(2)}) async-start(bf16[8,96,128]{2,1,0:T(8,128)(2,1)} %front.1), calls=%async_computation | async-start | bytes 393216 | tf_op jit(solution)/shard_map/all_to_all | solution.py:533
  8.4 0.0 copy-start.1
  8.4 0.9 %copy-done.1 = bf16[576,64]{0,1:T(8,128)(2,1)S(1)} copy-done((bf16[576,64]{0,1:T(8,128)(2,1)S(1)}, bf16[576,64]{0,1:T(8,128)(2,1)}, u32[]{:S(2)}) %copy-start.1) | copy-done | bytes 73752
  9.3 0.0 copy-start.2
  9.3 0.8 %copy-done.2 = f32[64,2,64]{2,1,0:T(2,128)S(1)} copy-done((f32[64,2,64]{2,1,0:T(2,128)S(1)}, f32[64,2,64]{2,1,0:T(2,128)}, u32[]{:S(2)}) %copy-start.2) | copy-done | bytes 32792
  10.2 0.0 copy-start.3
  10.2 0.7 %copy-done.3 = s32[1024]{0:T(1024)S(1)} copy-done((s32[1024]{0:T(1024)S(1)}, s32[1024]{0:T(1024)}, u32[]{:S(2)}) %copy-start.3) | copy-done | bytes 4120
  10.9 0.6 prepare.1
  11.4 3.1 %all-to-all-done.same = bf16[8,96,128]{2,1,0:T(8,128)(2,1)S(1)} async-done(((bf16[8,96,128]{2,1,0:T(8,128)(2,1)}), bf16[8,96,128]{2,1,0:T(8,128)(2,1)S(1)}, u32[]{:S(2)}, u32[]{:S(2)}) %all-to-all-start) | async-done | bytes 196640 | tf_op jit(solution)/shard_map/all_to_all | solution.py:533
  14.5 1.8 %collective-permute-start = (bf16[8,96,128]{2,1,0:T(8,128)(2,1)S(1)}, bf16[8,96,128]{2,1,0:T(8,128)(2,1)S(1)}, u32[]{:S(2)}, u32[]{:S(2)}) collective-permute-start(bf16[8,96,128]{2,1,0:T(8,128)(2,1)S(1)} %all-to-all-done.same), channel_id=1, source_target_pairs={{0,8},{4,12},{8,0},{12,4},{16,24},{20,28},{24,16},{28,20},{32,40},... | collective-permute-start | bytes 589832 | tf_op jit(solution)/shard_map/ppermute | solution.py:536
  16.3 1.1 %collective-permute-done.other = bf16[8,96,128]{2,1,0:T(8,128)(2,1)S(1)} collective-permute-done((bf16[8,96,128]{2,1,0:T(8,128)(2,1)S(1)}, bf16[8,96,128]{2,1,0:T(8,128)(2,1)S(1)}, u32[]{:S(2)}, u32[]{:S(2)}) %collective-permute-start) | collective-permute-done | bytes 196640 | tf_op jit(solution)/shard_map/ppermute | solution.py:536
  17.4 0.0 copy-done.5
  17.4 0.0 copy-done.4
  17.4 7.1 %tiles.1 = (f32[240,128]{1,0:T(8,128)S(1)}, bf16[240,128]{1,0:T(8,128)(2,1)S(1)}) custom-call(bf16[8,96,128]{2,1,0:T(8,128)(2,1)S(1)} %all-to-all-done.same, bf16[8,96,128]{2,1,0:T(8,128)(2,1)S(1)} %collective-permute-done.other, f32[1,64]{1,0:T(1,128)S(1)} %bitcast.10, f32[1,64]{1,0:T(1,128)S(1)} %bitcast.11, bf16[768,128]{1,0:T(8,128)(2,1)S(1)} %get-tuple-element.36.fwd_w, ...), custom_call_target="tpu_custom_call" | custom-call | flops 2000000000 | bytes 1000000 | tf_op jit(solution)/shard_map/tiles/pallas_call | solution.py:337
  24.5 0.0 copy-start
  24.6 0.4 collective-permute-start.1
  25.0 0.9 %collective-permute-done.1.received = bf16[240,128]{1,0:T(8,128)(2,1)S(1)} collective-permute-done((bf16[240,128]{1,0:T(8,128)(2,1)S(1)}, bf16[240,128]{1,0:T(8,128)(2,1)S(1)}, u32[]{:S(2)}, u32[]{:S(2)}) %collective-permute-start.1) | collective-permute-done | bytes 61472 | tf_op jit(solution)/shard_map/ppermute | solution.py:538
  25.9 14.1 %all_to_all.15.parts = bf16[16,112,128]{2,1,0:T(8,128)(2,1)S(1)} all-to-all(bf16[16,112,128]{2,1,0:T(8,128)(2,1)S(1)} %join.1), channel_id=1, replica_groups={{0,4,16,20,32,36,48,52,64,68,80,84,96,100,112,116},{8,12,24,28,40,44,56..., dimensions={0} | all-to-all | bytes 917504 | tf_op jit(solution)/shard_map/all_to_all | solution.py:539
  40.1 0.7 %sums.1 = (bf16[16,48,128]{2,1,0:T(8,128)(2,1)S(1)}, bf16[32,128]{1,0:T(8,128)(2,1)S(1)}, bf16[32,128]{1,0:T(8,128)(2,1)S(1)}) custom-call(bf16[16,112,128]{2,1,0:T(8,128)(2,1)S(1)} %all_to_all.15.parts, bf16[8,96,128]{2,1,0:T(8,128)(2,1)S(1)} %all-to-all-done.same, bf16[8,96,128]{2,1,0:T(8,128)(2,1)S(1)} %collective-permute-done.other), custom_call_target="tpu_custom_call" | custom-call | tf_op jit(solution)/shard_map/sums/pallas_call | solution.py:445
  40.8 11.1 %all_to_all.16.same = bf16[16,48,128]{2,1,0:T(8,128)(2,1)S(1)} all-to-all(bf16[16,48,128]{2,1,0:T(8,128)(2,1)S(1)} %get-tuple-element.43), channel_id=1, replica_groups={{0,4,16,20,32,36,48,52,64,68,80,84,96,100,112,116},{8,12,24,28,40,44,56..., dimensions={0} | all-to-all | bytes 393216 | tf_op jit(solution)/shard_map/all_to_all | solution.py:541
  51.9 2.7 %collective-permute-start.2 = (bf16[16,48,128]{2,1,0:T(8,128)(2,1)S(1)}, bf16[16,48,128]{2,1,0:T(8,128)(2,1)S(1)}, u32[]{:S(2)}, u32[]{:S(2)}) collective-permute-start(bf16[16,48,128]{2,1,0:T(8,128)(2,1)S(1)} %all_to_all.16.same), channel_id=1, source_target_pairs={{0,8},{4,12},{8,0},{12,4},{16,24},{20,28},{24,16},{28,20},{32,40},... | collective-permute-start | bytes 589832 | tf_op jit(solution)/shard_map/ppermute | solution.py:544
  54.7 0.0 collective-permute-start.3
  54.7 1.2 %collective-permute-done.3.received = bf16[32,128]{1,0:T(8,128)(2,1)S(1)} collective-permute-done((bf16[32,128]{1,0:T(8,128)(2,1)S(1)}, bf16[32,128]{1,0:T(8,128)(2,1)S(1)}, u32[]{:S(2)}, u32[]{:S(2)}) %collective-permute-start.3) | collective-permute-done | bytes 8224 | tf_op jit(solution)/shard_map/ppermute | solution.py:544
  55.8 0.0 collective-permute-done.2.other
  55.8 0.0 copy-done
  55.8 1.6 %outputs.1 = (f32[1024,128]{1,0:T(8,128)}, f32[64,576]{1,0:T(8,128)}, bf16[32,1024]{1,0:T(8,128)(2,1)}, f32[1,64]{1,0:T(1,128)}, f32[1,64]{1,0:T(1,128)}, /*index=5*/f32[1,1]{1,0:T(1,128)}) custom-call(bf16[16,48,128]{2,1,0:T(8,128)(2,1)S(1)} %all_to_all.16.same, bf16[16,48,128]{2,1,0:T(8,128)(2,1)S(1)} %collective-permute-done.2.other, ...), custom_call_target="tpu_custom_call" | custom-call | tf_op jit(solution)/shard_map/outputs/pallas_call | solution.py:506
  (1 shorter events, 0.0 us)
Async XLA Ops:
  0.6 16.8 %copy-start.5 = (f32[64]{0:T(128)S(1)}, f32[64]{0:T(128)}, u32[]{:S(2)}) copy-start(f32[64]{0:T(128)} %param.11) | copy-start | bytes 772
  0.6 16.8 %copy-start.4 = (f32[64]{0:T(128)S(1)}, f32[64]{0:T(128)}, u32[]{:S(2)}) copy-start(f32[64]{0:T(128)} %param.10) | copy-start | bytes 772
  2.6 12.0 %all-to-all-start = ((bf16[8,96,128]{2,1,0:T(8,128)(2,1)}), bf16[8,96,128]{2,1,0:T(8,128)(2,1)S(1)}, u32[]{:S(2)}, u32[]{:S(2)}) async-start(bf16[8,96,128]{2,1,0:T(8,128)(2,1)} %front.1), calls=%async_computation | async-start | bytes 393216 | tf_op jit(solution)/shard_map/all_to_all | solution.py:533
  8.4 0.9 %copy-start.1 = (bf16[576,64]{0,1:T(8,128)(2,1)S(1)}, bf16[576,64]{0,1:T(8,128)(2,1)}, u32[]{:S(2)}) copy-start(bf16[576,64]{0,1:T(8,128)(2,1)} %param.9) | copy-start | bytes 221188
  9.3 0.8 %copy-start.2 = (f32[64,2,64]{2,1,0:T(2,128)S(1)}, f32[64,2,64]{2,1,0:T(2,128)}, u32[]{:S(2)}) copy-start(f32[64,2,64]{2,1,0:T(2,128)} %target.1) | copy-start | bytes 98308
  10.2 0.7 %copy-start.3 = (s32[1024]{0:T(1024)S(1)}, s32[1024]{0:T(1024)}, u32[]{:S(2)}) copy-start(s32[1024]{0:T(1024)} %param.13) | copy-start | bytes 12292
  14.5 2.9 %collective-permute-start = (bf16[8,96,128]{2,1,0:T(8,128)(2,1)S(1)}, bf16[8,96,128]{2,1,0:T(8,128)(2,1)S(1)}, u32[]{:S(2)}, u32[]{:S(2)}) collective-permute-start(bf16[8,96,128]{2,1,0:T(8,128)(2,1)S(1)} %all-to-all-done.same), channel_id=1, source_target_pairs={{0,8},{4,12},{8,0},{12,4},{16,24},{20,28},{24,16},{28,20},{32,40},... | collective-permute-start | bytes 589832 | tf_op jit(solution)/shard_map/ppermute | solution.py:536
  24.5 31.3 %copy-start = (bf16[1024,128]{1,0:T(8,128)(2,1)S(1)}, bf16[1024,128]{1,0:T(8,128)(2,1)}, u32[]{:S(2)}) copy-start(bf16[1024,128]{1,0:T(8,128)(2,1)} %w_proj.1) | copy-start | bytes 786436
  24.6 1.3 %collective-permute-start.1 = (bf16[240,128]{1,0:T(8,128)(2,1)S(1)}, bf16[240,128]{1,0:T(8,128)(2,1)S(1)}, u32[]{:S(2)}, u32[]{:S(2)}) collective-permute-start(bf16[240,128]{1,0:T(8,128)(2,1)S(1)} %get-tuple-element.42), channel_id=1, source_target_pairs={{0,8},{4,12},{8,0},{12,4},{16,24},{20,28},{24,16},{28,20},{32,40},... | collective-permute-start | bytes 184328 | tf_op jit(solution)/shard_map/ppermute | solution.py:538
  51.9 3.9 %collective-permute-start.2 = (bf16[16,48,128]{2,1,0:T(8,128)(2,1)S(1)}, bf16[16,48,128]{2,1,0:T(8,128)(2,1)S(1)}, u32[]{:S(2)}, u32[]{:S(2)}) collective-permute-start(bf16[16,48,128]{2,1,0:T(8,128)(2,1)S(1)} %all_to_all.16.same), channel_id=1, source_target_pairs={{0,8},{4,12},{8,0},{12,4},{16,24},{20,28},{24,16},{28,20},{32,40},... | collective-permute-start | bytes 589832 | tf_op jit(solution)/shard_map/ppermute | solution.py:544
  54.7 1.2 %collective-permute-start.3 = (bf16[32,128]{1,0:T(8,128)(2,1)S(1)}, bf16[32,128]{1,0:T(8,128)(2,1)S(1)}, u32[]{:S(2)}, u32[]{:S(2)}) collective-permute-start(bf16[32,128]{1,0:T(8,128)(2,1)S(1)} %get-tuple-element.47), channel_id=1, source_target_pairs={{0,8},{4,12},{8,0},{12,4},{16,24},{20,28},{24,16},{28,20},{32,40},... | collective-permute-start | bytes 24584 | tf_op jit(solution)/shard_map/ppermute | solution.py:544

commit v7 on v6

--- a/solution.py
+++ b/solution.py
@@ -15,12 +15,10 @@
 
 
 def gelu_parts(x, half):
-    square = x * x
-    t = jnp.tanh(x * (GELU_K + (GELU_K * GELU_C) * square))
-    one_plus = 1.0 + t
-    scaled = x * half
-    value = scaled * one_plus
-    slope = one_plus * (half + (scaled * (1.0 - t)) * (GELU_K + (3.0 * GELU_K * GELU_C) * square))
+    inner = GELU_K + (GELU_K * GELU_C) * (x * x)
+    gate = half + half * jnp.tanh(x * inner)
+    value = x * gate
+    slope = gate + (value * (1.0 - gate)) * (6.0 * inner - 4.0 * GELU_K)
     return value, slope
 
 
@@ -89,7 +87,6 @@
         for k in range(4):
             row = ty * 256 + k * 64
             bwd_w[row : row + 64, :] = jnp.concatenate([left[k], right[k]], axis=1).astype(BF16)
-
     mask_all = mask[...].astype(F32)
     mask_lane = lane_ids((8, 128))
     by_band = jnp.concatenate(
@@ -152,7 +149,7 @@
     same, other, conv_b, w_out, fwd_w, bwd_w, goal, row_mask, col_mask,
     keep, send,
     rows_u, cols_v, pair, slope, grads, pre, hid16, hid32, weighted, guess, grad_rows, grad_cols, grad_w,
-    place_u, place_v,
+    place_u, place_v, fwd_2, bwd_2,
 ):
     band = lax.axis_index("band")
     core = band % 2
@@ -164,6 +161,16 @@
     grads[640:768, :] = zero_rows
     grads[128:640, 0:128] = jnp.zeros((512, 128), BF16)
     grads[128:640, 1152:1280] = jnp.zeros((512, 128), BF16)
+
+    none = jnp.zeros((256, 128), BF16)
+    for t in range(4):
+        row = slice(t * 256, t * 256 + 256)
+        for parity in range(2):
+            lane = slice(parity * 128, parity * 128 + 128)
+            ty = t - parity
+            fwd_2[row, lane] = fwd_w[ty * 256 : ty * 256 + 256, :] if 0 <= ty < 3 else none
+            ty = parity - t + 2
+            bwd_2[row, lane] = bwd_w[ty * 256 : ty * 256 + 256, :] if 0 <= ty < 3 else none
 
     def channels(which, rows):
         inside = jnp.clip(which, 0, BANDS - 1)
@@ -213,11 +220,22 @@
 
     def conv_stage(bp):
         lane = bp * 128
-        pre[:, lane : lane + 128] = (
-            dot(pair[0:512, lane : lane + 256], fwd_w[0:256, :])
-            + dot(pair[64:576, lane : lane + 256], fwd_w[256:512, :])
-            + dot(pair[128:640, lane : lane + 256], fwd_w[512:768, :])
+        part = dot(
+            jnp.concatenate(
+                [
+                    jnp.concatenate(
+                        [pair[(2 * a + t) * 64 : (2 * a + t) * 64 + 64, lane : lane + 256] for a in range(4)], axis=0
+                    )
+                    for t in range(4)
+                ],
+                axis=1,
+            ),
+            fwd_2[...],
         )
+        for a in range(4):
+            for parity in range(2):
+                row = (2 * a + parity) * 64
+                pre[row : row + 64, lane : lane + 128] = part[a * 64 : a * 64 + 64, parity * 128 : parity * 128 + 128]
 
     def act_stage(bp):
         lane = slice(bp * 128, bp * 128 + 128)
@@ -260,34 +278,50 @@
 
     def back_stage(bp):
         lane = bp * 128
-        part = (
-            dot(grads[128:768, lane : lane + 256], bwd_w[0:256, :])
-            + dot(grads[64:704, lane : lane + 256], bwd_w[256:512, :])
-            + dot(grads[0:640, lane : lane + 256], bwd_w[512:768, :])
-        ) * slope[:, lane : lane + 128]
-        if bp == 0:
-            grad_rows[...] = part
-        else:
-            grad_rows[...] += part
-        grad_cols[bp * 8 : bp * 8 + 8, :] = jnp.sum(part.reshape(80, 8, 128), axis=0)
+        part = dot(
+            jnp.concatenate(
+                [
+                    jnp.concatenate(
+                        [grads[(2 * a + t) * 64 : (2 * a + t) * 64 + 64, lane : lane + 256] for a in range(5)], axis=0
+                    )
+                    for t in range(4)
+                ],
+                axis=1,
+            ),
+            bwd_2[...],
+        )
+        col_sum = jnp.zeros((8, 128), F32)
+        for a in range(5):
+            for parity in range(2):
+                row = (2 * a + parity) * 64
+                block = (
+                    part[a * 64 : a * 64 + 64, parity * 128 : parity * 128 + 128]
+                    * slope[row : row + 64, lane : lane + 128]
+                )
+                if bp == 0:
+                    grad_rows[row : row + 64, :] = block
+                else:
+                    grad_rows[row : row + 64, :] += block
+                col_sum = col_sum + jnp.sum(block.reshape(8, 8, 128), axis=0)
+        grad_cols[bp * 8 : bp * 8 + 8, :] = col_sum
 
     zero8 = jnp.zeros((8, 128), F32)
     totals = (zero8, zero8, zero8)
     for step in range(15):
+        if step < 9:
+            pair_stage(step)
+        if 2 <= step < 10:
+            conv_stage(step - 2)
+        if 3 <= step < 11:
+            act_stage(step - 3)
         if 6 <= step:
             back_stage(step - 6)
+        if 5 <= step < 13:
+            totals = loss_stage(step - 5, totals)
         if 6 <= step < 14:
             weights_stage(step - 6)
-        if 5 <= step < 13:
-            totals = loss_stage(step - 5, totals)
         if 4 <= step < 12:
             pred_stage(step - 4)
-        if 3 <= step < 11:
-            act_stage(step - 3)
-        if 2 <= step < 10:
-            conv_stage(step - 2)
-        if step < 9:
-            pair_stage(step)
 
     row_part = jnp.sum(grad_rows[...].reshape(80, 8, 128), axis=1)
     place_u[...] = jnp.zeros(place_u.shape, F32)
@@ -333,6 +367,7 @@
         ((80, 128), F32), ((72, 128), F32), ((640, 1152), BF16), ((640, 1152), F32), ((768, 1280), BF16),
         ((512, 1024), F32), ((512, 1024), BF16), ((512, 1024), F32), ((512, 1024), F32), ((512, 1024), F32),
         ((640, 128), F32), ((72, 128), F32), ((128, 768), F32), ((208, 128), F32), ((208, 128), F32),
+        ((1024, 256), BF16), ((1024, 256), BF16),
     ]
     return pl.pallas_call(
         tile_kernel,
@@ -458,19 +493,14 @@
 
 
 def final_kernel(
-    same, other, mine, received, w_proj, grad_proj_hbm, grad_conv_hbm, grad_feats_hbm, bias, w_out, loss,
-    grad_proj, grad_conv_t, grad_feats, sems,
+    same, other, mine, received, w_proj,
+    grad_proj_hbm, grad_conv_hbm, grad_feats_hbm, bias_hbm, w_out_hbm, loss_hbm,
+    grad_proj, grad_conv_t, grad_feats, bias, w_out, loss, sems,
 ):
     is_first = lax.axis_index("band") % 2 == 0
     half_lane = lane_ids((1, 128)) < 64
     firsts, seconds = [], []
     puts = []
-    gproj = mine[...] + received[...]
-    grad_feats[...] = lax.dot_general(
-        gproj, w_proj[...], (((1,), (1,)), ((), ())), preferred_element_type=F32
-    ).astype(BF16)
-    put_feats = pltpu.make_async_copy(grad_feats, grad_feats_hbm, sems.at[5])
-    put_feats.start()
     for k in range(4):
         for chip in range(4 * k, 4 * k + 4):
             here = same[chip].astype(F32)
@@ -498,6 +528,15 @@
     bias[...] = small[:, 0:64]
     w_out[...] = small[:, 64:128]
     loss[...] = (firsts[0][12:13] + firsts[0][13:14])[:, 0:1]
+    for k, (held, result) in enumerate(((bias, bias_hbm), (w_out, w_out_hbm), (loss, loss_hbm))):
+        puts.append(pltpu.make_async_copy(held, result, sems.at[6 + k]))
+        puts[5 + k].start()
+    gproj = mine[...] + received[...]
+    grad_feats[...] = lax.dot_general(
+        gproj, w_proj[...], (((1,), (1,)), ((), ())), preferred_element_type=F32
+    ).astype(BF16)
+    put_feats = pltpu.make_async_copy(grad_feats, grad_feats_hbm, sems.at[5])
+    put_feats.start()
     for put in puts + [put_feats]:
         put.wait()
 
@@ -514,12 +553,15 @@
             jax.ShapeDtypeStruct((1, 1), F32),
         ),
         in_specs=[pl.BlockSpec(memory_space=pltpu.VMEM)] * len(operands),
-        out_specs=(pl.BlockSpec(memory_space=pltpu.HBM),) * 3 + (pl.BlockSpec(memory_space=pltpu.VMEM),) * 3,
+        out_specs=(pl.BlockSpec(memory_space=pltpu.HBM),) * 6,
         scratch_shapes=[
             pltpu.VMEM((1024, 128), F32),
             pltpu.VMEM((64, 576), F32),
             pltpu.VMEM((32, 1024), BF16),
-            pltpu.SemaphoreType.DMA((6,)),
+            pltpu.VMEM((1, 64), F32),
+            pltpu.VMEM((1, 64), F32),
+            pltpu.VMEM((1, 1), F32),
+            pltpu.SemaphoreType.DMA((9,)),
         ],
         compiler_params=pltpu.CompilerParams(vmem_limit_bytes=8 * 2**20),
         name="outputs",

time: 57.9 us -> 56.5 us (0.976)
  Pallas kernels: 12 us -> 10.6 us
    pallas_call x1, Pallas kernels: 7.13 us -> 6.25 us  [tile_call(): pl.pallas_call(tile_kernel, out_shape=(jax.ShapeDtypeStruct((240, 128), F...]
where the time goes in v7:
time: 56.5 us; the launch traced here: 56 us
  blocking collectives  25.3 us (45%)
  starting transfers between devices  10.9 us (19%)
  Pallas kernels  10.6 us (19%)
  waiting for transfers between devices  6.23 us (11%)
  local copies, waits for them, and re-layouts  2.42 us (4%)
  between operations  0.69 us (1%)
    all_to_all x1, blocking collectives, body(): lax.all_to_all(joined, GROUP, 0, 0, tiled=True, axis_index_groups=same_core)  14.1 us
    all_to_all x1, blocking collectives, body(): lax.all_to_all(sums, GROUP, 0, 0, tiled=True, axis_index_groups=same_core)  11.1 us
    pallas_call x1, Pallas kernels, tile_call(): pl.pallas_call(tile_kernel, out_shape=(jax.ShapeDtypeStruct((240, 128), F...  6.25 us
    all_to_all x1, starting transfers between devices, body(): lax.all_to_all(front_call(feats, w_proj), GROUP, 0, 0, tiled=True, axis_i...  5.87 us
    all_to_all x1, waiting for transfers between devices, body(): lax.all_to_all(front_call(feats, w_proj), GROUP, 0, 0, tiled=True, axis_i...  3.09 us
    ppermute x1, starting transfers between devices, body(): lax.ppermute(every, GROUP, swap)  2.72 us
    unnamed x12, local copies, waits for them, and re-layouts  2.42 us
    pallas_call x1, Pallas kernels, front_call(): pl.pallas_call(front_kernel, out_shape=jax.ShapeDtypeStruct((8, 96, 128),...  1.9 us
  transfers between devices with their start and end apart: 5, of which 4 were waited for; matrix products, arithmetic and copies ran while one was open for 0% of the time, Pallas kernels for 1%

profile of v7, /device:TPU:1, one launch (start us, length us, event | category | flops | bytes accessed | tf_op | source)
XLA Modules:
  0.0 56.0 jit_solution(13428954563970276054)
XLA Ops:
  0.6 0.0 copy-start.5
  0.6 0.0 copy-start.4
  0.7 1.9 %front.1 = bf16[8,96,128]{2,1,0:T(8,128)(2,1)} custom-call(bf16[64,1024]{1,0:T(8,128)(2,1)} %feats_hbm.1, bf16[1024,128]{1,0:T(8,128)(2,1)} %w_proj.1), custom_call_target="tpu_custom_call" | custom-call | tf_op jit(solution)/shard_map/front/pallas_call | solution.py:57
  2.6 5.9 %all-to-all-start = ((bf16[8,96,128]{2,1,0:T(8,128)(2,1)}), bf16[8,96,128]{2,1,0:T(8,128)(2,1)S(1)}, u32[]{:S(2)}, u32[]{:S(2)}) async-start(bf16[8,96,128]{2,1,0:T(8,128)(2,1)} %front.1), calls=%async_computation | async-start | bytes 393216 | tf_op jit(solution)/shard_map/all_to_all | solution.py:575
  8.4 0.0 copy-start.1
  8.4 0.9 %copy-done.1 = bf16[576,64]{0,1:T(8,128)(2,1)S(1)} copy-done((bf16[576,64]{0,1:T(8,128)(2,1)S(1)}, bf16[576,64]{0,1:T(8,128)(2,1)}, u32[]{:S(2)}) %copy-start.1) | copy-done | bytes 73752
  9.3 0.0 copy-start.2
  9.3 0.8 %copy-done.2 = f32[64,2,64]{2,1,0:T(2,128)S(1)} copy-done((f32[64,2,64]{2,1,0:T(2,128)S(1)}, f32[64,2,64]{2,1,0:T(2,128)}, u32[]{:S(2)}) %copy-start.2) | copy-done | bytes 32792
  10.2 0.0 copy-start.3
  10.2 0.7 %copy-done.3 = s32[1024]{0:T(1024)S(1)} copy-done((s32[1024]{0:T(1024)S(1)}, s32[1024]{0:T(1024)}, u32[]{:S(2)}) %copy-start.3) | copy-done | bytes 4120
  10.9 0.6 %prepare.1 = (bf16[768,128]{1,0:T(8,128)(2,1)S(1)}, bf16[768,128]{1,0:T(8,128)(2,1)S(1)}, f32[512,1024]{1,0:T(8,128)S(1)}, f32[512,128]{1,0:T(8,128)S(1)}, f32[64,128]{1,0:T(8,128)S(1)}) custom-call(s32[8,128]{1,0:T(8,128)S(1)} %bitcast.9, f32[64,2,64]{2,1,0:T(2,128)S(1)} %copy-done.2, bf16[64,576]{1,0:T(8,128)(2,1)S(1)} %bitcast.8), custom_call_target="tpu_custom_call" | custom-call | flops 300000000 | bytes 4000000 | tf_op jit(solution)/shard_map/prepare/pallas_call | solution.py:137
  11.4 3.1 %all-to-all-done.same = bf16[8,96,128]{2,1,0:T(8,128)(2,1)S(1)} async-done(((bf16[8,96,128]{2,1,0:T(8,128)(2,1)}), bf16[8,96,128]{2,1,0:T(8,128)(2,1)S(1)}, u32[]{:S(2)}, u32[]{:S(2)}) %all-to-all-start) | async-done | bytes 196640 | tf_op jit(solution)/shard_map/all_to_all | solution.py:575
  14.5 1.8 %collective-permute-start = (bf16[8,96,128]{2,1,0:T(8,128)(2,1)S(1)}, bf16[8,96,128]{2,1,0:T(8,128)(2,1)S(1)}, u32[]{:S(2)}, u32[]{:S(2)}) collective-permute-start(bf16[8,96,128]{2,1,0:T(8,128)(2,1)S(1)} %all-to-all-done.same), channel_id=1, source_target_pairs={{0,8},{4,12},{8,0},{12,4},{16,24},{20,28},{24,16},{28,20},{32,40},... | collective-permute-start | bytes 589832 | tf_op jit(solution)/shard_map/ppermute | solution.py:578
  16.3 1.1 %collective-permute-done.other = bf16[8,96,128]{2,1,0:T(8,128)(2,1)S(1)} collective-permute-done((bf16[8,96,128]{2,1,0:T(8,128)(2,1)S(1)}, bf16[8,96,128]{2,1,0:T(8,128)(2,1)S(1)}, u32[]{:S(2)}, u32[]{:S(2)}) %collective-permute-start) | collective-permute-done | bytes 196640 | tf_op jit(solution)/shard_map/ppermute | solution.py:578
  17.4 0.0 copy-done.5
  17.4 0.0 copy-done.4
  17.4 6.3 %tiles.1 = (f32[240,128]{1,0:T(8,128)S(1)}, bf16[240,128]{1,0:T(8,128)(2,1)S(1)}) custom-call(bf16[8,96,128]{2,1,0:T(8,128)(2,1)S(1)} %all-to-all-done.same, bf16[8,96,128]{2,1,0:T(8,128)(2,1)S(1)} %collective-permute-done.other, f32[1,64]{1,0:T(1,128)S(1)} %bitcast.10, f32[1,64]{1,0:T(1,128)S(1)} %bitcast.11, bf16[768,128]{1,0:T(8,128)(2,1)S(1)} %get-tuple-element.36.fwd_w, ...), custom_call_target="tpu_custom_call" | custom-call | flops 2000000000 | bytes 1000000 | tf_op jit(solution)/shard_map/tiles/pallas_call | solution.py:372
  23.7 0.0 copy-start
  23.7 0.4 collective-permute-start.1
  24.1 0.9 %collective-permute-done.1.received = bf16[240,128]{1,0:T(8,128)(2,1)S(1)} collective-permute-done((bf16[240,128]{1,0:T(8,128)(2,1)S(1)}, bf16[240,128]{1,0:T(8,128)(2,1)S(1)}, u32[]{:S(2)}, u32[]{:S(2)}) %collective-permute-start.1) | collective-permute-done | bytes 61472 | tf_op jit(solution)/shard_map/ppermute | solution.py:580
  25.1 14.1 %all_to_all.15.parts = bf16[16,112,128]{2,1,0:T(8,128)(2,1)S(1)} all-to-all(bf16[16,112,128]{2,1,0:T(8,128)(2,1)S(1)} %join.1), channel_id=1, replica_groups={{0,4,16,20,32,36,48,52,64,68,80,84,96,100,112,116},{8,12,24,28,40,44,56..., dimensions={0} | all-to-all | bytes 917504 | tf_op jit(solution)/shard_map/all_to_all | solution.py:581
  39.2 0.7 %sums.1 = (bf16[16,48,128]{2,1,0:T(8,128)(2,1)S(1)}, bf16[32,128]{1,0:T(8,128)(2,1)S(1)}, bf16[32,128]{1,0:T(8,128)(2,1)S(1)}) custom-call(bf16[16,112,128]{2,1,0:T(8,128)(2,1)S(1)} %all_to_all.15.parts, bf16[8,96,128]{2,1,0:T(8,128)(2,1)S(1)} %all-to-all-done.same, bf16[8,96,128]{2,1,0:T(8,128)(2,1)S(1)} %collective-permute-done.other), custom_call_target="tpu_custom_call" | custom-call | tf_op jit(solution)/shard_map/sums/pallas_call | solution.py:480
  39.9 11.1 %all_to_all.16.same = bf16[16,48,128]{2,1,0:T(8,128)(2,1)S(1)} all-to-all(bf16[16,48,128]{2,1,0:T(8,128)(2,1)S(1)} %get-tuple-element.43), channel_id=1, replica_groups={{0,4,16,20,32,36,48,52,64,68,80,84,96,100,112,116},{8,12,24,28,40,44,56..., dimensions={0} | all-to-all | bytes 393216 | tf_op jit(solution)/shard_map/all_to_all | solution.py:583
  51.1 2.7 %collective-permute-start.2 = (bf16[16,48,128]{2,1,0:T(8,128)(2,1)S(1)}, bf16[16,48,128]{2,1,0:T(8,128)(2,1)S(1)}, u32[]{:S(2)}, u32[]{:S(2)}) collective-permute-start(bf16[16,48,128]{2,1,0:T(8,128)(2,1)S(1)} %all_to_all.16.same), channel_id=1, source_target_pairs={{0,8},{4,12},{8,0},{12,4},{16,24},{20,28},{24,16},{28,20},{32,40},... | collective-permute-start | bytes 589832 | tf_op jit(solution)/shard_map/ppermute | solution.py:586
  53.8 0.0 collective-permute-start.3
  53.8 1.2 %collective-permute-done.3.received = bf16[32,128]{1,0:T(8,128)(2,1)S(1)} collective-permute-done((bf16[32,128]{1,0:T(8,128)(2,1)S(1)}, bf16[32,128]{1,0:T(8,128)(2,1)S(1)}, u32[]{:S(2)}, u32[]{:S(2)}) %collective-permute-start.3) | collective-permute-done | bytes 8224 | tf_op jit(solution)/shard_map/ppermute | solution.py:586
  55.0 0.0 collective-permute-done.2.other
  55.0 0.0 copy-done
  55.0 1.1 %outputs.1 = (f32[1024,128]{1,0:T(8,128)}, f32[64,576]{1,0:T(8,128)}, bf16[32,1024]{1,0:T(8,128)(2,1)}, f32[1,64]{1,0:T(1,128)}, f32[1,64]{1,0:T(1,128)}, /*index=5*/f32[1,1]{1,0:T(1,128)}) custom-call(bf16[16,48,128]{2,1,0:T(8,128)(2,1)S(1)} %all_to_all.16.same, bf16[16,48,128]{2,1,0:T(8,128)(2,1)S(1)} %collective-permute-done.2.other, ...), custom_call_target="tpu_custom_call" | custom-call | tf_op jit(solution)/shard_map/outputs/pallas_call | solution.py:545
  (1 shorter events, 0.0 us)
Async XLA Ops:
  0.6 16.8 %copy-start.5 = (f32[64]{0:T(128)S(1)}, f32[64]{0:T(128)}, u32[]{:S(2)}) copy-start(f32[64]{0:T(128)} %param.11) | copy-start | bytes 772
  0.6 16.8 %copy-start.4 = (f32[64]{0:T(128)S(1)}, f32[64]{0:T(128)}, u32[]{:S(2)}) copy-start(f32[64]{0:T(128)} %param.10) | copy-start | bytes 772
  2.6 12.0 %all-to-all-start = ((bf16[8,96,128]{2,1,0:T(8,128)(2,1)}), bf16[8,96,128]{2,1,0:T(8,128)(2,1)S(1)}, u32[]{:S(2)}, u32[]{:S(2)}) async-start(bf16[8,96,128]{2,1,0:T(8,128)(2,1)} %front.1), calls=%async_computation | async-start | bytes 393216 | tf_op jit(solution)/shard_map/all_to_all | solution.py:575
  8.4 0.9 %copy-start.1 = (bf16[576,64]{0,1:T(8,128)(2,1)S(1)}, bf16[576,64]{0,1:T(8,128)(2,1)}, u32[]{:S(2)}) copy-start(bf16[576,64]{0,1:T(8,128)(2,1)} %param.9) | copy-start | bytes 221188
  9.3 0.8 %copy-start.2 = (f32[64,2,64]{2,1,0:T(2,128)S(1)}, f32[64,2,64]{2,1,0:T(2,128)}, u32[]{:S(2)}) copy-start(f32[64,2,64]{2,1,0:T(2,128)} %target.1) | copy-start | bytes 98308
  10.2 0.7 %copy-start.3 = (s32[1024]{0:T(1024)S(1)}, s32[1024]{0:T(1024)}, u32[]{:S(2)}) copy-start(s32[1024]{0:T(1024)} %param.13) | copy-start | bytes 12292
  14.5 2.9 %collective-permute-start = (bf16[8,96,128]{2,1,0:T(8,128)(2,1)S(1)}, bf16[8,96,128]{2,1,0:T(8,128)(2,1)S(1)}, u32[]{:S(2)}, u32[]{:S(2)}) collective-permute-start(bf16[8,96,128]{2,1,0:T(8,128)(2,1)S(1)} %all-to-all-done.same), channel_id=1, source_target_pairs={{0,8},{4,12},{8,0},{12,4},{16,24},{20,28},{24,16},{28,20},{32,40},... | collective-permute-start | bytes 589832 | tf_op jit(solution)/shard_map/ppermute | solution.py:578
  23.7 31.3 %copy-start = (bf16[1024,128]{1,0:T(8,128)(2,1)S(1)}, bf16[1024,128]{1,0:T(8,128)(2,1)}, u32[]{:S(2)}) copy-start(bf16[1024,128]{1,0:T(8,128)(2,1)} %w_proj.1) | copy-start | bytes 786436
  23.7 1.3 %collective-permute-start.1 = (bf16[240,128]{1,0:T(8,128)(2,1)S(1)}, bf16[240,128]{1,0:T(8,128)(2,1)S(1)}, u32[]{:S(2)}, u32[]{:S(2)}) collective-permute-start(bf16[240,128]{1,0:T(8,128)(2,1)S(1)} %get-tuple-element.42), channel_id=1, source_target_pairs={{0,8},{4,12},{8,0},{12,4},{16,24},{20,28},{24,16},{28,20},{32,40},... | collective-permute-start | bytes 184328 | tf_op jit(solution)/shard_map/ppermute | solution.py:580
  51.1 3.9 %collective-permute-start.2 = (bf16[16,48,128]{2,1,0:T(8,128)(2,1)S(1)}, bf16[16,48,128]{2,1,0:T(8,128)(2,1)S(1)}, u32[]{:S(2)}, u32[]{:S(2)}) collective-permute-start(bf16[16,48,128]{2,1,0:T(8,128)(2,1)S(1)} %all_to_all.16.same), channel_id=1, source_target_pairs={{0,8},{4,12},{8,0},{12,4},{16,24},{20,28},{24,16},{28,20},{32,40},... | collective-permute-start | bytes 589832 | tf_op jit(solution)/shard_map/ppermute | solution.py:586
  53.8 1.2 %collective-permute-start.3 = (bf16[32,128]{1,0:T(8,128)(2,1)S(1)}, bf16[32,128]{1,0:T(8,128)(2,1)S(1)}, u32[]{:S(2)}, u32[]{:S(2)}) collective-permute-start(bf16[32,128]{1,0:T(8,128)(2,1)S(1)} %get-tuple-element.47), channel_id=1, source_target_pairs={{0,8},{4,12},{8,0},{12,4},{16,24},{20,28},{24,16},{28,20},{32,40},... | collective-permute-start | bytes 24584 | tf_op jit(solution)/shard_map/ppermute | solution.py:586

commit v8 on v7

--- a/solution.py
+++ b/solution.py
@@ -156,21 +156,18 @@
     first = band + 2 * lax.axis_index("off")
     half_lane = lane_ids((1, 128)) < 64
 
-    zero_rows = jnp.zeros((128, 1280), BF16)
-    grads[0:128, :] = zero_rows
-    grads[640:768, :] = zero_rows
-    grads[128:640, 0:128] = jnp.zeros((512, 128), BF16)
-    grads[128:640, 1152:1280] = jnp.zeros((512, 128), BF16)
-
     none = jnp.zeros((256, 128), BF16)
     for t in range(4):
-        row = slice(t * 256, t * 256 + 256)
         for parity in range(2):
-            lane = slice(parity * 128, parity * 128 + 128)
             ty = t - parity
-            fwd_2[row, lane] = fwd_w[ty * 256 : ty * 256 + 256, :] if 0 <= ty < 3 else none
-            ty = parity - t + 2
-            bwd_2[row, lane] = bwd_w[ty * 256 : ty * 256 + 256, :] if 0 <= ty < 3 else none
+            fwd_2[t * 256 : t * 256 + 256, parity * 128 : parity * 128 + 128] = (
+                fwd_w[ty * 256 : ty * 256 + 256, :] if 0 <= ty < 3 else none
+            )
+    for t, taps in enumerate(((2, None, 0, 1), (1, 2, None, 0))):
+        for k, ty in enumerate(taps):
+            bwd_2[t * 256 : t * 256 + 256, k * 128 : k * 128 + 128] = (
+                none if ty is None else bwd_w[ty * 256 : ty * 256 + 256, :]
+            )
 
     def channels(which, rows):
         inside = jnp.clip(which, 0, BANDS - 1)
@@ -260,7 +257,7 @@
             residue = guess[row, lane] - goal[row, lane]
             grad_pred = weight * residue
             grad_pre = grad_pred * weighted[row, lane]
-            grads[128 + aq * 64 : 192 + aq * 64, bp * 128 + 128 : bp * 128 + 256] = grad_pre.astype(BF16)
+            grads[row, lane] = grad_pre.astype(BF16)
             loss_sum = loss_sum + jnp.sum((grad_pred * residue).reshape(8, 8, 128), axis=0)
             bias_sum = bias_sum + jnp.sum(grad_pre.reshape(8, 8, 128), axis=0)
             out_sum = out_sum + jnp.sum((grad_pred * hid32[row, lane]).reshape(8, 8, 128), axis=0)
@@ -268,7 +265,7 @@
 
     def weights_stage(bp):
         lane = bp * 128
-        turned = grads[128:640, lane + 128 : lane + 256].T
+        turned = grads[:, lane : lane + 128].T
         for ty in range(3):
             part = dot(turned, pair[ty * 64 : ty * 64 + 512, lane : lane + 256])
             if bp == 0:
@@ -278,26 +275,32 @@
 
     def back_stage(bp):
         lane = bp * 128
-        part = dot(
-            jnp.concatenate(
-                [
-                    jnp.concatenate(
-                        [grads[(2 * a + t) * 64 : (2 * a + t) * 64 + 64, lane : lane + 256] for a in range(5)], axis=0
-                    )
-                    for t in range(4)
-                ],
-                axis=1,
-            ),
-            bwd_2[...],
+        left, right = max(bp - 1, 0) * 128, min(bp + 1, 8) * 128
+        rows = jnp.concatenate(
+            [
+                jnp.concatenate(
+                    [grads[(2 * a + t) * 64 : (2 * a + t) * 64 + 64, left:right] for a in range(4)], axis=0
+                )
+                for t in range(2)
+            ],
+            axis=1,
         )
+        if bp == 0:
+            both = dot(rows, jnp.concatenate([bwd_2[128:256, :], bwd_2[384:512, :]], axis=0))
+        elif bp == 8:
+            both = dot(rows, jnp.concatenate([bwd_2[0:128, :], bwd_2[256:384, :]], axis=0))
+        else:
+            both = dot(rows, bwd_2[...])
         col_sum = jnp.zeros((8, 128), F32)
         for a in range(5):
             for parity in range(2):
                 row = (2 * a + parity) * 64
-                block = (
-                    part[a * 64 : a * 64 + 64, parity * 128 : parity * 128 + 128]
-                    * slope[row : row + 64, lane : lane + 128]
-                )
+                block = 0.0
+                if a < 4:
+                    block = both[a * 64 : a * 64 + 64, 256 + parity * 128 : 384 + parity * 128]
+                if a > 0:
+                    block = block + both[a * 64 - 64 : a * 64, parity * 128 : parity * 128 + 128]
+                block = block * slope[row : row + 64, lane : lane + 128]
                 if bp == 0:
                     grad_rows[row : row + 64, :] = block
                 else:
@@ -364,10 +367,10 @@
 
 def tile_call(*operands):
     shapes = [
-        ((80, 128), F32), ((72, 128), F32), ((640, 1152), BF16), ((640, 1152), F32), ((768, 1280), BF16),
+        ((80, 128), F32), ((72, 128), F32), ((640, 1152), BF16), ((640, 1152), F32), ((512, 1024), BF16),
         ((512, 1024), F32), ((512, 1024), BF16), ((512, 1024), F32), ((512, 1024), F32), ((512, 1024), F32),
         ((640, 128), F32), ((72, 128), F32), ((128, 768), F32), ((208, 128), F32), ((208, 128), F32),
-        ((1024, 256), BF16), ((1024, 256), BF16),
+        ((1024, 256), BF16), ((512, 512), BF16),
     ]
     return pl.pallas_call(
         tile_kernel,
@@ -428,11 +431,15 @@
     bins[...] = jnp.zeros(bins.shape, F32)
     split = jnp.where(core == 0, 72, 104)
     used = row_ids((104, 128)) < split
-    for chip in range(CHIPS):
-        piece = jnp.where(used, parts[chip].astype(F32)[0:104], 0.0)
-        start = pl.multiple_of(chip // 2 * 128 + core * (chip % 2 * 128) + 56, 8)
-        bins[pl.ds(start, 104), :] += piece
-        bins[pl.ds(pl.multiple_of(start + split, 8), 104), :] += pltpu.roll(piece, 64, 1)
+    def piece(chip):
+        return parts[chip].astype(F32)[0:104] if 0 <= chip < CHIPS else 0.0
+
+    for step in range(9):
+        both = piece(2 * step) + jnp.where(core == 0, piece(2 * step + 1), piece(2 * step - 1))
+        both = jnp.where(used, both, 0.0)
+        start = step * 128 + 56
+        bins[start : start + 104, :] += both
+        bins[pl.ds(pl.multiple_of(start + split, 8), 104), :] += pltpu.roll(both, 64, 1)
 
     def own_half(x):
         return jnp.where(

time: 56.5 us -> 56.1 us (level)
  no operation moved by 1% of the time
where the time goes in v8:
time: 56.1 us; the launch traced here: 55.7 us
  blocking collectives  25.2 us (45%)
  starting transfers between devices  10.9 us (19%)
  Pallas kernels  10.3 us (18%)
  waiting for transfers between devices  6.23 us (11%)
  local copies, waits for them, and re-layouts  2.42 us (4%)
  between operations  0.7 us (1%)
    all_to_all x1, blocking collectives, body(): lax.all_to_all(joined, GROUP, 0, 0, tiled=True, axis_index_groups=same_core)  14.1 us
    all_to_all x1, blocking collectives, body(): lax.all_to_all(sums, GROUP, 0, 0, tiled=True, axis_index_groups=same_core)  11.1 us
    pallas_call x1, Pallas kernels, tile_call(): pl.pallas_call(tile_kernel, out_shape=(jax.ShapeDtypeStruct((240, 128), F...  5.97 us
    all_to_all x1, starting transfers between devices, body(): lax.all_to_all(front_call(feats, w_proj), GROUP, 0, 0, tiled=True, axis_i...  5.87 us
    all_to_all x1, waiting for transfers between devices, body(): lax.all_to_all(front_call(feats, w_proj), GROUP, 0, 0, tiled=True, axis_i...  3.09 us
    ppermute x1, starting transfers between devices, body(): lax.ppermute(every, GROUP, swap)  2.72 us
    unnamed x12, local copies, waits for them, and re-layouts  2.42 us
    pallas_call x1, Pallas kernels, front_call(): pl.pallas_call(front_kernel, out_shape=jax.ShapeDtypeStruct((8, 96, 128),...  1.9 us
  transfers between devices with their start and end apart: 5, of which 4 were waited for; matrix products, arithmetic and copies ran while one was open for 0% of the time, Pallas kernels for 1%

profile of v8, /device:TPU:1, one launch (start us, length us, event | category | flops | bytes accessed | tf_op | source)
XLA Modules:
  0.0 55.7 jit_solution(6803432932475329547)
XLA Ops:
  0.6 0.0 copy-start.5
  0.6 0.0 copy-start.4
  0.7 1.9 %front.1 = bf16[8,96,128]{2,1,0:T(8,128)(2,1)} custom-call(bf16[64,1024]{1,0:T(8,128)(2,1)} %feats_hbm.1, bf16[1024,128]{1,0:T(8,128)(2,1)} %w_proj.1), custom_call_target="tpu_custom_call" | custom-call | tf_op jit(solution)/shard_map/front/pallas_call | solution.py:57
  2.6 5.9 %all-to-all-start = ((bf16[8,96,128]{2,1,0:T(8,128)(2,1)}), bf16[8,96,128]{2,1,0:T(8,128)(2,1)S(1)}, u32[]{:S(2)}, u32[]{:S(2)}) async-start(bf16[8,96,128]{2,1,0:T(8,128)(2,1)} %front.1), calls=%async_computation | async-start | bytes 393216 | tf_op jit(solution)/shard_map/all_to_all | solution.py:582
  8.4 0.0 copy-start.1
  8.4 0.9 %copy-done.1 = bf16[576,64]{0,1:T(8,128)(2,1)S(1)} copy-done((bf16[576,64]{0,1:T(8,128)(2,1)S(1)}, bf16[576,64]{0,1:T(8,128)(2,1)}, u32[]{:S(2)}) %copy-start.1) | copy-done | bytes 73752
  9.3 0.0 copy-start.2
  9.3 0.8 %copy-done.2 = f32[64,2,64]{2,1,0:T(2,128)S(1)} copy-done((f32[64,2,64]{2,1,0:T(2,128)S(1)}, f32[64,2,64]{2,1,0:T(2,128)}, u32[]{:S(2)}) %copy-start.2) | copy-done | bytes 32792
  10.2 0.0 copy-start.3
  10.2 0.7 %copy-done.3 = s32[1024]{0:T(1024)S(1)} copy-done((s32[1024]{0:T(1024)S(1)}, s32[1024]{0:T(1024)}, u32[]{:S(2)}) %copy-start.3) | copy-done | bytes 4120
  10.9 0.6 %prepare.1 = (bf16[768,128]{1,0:T(8,128)(2,1)S(1)}, bf16[768,128]{1,0:T(8,128)(2,1)S(1)}, f32[512,1024]{1,0:T(8,128)S(1)}, f32[512,128]{1,0:T(8,128)S(1)}, f32[64,128]{1,0:T(8,128)S(1)}) custom-call(s32[8,128]{1,0:T(8,128)S(1)} %bitcast.9, f32[64,2,64]{2,1,0:T(2,128)S(1)} %copy-done.2, bf16[64,576]{1,0:T(8,128)(2,1)S(1)} %bitcast.8), custom_call_target="tpu_custom_call" | custom-call | flops 300000000 | bytes 4000000 | tf_op jit(solution)/shard_map/prepare/pallas_call | solution.py:137
  11.4 3.1 %all-to-all-done.same = bf16[8,96,128]{2,1,0:T(8,128)(2,1)S(1)} async-done(((bf16[8,96,128]{2,1,0:T(8,128)(2,1)}), bf16[8,96,128]{2,1,0:T(8,128)(2,1)S(1)}, u32[]{:S(2)}, u32[]{:S(2)}) %all-to-all-start) | async-done | bytes 196640 | tf_op jit(solution)/shard_map/all_to_all | solution.py:582
  14.5 1.8 %collective-permute-start = (bf16[8,96,128]{2,1,0:T(8,128)(2,1)S(1)}, bf16[8,96,128]{2,1,0:T(8,128)(2,1)S(1)}, u32[]{:S(2)}, u32[]{:S(2)}) collective-permute-start(bf16[8,96,128]{2,1,0:T(8,128)(2,1)S(1)} %all-to-all-done.same), channel_id=1, source_target_pairs={{0,8},{4,12},{8,0},{12,4},{16,24},{20,28},{24,16},{28,20},{32,40},... | collective-permute-start | bytes 589832 | tf_op jit(solution)/shard_map/ppermute | solution.py:585
  16.3 1.1 %collective-permute-done.other = bf16[8,96,128]{2,1,0:T(8,128)(2,1)S(1)} collective-permute-done((bf16[8,96,128]{2,1,0:T(8,128)(2,1)S(1)}, bf16[8,96,128]{2,1,0:T(8,128)(2,1)S(1)}, u32[]{:S(2)}, u32[]{:S(2)}) %collective-permute-start) | collective-permute-done | bytes 196640 | tf_op jit(solution)/shard_map/ppermute | solution.py:585
  17.4 0.0 copy-done.5
  17.4 0.0 copy-done.4
  17.4 6.0 %tiles.1 = (f32[240,128]{1,0:T(8,128)S(1)}, bf16[240,128]{1,0:T(8,128)(2,1)S(1)}) custom-call(bf16[8,96,128]{2,1,0:T(8,128)(2,1)S(1)} %all-to-all-done.same, bf16[8,96,128]{2,1,0:T(8,128)(2,1)S(1)} %collective-permute-done.other, f32[1,64]{1,0:T(1,128)S(1)} %bitcast.10, f32[1,64]{1,0:T(1,128)S(1)} %bitcast.11, bf16[768,128]{1,0:T(8,128)(2,1)S(1)} %get-tuple-element.36.fwd_w, ...), custom_call_target="tpu_custom_call" | custom-call | flops 2000000000 | bytes 1000000 | tf_op jit(solution)/shard_map/tiles/pallas_call | solution.py:375
  23.4 0.0 copy-start
  23.4 0.5 collective-permute-start.1
  23.8 0.9 %collective-permute-done.1.received = bf16[240,128]{1,0:T(8,128)(2,1)S(1)} collective-permute-done((bf16[240,128]{1,0:T(8,128)(2,1)S(1)}, bf16[240,128]{1,0:T(8,128)(2,1)S(1)}, u32[]{:S(2)}, u32[]{:S(2)}) %collective-permute-start.1) | collective-permute-done | bytes 61472 | tf_op jit(solution)/shard_map/ppermute | solution.py:587
  24.8 14.1 %all_to_all.15.parts = bf16[16,112,128]{2,1,0:T(8,128)(2,1)S(1)} all-to-all(bf16[16,112,128]{2,1,0:T(8,128)(2,1)S(1)} %join.1), channel_id=1, replica_groups={{0,4,16,20,32,36,48,52,64,68,80,84,96,100,112,116},{8,12,24,28,40,44,56..., dimensions={0} | all-to-all | bytes 917504 | tf_op jit(solution)/shard_map/all_to_all | solution.py:588
  38.9 0.7 %sums.1 = (bf16[16,48,128]{2,1,0:T(8,128)(2,1)S(1)}, bf16[32,128]{1,0:T(8,128)(2,1)S(1)}, bf16[32,128]{1,0:T(8,128)(2,1)S(1)}) custom-call(bf16[16,112,128]{2,1,0:T(8,128)(2,1)S(1)} %all_to_all.15.parts, bf16[8,96,128]{2,1,0:T(8,128)(2,1)S(1)} %all-to-all-done.same, bf16[8,96,128]{2,1,0:T(8,128)(2,1)S(1)} %collective-permute-done.other), custom_call_target="tpu_custom_call" | custom-call | tf_op jit(solution)/shard_map/sums/pallas_call | solution.py:487
  39.6 11.1 %all_to_all.16.same = bf16[16,48,128]{2,1,0:T(8,128)(2,1)S(1)} all-to-all(bf16[16,48,128]{2,1,0:T(8,128)(2,1)S(1)} %get-tuple-element.43), channel_id=1, replica_groups={{0,4,16,20,32,36,48,52,64,68,80,84,96,100,112,116},{8,12,24,28,40,44,56..., dimensions={0} | all-to-all | bytes 393216 | tf_op jit(solution)/shard_map/all_to_all | solution.py:590
  50.7 2.7 %collective-permute-start.2 = (bf16[16,48,128]{2,1,0:T(8,128)(2,1)S(1)}, bf16[16,48,128]{2,1,0:T(8,128)(2,1)S(1)}, u32[]{:S(2)}, u32[]{:S(2)}) collective-permute-start(bf16[16,48,128]{2,1,0:T(8,128)(2,1)S(1)} %all_to_all.16.same), channel_id=1, source_target_pairs={{0,8},{4,12},{8,0},{12,4},{16,24},{20,28},{24,16},{28,20},{32,40},... | collective-permute-start | bytes 589832 | tf_op jit(solution)/shard_map/ppermute | solution.py:593
  53.4 0.0 collective-permute-start.3
  53.5 1.2 %collective-permute-done.3.received = bf16[32,128]{1,0:T(8,128)(2,1)S(1)} collective-permute-done((bf16[32,128]{1,0:T(8,128)(2,1)S(1)}, bf16[32,128]{1,0:T(8,128)(2,1)S(1)}, u32[]{:S(2)}, u32[]{:S(2)}) %collective-permute-start.3) | collective-permute-done | bytes 8224 | tf_op jit(solution)/shard_map/ppermute | solution.py:593
  54.6 0.0 collective-permute-done.2.other
  54.6 0.0 copy-done
  54.6 1.1 %outputs.1 = (f32[1024,128]{1,0:T(8,128)}, f32[64,576]{1,0:T(8,128)}, bf16[32,1024]{1,0:T(8,128)(2,1)}, f32[1,64]{1,0:T(1,128)}, f32[1,64]{1,0:T(1,128)}, /*index=5*/f32[1,1]{1,0:T(1,128)}) custom-call(bf16[16,48,128]{2,1,0:T(8,128)(2,1)S(1)} %all_to_all.16.same, bf16[16,48,128]{2,1,0:T(8,128)(2,1)S(1)} %collective-permute-done.2.other, ...), custom_call_target="tpu_custom_call" | custom-call | tf_op jit(solution)/shard_map/outputs/pallas_call | solution.py:552
  (1 shorter events, 0.0 us)
Async XLA Ops:
  0.6 16.8 %copy-start.5 = (f32[64]{0:T(128)S(1)}, f32[64]{0:T(128)}, u32[]{:S(2)}) copy-start(f32[64]{0:T(128)} %param.11) | copy-start | bytes 772
  0.6 16.8 %copy-start.4 = (f32[64]{0:T(128)S(1)}, f32[64]{0:T(128)}, u32[]{:S(2)}) copy-start(f32[64]{0:T(128)} %param.10) | copy-start | bytes 772
  2.6 12.0 %all-to-all-start = ((bf16[8,96,128]{2,1,0:T(8,128)(2,1)}), bf16[8,96,128]{2,1,0:T(8,128)(2,1)S(1)}, u32[]{:S(2)}, u32[]{:S(2)}) async-start(bf16[8,96,128]{2,1,0:T(8,128)(2,1)} %front.1), calls=%async_computation | async-start | bytes 393216 | tf_op jit(solution)/shard_map/all_to_all | solution.py:582
  8.4 0.9 %copy-start.1 = (bf16[576,64]{0,1:T(8,128)(2,1)S(1)}, bf16[576,64]{0,1:T(8,128)(2,1)}, u32[]{:S(2)}) copy-start(bf16[576,64]{0,1:T(8,128)(2,1)} %param.9) | copy-start | bytes 221188
  9.3 0.8 %copy-start.2 = (f32[64,2,64]{2,1,0:T(2,128)S(1)}, f32[64,2,64]{2,1,0:T(2,128)}, u32[]{:S(2)}) copy-start(f32[64,2,64]{2,1,0:T(2,128)} %target.1) | copy-start | bytes 98308
  10.2 0.7 %copy-start.3 = (s32[1024]{0:T(1024)S(1)}, s32[1024]{0:T(1024)}, u32[]{:S(2)}) copy-start(s32[1024]{0:T(1024)} %param.13) | copy-start | bytes 12292
  14.5 2.9 %collective-permute-start = (bf16[8,96,128]{2,1,0:T(8,128)(2,1)S(1)}, bf16[8,96,128]{2,1,0:T(8,128)(2,1)S(1)}, u32[]{:S(2)}, u32[]{:S(2)}) collective-permute-start(bf16[8,96,128]{2,1,0:T(8,128)(2,1)S(1)} %all-to-all-done.same), channel_id=1, source_target_pairs={{0,8},{4,12},{8,0},{12,4},{16,24},{20,28},{24,16},{28,20},{32,40},... | collective-permute-start | bytes 589832 | tf_op jit(solution)/shard_map/ppermute | solution.py:585
  23.4 31.2 %copy-start = (bf16[1024,128]{1,0:T(8,128)(2,1)S(1)}, bf16[1024,128]{1,0:T(8,128)(2,1)}, u32[]{:S(2)}) copy-start(bf16[1024,128]{1,0:T(8,128)(2,1)} %w_proj.1) | copy-start | bytes 786436
  23.4 1.3 %collective-permute-start.1 = (bf16[240,128]{1,0:T(8,128)(2,1)S(1)}, bf16[240,128]{1,0:T(8,128)(2,1)S(1)}, u32[]{:S(2)}, u32[]{:S(2)}) collective-permute-start(bf16[240,128]{1,0:T(8,128)(2,1)S(1)} %get-tuple-element.42), channel_id=1, source_target_pairs={{0,8},{4,12},{8,0},{12,4},{16,24},{20,28},{24,16},{28,20},{32,40},... | collective-permute-start | bytes 184328 | tf_op jit(solution)/shard_map/ppermute | solution.py:587
  50.7 3.9 %collective-permute-start.2 = (bf16[16,48,128]{2,1,0:T(8,128)(2,1)S(1)}, bf16[16,48,128]{2,1,0:T(8,128)(2,1)S(1)}, u32[]{:S(2)}, u32[]{:S(2)}) collective-permute-start(bf16[16,48,128]{2,1,0:T(8,128)(2,1)S(1)} %all_to_all.16.same), channel_id=1, source_target_pairs={{0,8},{4,12},{8,0},{12,4},{16,24},{20,28},{24,16},{28,20},{32,40},... | collective-permute-start | bytes 589832 | tf_op jit(solution)/shard_map/ppermute | solution.py:593
  53.4 1.2 %collective-permute-start.3 = (bf16[32,128]{1,0:T(8,128)(2,1)S(1)}, bf16[32,128]{1,0:T(8,128)(2,1)S(1)}, u32[]{:S(2)}, u32[]{:S(2)}) collective-permute-start(bf16[32,128]{1,0:T(8,128)(2,1)S(1)} %get-tuple-element.47), channel_id=1, source_target_pairs={{0,8},{4,12},{8,0},{12,4},{16,24},{20,28},{24,16},{28,20},{32,40},... | collective-permute-start | bytes 24584 | tf_op jit(solution)/shard_map/ppermute | solution.py:593

commit v9 on v8

--- a/solution.py
+++ b/solution.py
@@ -199,7 +199,6 @@
     halves = ((row_ids((128, 128)) < 64) == (lane_ids((128, 128)) < 64)).astype(F32).astype(BF16)
 
     def pair_stage(bp):
-        lane = slice(bp * 128, bp * 128 + 128)
         block = first * 8 - 1 + 2 * bp
         spot = jnp.where(half_lane, block, block + 1)
         col_in = jnp.where((spot >= 0) & (spot < 128), 0.5, 0.0)
@@ -212,18 +211,18 @@
                 half = jnp.where(band == BANDS - 1, 0.0, col_in)
             x = (rows_u[aq * 8 : aq * 8 + 8, :][:, None, :] + v_here).reshape(64, 128)
             value, grade = gelu_parts(x, half)
-            pair[aq * 64 : aq * 64 + 64, lane] = value.astype(BF16)
-            slope[aq * 64 : aq * 64 + 64, lane] = grade
+            pair[bp][aq * 64 : aq * 64 + 64, :] = value.astype(BF16)
+            slope[bp][aq * 64 : aq * 64 + 64, :] = grade
 
     def conv_stage(bp):
-        lane = bp * 128
         part = dot(
             jnp.concatenate(
                 [
                     jnp.concatenate(
-                        [pair[(2 * a + t) * 64 : (2 * a + t) * 64 + 64, lane : lane + 256] for a in range(4)], axis=0
+                        [held[(2 * a + t) * 64 : (2 * a + t) * 64 + 64, :] for a in range(4)], axis=0
                     )
                     for t in range(4)
+                    for held in (pair[bp], pair[bp + 1])
                 ],
                 axis=1,
             ),
@@ -232,20 +231,18 @@
         for a in range(4):
             for parity in range(2):
                 row = (2 * a + parity) * 64
-                pre[row : row + 64, lane : lane + 128] = part[a * 64 : a * 64 + 64, parity * 128 : parity * 128 + 128]
+                pre[bp][row : row + 64, :] = part[a * 64 : a * 64 + 64, parity * 128 : parity * 128 + 128]
 
     def act_stage(bp):
-        lane = slice(bp * 128, bp * 128 + 128)
         for aq in range(8):
             row = slice(aq * 64, aq * 64 + 64)
-            value, grade = gelu_parts(pre[row, lane] + bias2, 0.5)
-            hid32[row, lane] = value
-            hid16[row, lane] = (value * out_w2).astype(BF16)
-            weighted[row, lane] = grade * out_w2
+            value, grade = gelu_parts(pre[bp][row, :] + bias2, 0.5)
+            hid32[bp][row, :] = value
+            hid16[bp][row, :] = (value * out_w2).astype(BF16)
+            weighted[bp][row, :] = grade * out_w2
 
     def pred_stage(bp):
-        lane = slice(bp * 128, bp * 128 + 128)
-        guess[:, lane] = dot(hid16[:, lane], halves)
+        guess[bp][...] = dot(hid16[bp][...], halves)
 
     def loss_stage(bp, sums):
         loss_sum, bias_sum, out_sum = sums
@@ -254,34 +251,34 @@
         for aq in range(8):
             row = slice(aq * 64, aq * 64 + 64)
             weight = (row_mask[row, :].reshape(8, 8, 128) * col_weight).reshape(64, 128)
-            residue = guess[row, lane] - goal[row, lane]
+            residue = guess[bp][row, :] - goal[row, lane]
             grad_pred = weight * residue
-            grad_pre = grad_pred * weighted[row, lane]
-            grads[row, lane] = grad_pre.astype(BF16)
+            grad_pre = grad_pred * weighted[bp][row, :]
+            grads[bp][row, :] = grad_pre.astype(BF16)
             loss_sum = loss_sum + jnp.sum((grad_pred * residue).reshape(8, 8, 128), axis=0)
             bias_sum = bias_sum + jnp.sum(grad_pre.reshape(8, 8, 128), axis=0)
-            out_sum = out_sum + jnp.sum((grad_pred * hid32[row, lane]).reshape(8, 8, 128), axis=0)
+            out_sum = out_sum + jnp.sum((grad_pred * hid32[bp][row, :]).reshape(8, 8, 128), axis=0)
         return loss_sum, bias_sum, out_sum
 
     def weights_stage(bp):
-        lane = bp * 128
-        turned = grads[:, lane : lane + 128].T
+        turned = grads[bp][...].T
         for ty in range(3):
-            part = dot(turned, pair[ty * 64 : ty * 64 + 512, lane : lane + 256])
+            rows = slice(ty * 64, ty * 64 + 512)
+            part = dot(turned, jnp.concatenate([pair[bp][rows, :], pair[bp + 1][rows, :]], axis=1))
             if bp == 0:
                 grad_w[:, ty * 256 : ty * 256 + 256] = part
             else:
                 grad_w[:, ty * 256 : ty * 256 + 256] += part
 
     def back_stage(bp):
-        lane = bp * 128
-        left, right = max(bp - 1, 0) * 128, min(bp + 1, 8) * 128
+        reach = [grads[k] for k in (bp - 1, bp) if 0 <= k < 8]
         rows = jnp.concatenate(
             [
                 jnp.concatenate(
-                    [grads[(2 * a + t) * 64 : (2 * a + t) * 64 + 64, left:right] for a in range(4)], axis=0
+                    [held[(2 * a + t) * 64 : (2 * a + t) * 64 + 64, :] for a in range(4)], axis=0
                 )
                 for t in range(2)
+                for held in reach
             ],
             axis=1,
         )
@@ -300,7 +297,7 @@
                     block = both[a * 64 : a * 64 + 64, 256 + parity * 128 : 384 + parity * 128]
                 if a > 0:
                     block = block + both[a * 64 - 64 : a * 64, parity * 128 : parity * 128 + 128]
-                block = block * slope[row : row + 64, lane : lane + 128]
+                block = block * slope[bp][row : row + 64, :]
                 if bp == 0:
                     grad_rows[row : row + 64, :] = block
                 else:
@@ -311,18 +308,18 @@
     zero8 = jnp.zeros((8, 128), F32)
     totals = (zero8, zero8, zero8)
     for step in range(15):
+        if 6 <= step:
+            back_stage(step - 6)
         if step < 9:
             pair_stage(step)
+        if 6 <= step < 14:
+            weights_stage(step - 6)
+        if 3 <= step < 11:
+            act_stage(step - 3)
         if 2 <= step < 10:
             conv_stage(step - 2)
-        if 3 <= step < 11:
-            act_stage(step - 3)
-        if 6 <= step:
-            back_stage(step - 6)
         if 5 <= step < 13:
             totals = loss_stage(step - 5, totals)
-        if 6 <= step < 14:
-            weights_stage(step - 6)
         if 4 <= step < 12:
             pred_stage(step - 4)
 
@@ -367,8 +364,9 @@
 
 def tile_call(*operands):
     shapes = [
-        ((80, 128), F32), ((72, 128), F32), ((640, 1152), BF16), ((640, 1152), F32), ((512, 1024), BF16),
-        ((512, 1024), F32), ((512, 1024), BF16), ((512, 1024), F32), ((512, 1024), F32), ((512, 1024), F32),
+        ((80, 128), F32), ((72, 128), F32), [((640, 128), BF16)] * 9, [((640, 128), F32)] * 9,
+        [((512, 128), BF16)] * 8, [((512, 128), F32)] * 8, [((512, 128), BF16)] * 8, [((512, 128), F32)] * 8,
+        [((512, 128), F32)] * 8, [((512, 128), F32)] * 8,
         ((640, 128), F32), ((72, 128), F32), ((128, 768), F32), ((208, 128), F32), ((208, 128), F32),
         ((1024, 256), BF16), ((512, 512), BF16),
     ]
@@ -377,7 +375,10 @@
         out_shape=(jax.ShapeDtypeStruct((240, 128), F32), jax.ShapeDtypeStruct((240, 128), BF16)),
         in_specs=[pl.BlockSpec(memory_space=pltpu.VMEM)] * len(operands),
         out_specs=(pl.BlockSpec(memory_space=pltpu.VMEM),) * 2,
-        scratch_shapes=[pltpu.VMEM(shape, kind) for shape, kind in shapes],
+        scratch_shapes=[
+            [pltpu.VMEM(*one) for one in entry] if isinstance(entry, list) else pltpu.VMEM(*entry)
+            for entry in shapes
+        ],
         compiler_params=pltpu.CompilerParams(vmem_limit_bytes=40 * 2**20),
         cost_estimate=pl.CostEstimate(flops=2 * 10**9, bytes_accessed=10**6, transcendentals=10**6),
         name="tiles",

time: 56.1 us -> 55.6 us (level)
  no operation moved by 1% of the time
where the time goes in v9:
time: 55.6 us; the launch traced here: 55.2 us
  blocking collectives  25.2 us (45%)
  starting transfers between devices  10.9 us (20%)
  Pallas kernels  9.79 us (18%)
  waiting for transfers between devices  6.23 us (11%)
  local copies, waits for them, and re-layouts  2.42 us (4%)
  between operations  0.69 us (1%)
    all_to_all x1, blocking collectives, body(): lax.all_to_all(joined, GROUP, 0, 0, tiled=True, axis_index_groups=same_core)  14.1 us
    all_to_all x1, blocking collectives, body(): lax.all_to_all(sums, GROUP, 0, 0, tiled=True, axis_index_groups=same_core)  11.1 us
    all_to_all x1, starting transfers between devices, body(): lax.all_to_all(front_call(feats, w_proj), GROUP, 0, 0, tiled=True, axis_i...  5.87 us
    pallas_call x1, Pallas kernels, tile_call(): pl.pallas_call(tile_kernel, out_shape=(jax.ShapeDtypeStruct((240, 128), F...  5.48 us
    all_to_all x1, waiting for transfers between devices, body(): lax.all_to_all(front_call(feats, w_proj), GROUP, 0, 0, tiled=True, axis_i...  3.09 us
    ppermute x1, starting transfers between devices, body(): lax.ppermute(every, GROUP, swap)  2.72 us
    unnamed x12, local copies, waits for them, and re-layouts  2.42 us
    pallas_call x1, Pallas kernels, front_call(): pl.pallas_call(front_kernel, out_shape=jax.ShapeDtypeStruct((8, 96, 128),...  1.9 us
  transfers between devices with their start and end apart: 5, of which 4 were waited for; matrix products, arithmetic and copies ran while one was open for 0% of the time, Pallas kernels for 1%

profile of v9, /device:TPU:1, one launch (start us, length us, event | category | flops | bytes accessed | tf_op | source)
XLA Modules:
  0.0 55.2 jit_solution(15061135254208190688)
XLA Ops:
  0.6 0.0 copy-start.5
  0.6 0.0 copy-start.4
  0.7 1.9 %front.1 = bf16[8,96,128]{2,1,0:T(8,128)(2,1)} custom-call(bf16[64,1024]{1,0:T(8,128)(2,1)} %feats_hbm.1, bf16[1024,128]{1,0:T(8,128)(2,1)} %w_proj.1), custom_call_target="tpu_custom_call" | custom-call | tf_op jit(solution)/shard_map/front/pallas_call | solution.py:57
  2.6 5.9 %all-to-all-start = ((bf16[8,96,128]{2,1,0:T(8,128)(2,1)}), bf16[8,96,128]{2,1,0:T(8,128)(2,1)S(1)}, u32[]{:S(2)}, u32[]{:S(2)}) async-start(bf16[8,96,128]{2,1,0:T(8,128)(2,1)} %front.1), calls=%async_computation | async-start | bytes 393216 | tf_op jit(solution)/shard_map/all_to_all | solution.py:583
  8.4 0.0 copy-start.1
  8.4 0.9 %copy-done.1 = bf16[576,64]{0,1:T(8,128)(2,1)S(1)} copy-done((bf16[576,64]{0,1:T(8,128)(2,1)S(1)}, bf16[576,64]{0,1:T(8,128)(2,1)}, u32[]{:S(2)}) %copy-start.1) | copy-done | bytes 73752
  9.3 0.0 copy-start.2
  9.3 0.8 %copy-done.2 = f32[64,2,64]{2,1,0:T(2,128)S(1)} copy-done((f32[64,2,64]{2,1,0:T(2,128)S(1)}, f32[64,2,64]{2,1,0:T(2,128)}, u32[]{:S(2)}) %copy-start.2) | copy-done | bytes 32792
  10.2 0.0 copy-start.3
  10.2 0.7 %copy-done.3 = s32[1024]{0:T(1024)S(1)} copy-done((s32[1024]{0:T(1024)S(1)}, s32[1024]{0:T(1024)}, u32[]{:S(2)}) %copy-start.3) | copy-done | bytes 4120
  10.9 0.6 %prepare.1 = (bf16[768,128]{1,0:T(8,128)(2,1)S(1)}, bf16[768,128]{1,0:T(8,128)(2,1)S(1)}, f32[512,1024]{1,0:T(8,128)S(1)}, f32[512,128]{1,0:T(8,128)S(1)}, f32[64,128]{1,0:T(8,128)S(1)}) custom-call(s32[8,128]{1,0:T(8,128)S(1)} %bitcast.9, f32[64,2,64]{2,1,0:T(2,128)S(1)} %copy-done.2, bf16[64,576]{1,0:T(8,128)(2,1)S(1)} %bitcast.8), custom_call_target="tpu_custom_call" | custom-call | flops 300000000 | bytes 4000000 | tf_op jit(solution)/shard_map/prepare/pallas_call | solution.py:137
  11.4 3.1 %all-to-all-done.same = bf16[8,96,128]{2,1,0:T(8,128)(2,1)S(1)} async-done(((bf16[8,96,128]{2,1,0:T(8,128)(2,1)}), bf16[8,96,128]{2,1,0:T(8,128)(2,1)S(1)}, u32[]{:S(2)}, u32[]{:S(2)}) %all-to-all-start) | async-done | bytes 196640 | tf_op jit(solution)/shard_map/all_to_all | solution.py:583
  14.5 1.8 %collective-permute-start = (bf16[8,96,128]{2,1,0:T(8,128)(2,1)S(1)}, bf16[8,96,128]{2,1,0:T(8,128)(2,1)S(1)}, u32[]{:S(2)}, u32[]{:S(2)}) collective-permute-start(bf16[8,96,128]{2,1,0:T(8,128)(2,1)S(1)} %all-to-all-done.same), channel_id=1, source_target_pairs={{0,8},{4,12},{8,0},{12,4},{16,24},{20,28},{24,16},{28,20},{32,40},... | collective-permute-start | bytes 589832 | tf_op jit(solution)/shard_map/ppermute | solution.py:586
  16.3 1.1 %collective-permute-done.other = bf16[8,96,128]{2,1,0:T(8,128)(2,1)S(1)} collective-permute-done((bf16[8,96,128]{2,1,0:T(8,128)(2,1)S(1)}, bf16[8,96,128]{2,1,0:T(8,128)(2,1)S(1)}, u32[]{:S(2)}, u32[]{:S(2)}) %collective-permute-start) | collective-permute-done | bytes 196640 | tf_op jit(solution)/shard_map/ppermute | solution.py:586
  17.4 0.0 copy-done.5
  17.4 0.0 copy-done.4
  17.4 5.5 %tiles.1 = (f32[240,128]{1,0:T(8,128)S(1)}, bf16[240,128]{1,0:T(8,128)(2,1)S(1)}) custom-call(bf16[8,96,128]{2,1,0:T(8,128)(2,1)S(1)} %all-to-all-done.same, bf16[8,96,128]{2,1,0:T(8,128)(2,1)S(1)} %collective-permute-done.other, f32[1,64]{1,0:T(1,128)S(1)} %bitcast.10, f32[1,64]{1,0:T(1,128)S(1)} %bitcast.11, bf16[768,128]{1,0:T(8,128)(2,1)S(1)} %get-tuple-element.36.fwd_w, ...), custom_call_target="tpu_custom_call" | custom-call | flops 2000000000 | bytes 1000000 | tf_op jit(solution)/shard_map/tiles/pallas_call | solution.py:373
  22.9 0.0 copy-start
  22.9 0.5 collective-permute-start.1
  23.4 0.9 %collective-permute-done.1.received = bf16[240,128]{1,0:T(8,128)(2,1)S(1)} collective-permute-done((bf16[240,128]{1,0:T(8,128)(2,1)S(1)}, bf16[240,128]{1,0:T(8,128)(2,1)S(1)}, u32[]{:S(2)}, u32[]{:S(2)}) %collective-permute-start.1) | collective-permute-done | bytes 61472 | tf_op jit(solution)/shard_map/ppermute | solution.py:588
  24.3 14.1 %all_to_all.15.parts = bf16[16,112,128]{2,1,0:T(8,128)(2,1)S(1)} all-to-all(bf16[16,112,128]{2,1,0:T(8,128)(2,1)S(1)} %join.1), channel_id=1, replica_groups={{0,4,16,20,32,36,48,52,64,68,80,84,96,100,112,116},{8,12,24,28,40,44,56..., dimensions={0} | all-to-all | bytes 917504 | tf_op jit(solution)/shard_map/all_to_all | solution.py:589
  38.4 0.7 %sums.1 = (bf16[16,48,128]{2,1,0:T(8,128)(2,1)S(1)}, bf16[32,128]{1,0:T(8,128)(2,1)S(1)}, bf16[32,128]{1,0:T(8,128)(2,1)S(1)}) custom-call(bf16[16,112,128]{2,1,0:T(8,128)(2,1)S(1)} %all_to_all.15.parts, bf16[8,96,128]{2,1,0:T(8,128)(2,1)S(1)} %all-to-all-done.same, bf16[8,96,128]{2,1,0:T(8,128)(2,1)S(1)} %collective-permute-done.other), custom_call_target="tpu_custom_call" | custom-call | tf_op jit(solution)/shard_map/sums/pallas_call | solution.py:488
  39.2 11.1 %all_to_all.16.same = bf16[16,48,128]{2,1,0:T(8,128)(2,1)S(1)} all-to-all(bf16[16,48,128]{2,1,0:T(8,128)(2,1)S(1)} %get-tuple-element.43), channel_id=1, replica_groups={{0,4,16,20,32,36,48,52,64,68,80,84,96,100,112,116},{8,12,24,28,40,44,56..., dimensions={0} | all-to-all | bytes 393216 | tf_op jit(solution)/shard_map/all_to_all | solution.py:591
  50.2 2.7 %collective-permute-start.2 = (bf16[16,48,128]{2,1,0:T(8,128)(2,1)S(1)}, bf16[16,48,128]{2,1,0:T(8,128)(2,1)S(1)}, u32[]{:S(2)}, u32[]{:S(2)}) collective-permute-start(bf16[16,48,128]{2,1,0:T(8,128)(2,1)S(1)} %all_to_all.16.same), channel_id=1, source_target_pairs={{0,8},{4,12},{8,0},{12,4},{16,24},{20,28},{24,16},{28,20},{32,40},... | collective-permute-start | bytes 589832 | tf_op jit(solution)/shard_map/ppermute | solution.py:594
  53.0 0.0 collective-permute-start.3
  53.0 1.2 %collective-permute-done.3.received = bf16[32,128]{1,0:T(8,128)(2,1)S(1)} collective-permute-done((bf16[32,128]{1,0:T(8,128)(2,1)S(1)}, bf16[32,128]{1,0:T(8,128)(2,1)S(1)}, u32[]{:S(2)}, u32[]{:S(2)}) %collective-permute-start.3) | collective-permute-done | bytes 8224 | tf_op jit(solution)/shard_map/ppermute | solution.py:594
  54.1 0.0 collective-permute-done.2.other
  54.1 0.0 copy-done
  54.1 1.1 %outputs.1 = (f32[1024,128]{1,0:T(8,128)}, f32[64,576]{1,0:T(8,128)}, bf16[32,1024]{1,0:T(8,128)(2,1)}, f32[1,64]{1,0:T(1,128)}, f32[1,64]{1,0:T(1,128)}, /*index=5*/f32[1,1]{1,0:T(1,128)}) custom-call(bf16[16,48,128]{2,1,0:T(8,128)(2,1)S(1)} %all_to_all.16.same, bf16[16,48,128]{2,1,0:T(8,128)(2,1)S(1)} %collective-permute-done.2.other, ...), custom_call_target="tpu_custom_call" | custom-call | tf_op jit(solution)/shard_map/outputs/pallas_call | solution.py:553
  (1 shorter events, 0.0 us)
Async XLA Ops:
  0.6 16.8 %copy-start.5 = (f32[64]{0:T(128)S(1)}, f32[64]{0:T(128)}, u32[]{:S(2)}) copy-start(f32[64]{0:T(128)} %param.11) | copy-start | bytes 772
  0.6 16.8 %copy-start.4 = (f32[64]{0:T(128)S(1)}, f32[64]{0:T(128)}, u32[]{:S(2)}) copy-start(f32[64]{0:T(128)} %param.10) | copy-start | bytes 772
  2.6 12.0 %all-to-all-start = ((bf16[8,96,128]{2,1,0:T(8,128)(2,1)}), bf16[8,96,128]{2,1,0:T(8,128)(2,1)S(1)}, u32[]{:S(2)}, u32[]{:S(2)}) async-start(bf16[8,96,128]{2,1,0:T(8,128)(2,1)} %front.1), calls=%async_computation | async-start | bytes 393216 | tf_op jit(solution)/shard_map/all_to_all | solution.py:583
  8.4 0.9 %copy-start.1 = (bf16[576,64]{0,1:T(8,128)(2,1)S(1)}, bf16[576,64]{0,1:T(8,128)(2,1)}, u32[]{:S(2)}) copy-start(bf16[576,64]{0,1:T(8,128)(2,1)} %param.9) | copy-start | bytes 221188
  9.3 0.8 %copy-start.2 = (f32[64,2,64]{2,1,0:T(2,128)S(1)}, f32[64,2,64]{2,1,0:T(2,128)}, u32[]{:S(2)}) copy-start(f32[64,2,64]{2,1,0:T(2,128)} %target.1) | copy-start | bytes 98308
  10.2 0.7 %copy-start.3 = (s32[1024]{0:T(1024)S(1)}, s32[1024]{0:T(1024)}, u32[]{:S(2)}) copy-start(s32[1024]{0:T(1024)} %param.13) | copy-start | bytes 12292
  14.5 2.9 %collective-permute-start = (bf16[8,96,128]{2,1,0:T(8,128)(2,1)S(1)}, bf16[8,96,128]{2,1,0:T(8,128)(2,1)S(1)}, u32[]{:S(2)}, u32[]{:S(2)}) collective-permute-start(bf16[8,96,128]{2,1,0:T(8,128)(2,1)S(1)} %all-to-all-done.same), channel_id=1, source_target_pairs={{0,8},{4,12},{8,0},{12,4},{16,24},{20,28},{24,16},{28,20},{32,40},... | collective-permute-start | bytes 589832 | tf_op jit(solution)/shard_map/ppermute | solution.py:586
  22.9 31.3 %copy-start = (bf16[1024,128]{1,0:T(8,128)(2,1)S(1)}, bf16[1024,128]{1,0:T(8,128)(2,1)}, u32[]{:S(2)}) copy-start(bf16[1024,128]{1,0:T(8,128)(2,1)} %w_proj.1) | copy-start | bytes 786436
  22.9 1.4 %collective-permute-start.1 = (bf16[240,128]{1,0:T(8,128)(2,1)S(1)}, bf16[240,128]{1,0:T(8,128)(2,1)S(1)}, u32[]{:S(2)}, u32[]{:S(2)}) collective-permute-start(bf16[240,128]{1,0:T(8,128)(2,1)S(1)} %get-tuple-element.42), channel_id=1, source_target_pairs={{0,8},{4,12},{8,0},{12,4},{16,24},{20,28},{24,16},{28,20},{32,40},... | collective-permute-start | bytes 184328 | tf_op jit(solution)/shard_map/ppermute | solution.py:588
  50.2 3.9 %collective-permute-start.2 = (bf16[16,48,128]{2,1,0:T(8,128)(2,1)S(1)}, bf16[16,48,128]{2,1,0:T(8,128)(2,1)S(1)}, u32[]{:S(2)}, u32[]{:S(2)}) collective-permute-start(bf16[16,48,128]{2,1,0:T(8,128)(2,1)S(1)} %all_to_all.16.same), channel_id=1, source_target_pairs={{0,8},{4,12},{8,0},{12,4},{16,24},{20,28},{24,16},{28,20},{32,40},... | collective-permute-start | bytes 589832 | tf_op jit(solution)/shard_map/ppermute | solution.py:594
  53.0 1.2 %collective-permute-start.3 = (bf16[32,128]{1,0:T(8,128)(2,1)S(1)}, bf16[32,128]{1,0:T(8,128)(2,1)S(1)}, u32[]{:S(2)}, u32[]{:S(2)}) collective-permute-start(bf16[32,128]{1,0:T(8,128)(2,1)S(1)} %get-tuple-element.47), channel_id=1, source_target_pairs={{0,8},{4,12},{8,0},{12,4},{16,24},{20,28},{24,16},{28,20},{32,40},... | collective-permute-start | bytes 24584 | tf_op jit(solution)/shard_map/ppermute | solution.py:594

commit v10 on v9

--- a/solution.py
+++ b/solution.py
@@ -41,6 +41,8 @@
     get_feats.start()
     get_w.start()
     get_feats.wait()
+    get_w.wait()
+    proj = dot(feats[...], w_proj[...]).astype(BF16)
     half_lane = lane_ids((1, 128)) < 64
     for q in range(8):
         block = feats[:, q * 128 : q * 128 + 128].astype(F32)
@@ -48,8 +50,6 @@
         low = jnp.where(half_lane, top, pltpu.roll(bottom, 64, 1))
         high = jnp.where(half_lane, pltpu.roll(top, 64, 1), bottom)
         out[q, 64:96, :] = jnp.where(off == 0, low, high).astype(BF16)
-    get_w.wait()
-    proj = dot(feats[...], w_proj[...]).astype(BF16)
     out[:, 0:64, :] = jnp.broadcast_to(proj[None], (8, 64, 128))
 
 
@@ -509,8 +509,8 @@
     half_lane = lane_ids((1, 128)) < 64
     firsts, seconds = [], []
     puts = []
-    for k in range(4):
-        for chip in range(4 * k, 4 * k + 4):
+    for k in range(1):
+        for chip in range(16 * k, 16 * k + 16):
             here = same[chip].astype(F32)
             there = other[chip].astype(F32)
             left = jnp.where(is_first, here, there)
@@ -521,7 +521,7 @@
             row = chip * 64
             grad_proj[row : row + 32, :] = jnp.where(half_lane, left, pltpu.roll(right, 64, 1))
             grad_proj[row + 32 : row + 64, :] = jnp.where(half_lane, pltpu.roll(left, 64, 1), right)
-        rows = pl.ds(k * 256, 256)
+        rows = pl.ds(k * 1024, 1024)
         puts.append(pltpu.make_async_copy(grad_proj.at[rows], grad_proj_hbm.at[rows], sems.at[k]))
         puts[k].start()
     wide = jnp.concatenate(seconds + [first[0:8] for first in firsts], axis=0)
@@ -531,14 +531,14 @@
     grad_conv_t[0:32, 512:576] = last[:, 0:64]
     grad_conv_t[32:64, 512:576] = last[:, 64:128]
     puts.append(pltpu.make_async_copy(grad_conv_t, grad_conv_hbm, sems.at[4]))
-    puts[4].start()
+    puts[1].start()
     small = firsts[0][10:11] + firsts[0][11:12]
     bias[...] = small[:, 0:64]
     w_out[...] = small[:, 64:128]
     loss[...] = (firsts[0][12:13] + firsts[0][13:14])[:, 0:1]
     for k, (held, result) in enumerate(((bias, bias_hbm), (w_out, w_out_hbm), (loss, loss_hbm))):
         puts.append(pltpu.make_async_copy(held, result, sems.at[6 + k]))
-        puts[5 + k].start()
+        puts[2 + k].start()
     gproj = mine[...] + received[...]
     grad_feats[...] = lax.dot_general(
         gproj, w_proj[...], (((1,), (1,)), ((), ())), preferred_element_type=F32

time: 55.6 us -> 55.7 us (level)
  no operation moved by 1% of the time
where the time goes in v10:
time: 55.7 us; the launch traced here: 55.3 us
  blocking collectives  25.2 us (45%)
  starting transfers between devices  10.9 us (20%)
  Pallas kernels  9.85 us (18%)
  waiting for transfers between devices  6.23 us (11%)
  local copies, waits for them, and re-layouts  2.42 us (4%)
  between operations  0.7 us (1%)
    all_to_all x1, blocking collectives, body(): lax.all_to_all(joined, GROUP, 0, 0, tiled=True, axis_index_groups=same_core)  14.1 us
    all_to_all x1, blocking collectives, body(): lax.all_to_all(sums, GROUP, 0, 0, tiled=True, axis_index_groups=same_core)  11.1 us
    all_to_all x1, starting transfers between devices, body(): lax.all_to_all(front_call(feats, w_proj), GROUP, 0, 0, tiled=True, axis_i...  5.87 us
    pallas_call x1, Pallas kernels, tile_call(): pl.pallas_call(tile_kernel, out_shape=(jax.ShapeDtypeStruct((240, 128), F...  5.48 us
    all_to_all x1, waiting for transfers between devices, body(): lax.all_to_all(front_call(feats, w_proj), GROUP, 0, 0, tiled=True, axis_i...  3.09 us
    ppermute x1, starting transfers between devices, body(): lax.ppermute(every, GROUP, swap)  2.72 us
    unnamed x12, local copies, waits for them, and re-layouts  2.42 us
    pallas_call x1, Pallas kernels, front_call(): pl.pallas_call(front_kernel, out_shape=jax.ShapeDtypeStruct((8, 96, 128),...  1.9 us
  transfers between devices with their start and end apart: 5, of which 4 were waited for; matrix products, arithmetic and copies ran while one was open for 0% of the time, Pallas kernels for 1%

profile of v10, /device:TPU:1, one launch (start us, length us, event | category | flops | bytes accessed | tf_op | source)
XLA Modules:
  0.0 55.3 jit_solution(8402882760608578416)
XLA Ops:
  0.6 0.0 copy-start.5
  0.6 0.0 copy-start.4
  0.7 1.9 %front.1 = bf16[8,96,128]{2,1,0:T(8,128)(2,1)} custom-call(bf16[64,1024]{1,0:T(8,128)(2,1)} %feats_hbm.1, bf16[1024,128]{1,0:T(8,128)(2,1)} %w_proj.1), custom_call_target="tpu_custom_call" | custom-call | tf_op jit(solution)/shard_map/front/pallas_call | solution.py:57
  2.6 5.9 %all-to-all-start = ((bf16[8,96,128]{2,1,0:T(8,128)(2,1)}), bf16[8,96,128]{2,1,0:T(8,128)(2,1)S(1)}, u32[]{:S(2)}, u32[]{:S(2)}) async-start(bf16[8,96,128]{2,1,0:T(8,128)(2,1)} %front.1), calls=%async_computation | async-start | bytes 393216 | tf_op jit(solution)/shard_map/all_to_all | solution.py:583
  8.4 0.0 copy-start.1
  8.4 0.9 %copy-done.1 = bf16[576,64]{0,1:T(8,128)(2,1)S(1)} copy-done((bf16[576,64]{0,1:T(8,128)(2,1)S(1)}, bf16[576,64]{0,1:T(8,128)(2,1)}, u32[]{:S(2)}) %copy-start.1) | copy-done | bytes 73752
  9.3 0.0 copy-start.2
  9.3 0.8 %copy-done.2 = f32[64,2,64]{2,1,0:T(2,128)S(1)} copy-done((f32[64,2,64]{2,1,0:T(2,128)S(1)}, f32[64,2,64]{2,1,0:T(2,128)}, u32[]{:S(2)}) %copy-start.2) | copy-done | bytes 32792
  10.2 0.0 copy-start.3
  10.2 0.7 %copy-done.3 = s32[1024]{0:T(1024)S(1)} copy-done((s32[1024]{0:T(1024)S(1)}, s32[1024]{0:T(1024)}, u32[]{:S(2)}) %copy-start.3) | copy-done | bytes 4120
  10.9 0.6 %prepare.1 = (bf16[768,128]{1,0:T(8,128)(2,1)S(1)}, bf16[768,128]{1,0:T(8,128)(2,1)S(1)}, f32[512,1024]{1,0:T(8,128)S(1)}, f32[512,128]{1,0:T(8,128)S(1)}, f32[64,128]{1,0:T(8,128)S(1)}) custom-call(s32[8,128]{1,0:T(8,128)S(1)} %bitcast.9, f32[64,2,64]{2,1,0:T(2,128)S(1)} %copy-done.2, bf16[64,576]{1,0:T(8,128)(2,1)S(1)} %bitcast.8), custom_call_target="tpu_custom_call" | custom-call | flops 300000000 | bytes 4000000 | tf_op jit(solution)/shard_map/prepare/pallas_call | solution.py:137
  11.4 3.1 %all-to-all-done.same = bf16[8,96,128]{2,1,0:T(8,128)(2,1)S(1)} async-done(((bf16[8,96,128]{2,1,0:T(8,128)(2,1)}), bf16[8,96,128]{2,1,0:T(8,128)(2,1)S(1)}, u32[]{:S(2)}, u32[]{:S(2)}) %all-to-all-start) | async-done | bytes 196640 | tf_op jit(solution)/shard_map/all_to_all | solution.py:583
  14.5 1.8 %collective-permute-start = (bf16[8,96,128]{2,1,0:T(8,128)(2,1)S(1)}, bf16[8,96,128]{2,1,0:T(8,128)(2,1)S(1)}, u32[]{:S(2)}, u32[]{:S(2)}) collective-permute-start(bf16[8,96,128]{2,1,0:T(8,128)(2,1)S(1)} %all-to-all-done.same), channel_id=1, source_target_pairs={{0,8},{4,12},{8,0},{12,4},{16,24},{20,28},{24,16},{28,20},{32,40},... | collective-permute-start | bytes 589832 | tf_op jit(solution)/shard_map/ppermute | solution.py:586
  16.3 1.1 %collective-permute-done.other = bf16[8,96,128]{2,1,0:T(8,128)(2,1)S(1)} collective-permute-done((bf16[8,96,128]{2,1,0:T(8,128)(2,1)S(1)}, bf16[8,96,128]{2,1,0:T(8,128)(2,1)S(1)}, u32[]{:S(2)}, u32[]{:S(2)}) %collective-permute-start) | collective-permute-done | bytes 196640 | tf_op jit(solution)/shard_map/ppermute | solution.py:586
  17.4 0.0 copy-done.5
  17.4 0.0 copy-done.4
  17.4 5.5 %tiles.1 = (f32[240,128]{1,0:T(8,128)S(1)}, bf16[240,128]{1,0:T(8,128)(2,1)S(1)}) custom-call(bf16[8,96,128]{2,1,0:T(8,128)(2,1)S(1)} %all-to-all-done.same, bf16[8,96,128]{2,1,0:T(8,128)(2,1)S(1)} %collective-permute-done.other, f32[1,64]{1,0:T(1,128)S(1)} %bitcast.10, f32[1,64]{1,0:T(1,128)S(1)} %bitcast.11, bf16[768,128]{1,0:T(8,128)(2,1)S(1)} %get-tuple-element.36.fwd_w, ...), custom_call_target="tpu_custom_call" | custom-call | flops 2000000000 | bytes 1000000 | tf_op jit(solution)/shard_map/tiles/pallas_call | solution.py:373
  22.9 0.0 copy-start
  22.9 0.5 collective-permute-start.1
  23.4 0.9 %collective-permute-done.1.received = bf16[240,128]{1,0:T(8,128)(2,1)S(1)} collective-permute-done((bf16[240,128]{1,0:T(8,128)(2,1)S(1)}, bf16[240,128]{1,0:T(8,128)(2,1)S(1)}, u32[]{:S(2)}, u32[]{:S(2)}) %collective-permute-start.1) | collective-permute-done | bytes 61472 | tf_op jit(solution)/shard_map/ppermute | solution.py:588
  24.3 14.1 %all_to_all.15.parts = bf16[16,112,128]{2,1,0:T(8,128)(2,1)S(1)} all-to-all(bf16[16,112,128]{2,1,0:T(8,128)(2,1)S(1)} %join.1), channel_id=1, replica_groups={{0,4,16,20,32,36,48,52,64,68,80,84,96,100,112,116},{8,12,24,28,40,44,56..., dimensions={0} | all-to-all | bytes 917504 | tf_op jit(solution)/shard_map/all_to_all | solution.py:589
  38.4 0.7 %sums.1 = (bf16[16,48,128]{2,1,0:T(8,128)(2,1)S(1)}, bf16[32,128]{1,0:T(8,128)(2,1)S(1)}, bf16[32,128]{1,0:T(8,128)(2,1)S(1)}) custom-call(bf16[16,112,128]{2,1,0:T(8,128)(2,1)S(1)} %all_to_all.15.parts, bf16[8,96,128]{2,1,0:T(8,128)(2,1)S(1)} %all-to-all-done.same, bf16[8,96,128]{2,1,0:T(8,128)(2,1)S(1)} %collective-permute-done.other), custom_call_target="tpu_custom_call" | custom-call | tf_op jit(solution)/shard_map/sums/pallas_call | solution.py:488
  39.2 11.1 %all_to_all.16.same = bf16[16,48,128]{2,1,0:T(8,128)(2,1)S(1)} all-to-all(bf16[16,48,128]{2,1,0:T(8,128)(2,1)S(1)} %get-tuple-element.43), channel_id=1, replica_groups={{0,4,16,20,32,36,48,52,64,68,80,84,96,100,112,116},{8,12,24,28,40,44,56..., dimensions={0} | all-to-all | bytes 393216 | tf_op jit(solution)/shard_map/all_to_all | solution.py:591
  50.2 2.7 %collective-permute-start.2 = (bf16[16,48,128]{2,1,0:T(8,128)(2,1)S(1)}, bf16[16,48,128]{2,1,0:T(8,128)(2,1)S(1)}, u32[]{:S(2)}, u32[]{:S(2)}) collective-permute-start(bf16[16,48,128]{2,1,0:T(8,128)(2,1)S(1)} %all_to_all.16.same), channel_id=1, source_target_pairs={{0,8},{4,12},{8,0},{12,4},{16,24},{20,28},{24,16},{28,20},{32,40},... | collective-permute-start | bytes 589832 | tf_op jit(solution)/shard_map/ppermute | solution.py:594
  53.0 0.0 collective-permute-start.3
  53.0 1.2 %collective-permute-done.3.received = bf16[32,128]{1,0:T(8,128)(2,1)S(1)} collective-permute-done((bf16[32,128]{1,0:T(8,128)(2,1)S(1)}, bf16[32,128]{1,0:T(8,128)(2,1)S(1)}, u32[]{:S(2)}, u32[]{:S(2)}) %collective-permute-start.3) | collective-permute-done | bytes 8224 | tf_op jit(solution)/shard_map/ppermute | solution.py:594
  54.1 0.0 collective-permute-done.2.other
  54.1 0.0 copy-done
  54.1 1.1 %outputs.1 = (f32[1024,128]{1,0:T(8,128)}, f32[64,576]{1,0:T(8,128)}, bf16[32,1024]{1,0:T(8,128)(2,1)}, f32[1,64]{1,0:T(1,128)}, f32[1,64]{1,0:T(1,128)}, /*index=5*/f32[1,1]{1,0:T(1,128)}) custom-call(bf16[16,48,128]{2,1,0:T(8,128)(2,1)S(1)} %all_to_all.16.same, bf16[16,48,128]{2,1,0:T(8,128)(2,1)S(1)} %collective-permute-done.2.other, ...), custom_call_target="tpu_custom_call" | custom-call | tf_op jit(solution)/shard_map/outputs/pallas_call | solution.py:553
  (1 shorter events, 0.0 us)
Async XLA Ops:
  0.6 16.8 %copy-start.5 = (f32[64]{0:T(128)S(1)}, f32[64]{0:T(128)}, u32[]{:S(2)}) copy-start(f32[64]{0:T(128)} %param.11) | copy-start | bytes 772
  0.6 16.8 %copy-start.4 = (f32[64]{0:T(128)S(1)}, f32[64]{0:T(128)}, u32[]{:S(2)}) copy-start(f32[64]{0:T(128)} %param.10) | copy-start | bytes 772
  2.6 12.0 %all-to-all-start = ((bf16[8,96,128]{2,1,0:T(8,128)(2,1)}), bf16[8,96,128]{2,1,0:T(8,128)(2,1)S(1)}, u32[]{:S(2)}, u32[]{:S(2)}) async-start(bf16[8,96,128]{2,1,0:T(8,128)(2,1)} %front.1), calls=%async_computation | async-start | bytes 393216 | tf_op jit(solution)/shard_map/all_to_all | solution.py:583
  8.4 0.9 %copy-start.1 = (bf16[576,64]{0,1:T(8,128)(2,1)S(1)}, bf16[576,64]{0,1:T(8,128)(2,1)}, u32[]{:S(2)}) copy-start(bf16[576,64]{0,1:T(8,128)(2,1)} %param.9) | copy-start | bytes 221188
  9.3 0.8 %copy-start.2 = (f32[64,2,64]{2,1,0:T(2,128)S(1)}, f32[64,2,64]{2,1,0:T(2,128)}, u32[]{:S(2)}) copy-start(f32[64,2,64]{2,1,0:T(2,128)} %target.1) | copy-start | bytes 98308
  10.2 0.7 %copy-start.3 = (s32[1024]{0:T(1024)S(1)}, s32[1024]{0:T(1024)}, u32[]{:S(2)}) copy-start(s32[1024]{0:T(1024)} %param.13) | copy-start | bytes 12292
  14.5 2.9 %collective-permute-start = (bf16[8,96,128]{2,1,0:T(8,128)(2,1)S(1)}, bf16[8,96,128]{2,1,0:T(8,128)(2,1)S(1)}, u32[]{:S(2)}, u32[]{:S(2)}) collective-permute-start(bf16[8,96,128]{2,1,0:T(8,128)(2,1)S(1)} %all-to-all-done.same), channel_id=1, source_target_pairs={{0,8},{4,12},{8,0},{12,4},{16,24},{20,28},{24,16},{28,20},{32,40},... | collective-permute-start | bytes 589832 | tf_op jit(solution)/shard_map/ppermute | solution.py:586
  22.9 31.3 %copy-start = (bf16[1024,128]{1,0:T(8,128)(2,1)S(1)}, bf16[1024,128]{1,0:T(8,128)(2,1)}, u32[]{:S(2)}) copy-start(bf16[1024,128]{1,0:T(8,128)(2,1)} %w_proj.1) | copy-start | bytes 786436
  22.9 1.4 %collective-permute-start.1 = (bf16[240,128]{1,0:T(8,128)(2,1)S(1)}, bf16[240,128]{1,0:T(8,128)(2,1)S(1)}, u32[]{:S(2)}, u32[]{:S(2)}) collective-permute-start(bf16[240,128]{1,0:T(8,128)(2,1)S(1)} %get-tuple-element.42), channel_id=1, source_target_pairs={{0,8},{4,12},{8,0},{12,4},{16,24},{20,28},{24,16},{28,20},{32,40},... | collective-permute-start | bytes 184328 | tf_op jit(solution)/shard_map/ppermute | solution.py:588
  50.2 3.9 %collective-permute-start.2 = (bf16[16,48,128]{2,1,0:T(8,128)(2,1)S(1)}, bf16[16,48,128]{2,1,0:T(8,128)(2,1)S(1)}, u32[]{:S(2)}, u32[]{:S(2)}) collective-permute-start(bf16[16,48,128]{2,1,0:T(8,128)(2,1)S(1)} %all_to_all.16.same), channel_id=1, source_target_pairs={{0,8},{4,12},{8,0},{12,4},{16,24},{20,28},{24,16},{28,20},{32,40},... | collective-permute-start | bytes 589832 | tf_op jit(solution)/shard_map/ppermute | solution.py:594
  53.0 1.2 %collective-permute-start.3 = (bf16[32,128]{1,0:T(8,128)(2,1)S(1)}, bf16[32,128]{1,0:T(8,128)(2,1)S(1)}, u32[]{:S(2)}, u32[]{:S(2)}) collective-permute-start(bf16[32,128]{1,0:T(8,128)(2,1)S(1)} %get-tuple-element.47), channel_id=1, source_target_pairs={{0,8},{4,12},{8,0},{12,4},{16,24},{20,28},{24,16},{28,20},{32,40},... | collective-permute-start | bytes 24584 | tf_op jit(solution)/shard_map/ppermute | solution.py:594
